TPU v7x, 32 devices: a whole 2x2x4 slice. The times are simulated.
32 devices in a mesh: slab: 8 (over z, y), strip: 4 (over x, core).
Axes of the slice: x: 2, y: 2, z: 4, core: 2. Of those that a mesh axis runs over, the one named last changes fastest.
Arguments:
- colors: bfloat16 [8, 4, 16, 32, 128], P('slab', 'strip'), may hold values from -6 to 6
- transmit: bfloat16 [8, 4, 16, 128], P('slab', 'strip'), may hold values from 0.099609375 to 1
- pair_counts: int32 [4, 8, 8], P('strip'), may hold values from 0 to 2, as said below
- slot_block: int32 [4, 8, 16], P('strip'), may hold values from 0 to 1023, as said below
- assign: int32 [4, 1024], P('strip'), may hold values from 0 to 1023, as said below
- depth_rank: int32 [8], replicated, may hold values from 0 to 7, each once
- w_in: bfloat16 [256, 32], replicated, may hold values from -1 to 1
- trans_weight: bfloat16 [256], replicated, may hold values from -6 to 6
- w_mid: bfloat16 [2, 256, 256], replicated, may hold values from -0.375 to 0.375
- w_out: bfloat16 [4, 256], replicated, may hold values from -0.375 to 0.375
Outputs:
- display: bfloat16 [8, 4, 128, 4, 128], P('slab', None, 'strip')
Inputs may be any that keep to these rules, and one draw needn't show every extreme that they name: pair_counts[t, s, c] counts the span blocks renderer s of strip t sends to compositor c; in every strip one compositor gets 2 from every renderer. `slot_block`: the live slots of renderer s come first, grouped by compositor in increasing order, pair_counts[t, s, c] of them for compositor c, naming distinct blocks b with assign[t, b] // 128 = c; other slots are ignored. Each strip's row is a permutation: block b goes to compositor assign[t, b] // 128 at local position assign[t, b] % 128. `depth_rank`: a permutation.
All inputs are finite; a program needn't handle non-finite values.
Results may differ from a plain program's by a relative error of at most 0.0068.
Values may be sent and summed in bfloat16 or wider, within the bound.
No kernel may reach another device: no remote copies, remote signals or barrier semaphores. Data moves between devices by JAX's collectives and lax.ppermute only.
A program may use at most 128 MiB of HBM per device.

v0:
```python
import functools

import jax
import jax.numpy as jnp
from jax import lax
from jax.experimental import pallas as pl
from jax.experimental.pallas import tpu as pltpu
from jax.sharding import PartitionSpec as P

MOST = 2
LB = 128


EXACT_PRECISION = lax.Precision.HIGHEST


def shade_blocks(blend_color, trans_field, w_in, trans_weight, w_mid, w_out):
    summed = jnp.einsum("hf,lfp->lhp", w_in, blend_color, preferred_element_type=jnp.float32)
    summed = summed + trans_weight.astype(jnp.float32)[None, :, None] * trans_field[:, None, :]
    hidden = jax.nn.silu(summed).astype(jnp.bfloat16)
    for layer_index in range(w_mid.shape[0]):
        hidden = jax.nn.silu(
            jnp.einsum(
                "hg,lgp->lhp", w_mid[layer_index], hidden, preferred_element_type=jnp.float32
            )
        ).astype(jnp.bfloat16)
    return jnp.einsum("oh,lhp->lop", w_out, hidden, preferred_element_type=jnp.float32).astype(
        jnp.bfloat16
    )


def dense_device(
    colors, transmit, pair_counts, slot_block, assign, depth_rank, w_in, trans_weight, w_mid, w_out
):
    myself = lax.axis_index("slab")
    counts = pair_counts[0]
    blocks_all = slot_block[0]
    assign_row = assign[0]
    offsets = jnp.cumsum(counts, axis=1) - counts
    slot_rank = jnp.arange(MOST, dtype=jnp.int32)
    my_counts = lax.dynamic_index_in_dim(counts, myself, 0, keepdims=False)
    my_offsets = lax.dynamic_index_in_dim(offsets, myself, 0, keepdims=False)
    send_slots = jnp.where(
        slot_rank[None, :] < my_counts[:, None], my_offsets[:, None] + slot_rank[None, :], 0
    )
    send_color = colors[0, 0][send_slots]
    send_trans = transmit[0, 0][send_slots][:, :, None, :]
    incoming = lax.dynamic_index_in_dim(counts, myself, 1, keepdims=False)
    in_offsets = lax.dynamic_index_in_dim(offsets, myself, 1, keepdims=False)
    live_slot = slot_rank[None, :] < incoming[:, None]
    recv_slots = jnp.where(live_slot, in_offsets[:, None] + slot_rank[None, :], 0)
    recv_blocks = jnp.take_along_axis(blocks_all, recv_slots, axis=1)
    local_pos = assign_row[recv_blocks] - myself * LB
    live_flat = live_slot.reshape(-1)
    local_flat = jnp.where(live_flat, local_pos.reshape(-1), -1)
    depth_flat = jnp.repeat(depth_rank, MOST)
    ahead_table = (
        (local_flat[:, None] == local_flat[None, :])
        & (depth_flat[None, :] < depth_flat[:, None])
        & live_flat[None, :]
    )
    ahead_table = ahead_table.astype(jnp.float32)
    owner_table = (jnp.arange(LB, dtype=jnp.int32)[:, None] == local_flat[None, :]).astype(
        jnp.float32
    )
    got_color = lax.all_to_all(send_color, "slab", split_axis=0, concat_axis=0, tiled=True)
    got_trans = lax.all_to_all(send_trans, "slab", split_axis=0, concat_axis=0, tiled=True)
    pixel_count = got_color.shape[3]
    item_count = got_color.shape[0] * got_color.shape[1]
    log_trans = jnp.log(got_trans.reshape(item_count, pixel_count).astype(jnp.float32))
    log_trans = jnp.where(live_flat[:, None], log_trans, 0.0)
    front_log = jnp.dot(ahead_table, log_trans, precision=EXACT_PRECISION)
    front_share = jnp.where(live_flat[:, None], jnp.exp(front_log), 0.0)
    weighted = front_share[:, None, :] * got_color.reshape(item_count, -1, pixel_count).astype(
        jnp.float32
    )
    blend_sum = jnp.dot(owner_table, weighted.reshape(item_count, -1), precision=EXACT_PRECISION)
    blend_color = blend_sum.reshape(LB, -1, pixel_count).astype(jnp.bfloat16)
    trans_field = jnp.exp(jnp.dot(owner_table, log_trans, precision=EXACT_PRECISION))
    shaded = shade_blocks(blend_color, trans_field, w_in, trans_weight, w_mid, w_out)
    display_tiles = lax.all_to_all(shaded[None], "strip", split_axis=1, concat_axis=0, tiled=True)
    return display_tiles[None]


SMEM = pltpu.SMEM
VMEM = pltpu.VMEM
ROWS = 8
GROUP = 4


def exchange_order(n_slab):
    half = n_slab // 2
    flip = 1 if half % 2 == 0 else 0
    return [s for i in range(half) for s in (half + (i ^ flip), i)]


def pack_kernel(far_counts, far_colors, far_transmit, sends, counts, colors, transmit, sems):
    n_slab = sends.shape[0]
    place = [exchange_order(n_slab).index(c) for c in range(n_slab)]
    slots, feats, span = colors.shape[2:]
    me = lax.axis_index("slab")
    copies = [
        pltpu.make_async_copy(far, near, sems.at[i])
        for i, (far, near) in enumerate(
            ((far_counts, counts), (far_transmit, transmit), (far_colors, colors))
        )
    ]
    for copy in copies:
        copy.start()
    copies[0].wait()
    mine = counts[0, pl.ds(me, 1), :].astype(jnp.float32)
    before = lax.broadcasted_iota(jnp.int32, mine.shape, 1)
    row = lax.broadcasted_iota(jnp.int32, (ROWS, slots), 0).astype(jnp.float32)
    lane = lax.broadcasted_iota(jnp.int32, (ROWS, slots), 1).astype(jnp.float32)
    offs, picks = [], []
    for c in range(n_slab):
        off = jnp.sum(jnp.where(before < c, mine, 0.0), axis=1, keepdims=True)
        offs.append(off)
        hit = (row < MOST) & (lane - row == off)
        picks.append(jnp.where(hit, 1.0, 0.0))
    pick = jnp.concatenate(picks).astype(jnp.bfloat16)
    copies[1].wait()
    tails = jnp.dot(pick, transmit[0, 0], preferred_element_type=jnp.float32)
    for c in range(n_slab):
        tail = tails[c * ROWS : (c + 1) * ROWS]
        sends[place[c], pl.ds(MOST * feats, ROWS), :] = tail.astype(jnp.bfloat16)
    copies[2].wait()
    for c in range(n_slab):
        off = jnp.broadcast_to(offs[c], (feats, span)).astype(jnp.bfloat16)
        for r in range(MOST):
            last = min(MOST * c + r, slots - 1)
            block = colors[0, 0, last]
            for slot in range(r, last):
                block = jnp.where(off == slot - r, colors[0, 0, slot], block)
            sends[place[c], pl.ds(r * feats, feats), :] = block


def plan_kernel(n_slab, slots, *refs):
    (counts, blocks, assign, depth), (rows, codes) = refs[:4], refs[4:]
    items = n_slab * MOST
    outs = codes.shape[1] // (2 * items)
    me = lax.axis_index("slab")
    row = lax.broadcasted_iota(jnp.int32, rows.shape[1:], 0)
    item_lane = lax.broadcasted_iota(jnp.int32, codes.shape, 1) // outs
    posv = jnp.zeros(rows.shape[1:], jnp.int32)
    depthv = jnp.zeros(rows.shape[1:], jnp.int32)
    firstv = jnp.zeros(rows.shape[1:], jnp.int32)
    codev = jnp.full(codes.shape, -1, jnp.int32)
    pos = []
    for k, s in enumerate(exchange_order(n_slab)):
        off = jnp.int32(0)
        for c in range(n_slab):
            off = off + jnp.where(c < me, counts[0, s, c], 0)
        count = counts[0, s, me]
        for r in range(MOST):
            i = k * MOST + r
            slot = jnp.minimum(off + r, slots - 1)
            here = assign[0, blocks[0, s, slot]] - me * LB
            here = jnp.where(r < count, here, -1)
            first = jnp.int32(i)
            for j in reversed(range(i)):
                first = jnp.where(pos[j] == here, j, first)
            pos.append(here)
            firstv = jnp.where(row == i, first, firstv)
            posv = jnp.where(row == i, here, posv)
            depthv = jnp.where(row == i, depth[s], depthv)
            codev = jnp.where(item_lane == i, jnp.where(first == i, here, -1), codev)
    rows[0] = posv
    rows[1] = depthv
    rows[2] = firstv
    codes[...] = codev.astype(jnp.float32).astype(jnp.bfloat16)


def place_kernel(w_in, trans_weight, far_out, far_mid, w_first, w_out, w_later, w_mid, sems):
    copy = pltpu.make_async_copy(far_mid, w_mid, sems.at[0])
    copy.start()
    feats, hidden = w_in.shape
    half_in = (w_in[...].astype(jnp.float32) * 0.5).astype(jnp.bfloat16)
    half_trans = trans_weight[...].astype(jnp.float32) * 0.5
    sub = lax.broadcasted_iota(jnp.int32, (16, hidden), 0)
    w_first[...] = jnp.zeros_like(w_first)
    for a in range(GROUP):
        w_first[a, pl.ds(a * feats, feats), :] = half_in
        tail = jnp.where(sub // 2 == a, half_trans, 0.0)
        w_first[a, pl.ds(GROUP * feats, 16), :] = tail.astype(jnp.bfloat16)
    w_out[...] = far_out[...]
    copy.wait()
    for m in range(w_mid.shape[0]):
        w_later[m] = (w_mid[m].astype(jnp.float32).T * 0.5).astype(jnp.bfloat16)


def silu_half(u):
    return (u + u * jnp.tanh(u)).astype(jnp.bfloat16)


def later_layers(h, w_mid, w_out):
    for m in range(w_mid.shape[0]):
        h = silu_half(jnp.dot(h, w_mid[m], preferred_element_type=jnp.float32))
    y = lax.dot_general(
        w_out[...], h, (((1,), (1,)), ((), ())), preferred_element_type=jnp.float32
    )
    return y.astype(jnp.bfloat16).astype(jnp.float32)


def empty_kernel(trans_weight, w_mid, w_out, out):
    u = trans_weight[...].astype(jnp.float32) * 0.5
    h = silu_half(jnp.broadcast_to(u, (out.shape[1], u.shape[1])))
    y = later_layers(h, w_mid, w_out)
    outs = w_out.shape[0]
    for at in range(0, out.shape[0], outs):
        out[pl.ds(at, outs), :] = y


def shade_kernel(rows, codes, got, w_first, w_mid, w_out, out, acc, xt, ys):
    items, feats, span = acc.shape
    outs = w_out.shape[0]

    posv, depthv = rows[0], rows[1]
    front = jnp.ones((items, span), jnp.float32)
    total = jnp.ones((items, span), jnp.float32)
    for k in range(items // MOST):
        tail = got[k, pl.ds(MOST * feats, ROWS), :].astype(jnp.float32)
        for r in range(MOST):
            j = k * MOST + r
            trans_j = tail[r : r + 1, :]
            same = posv == posv[j : j + 1, :]
            total = jnp.where(same, total * trans_j, total)
            front = jnp.where(same & (depthv > depthv[j : j + 1, :]), front * trans_j, front)
    acc[...] = jnp.zeros_like(acc)
    for j in range(items):
        k, r = divmod(j, MOST)
        color = got[k, pl.ds(r * feats, feats), :].astype(jnp.float32)
        at = rows[2, j, 0]
        acc[at] = acc[at] + front[j : j + 1, :] * color
    total_hi = total.astype(jnp.bfloat16).astype(jnp.float32)
    total_lo = total - total_hi
    groups = items // GROUP
    sub = lax.broadcasted_iota(jnp.int32, (16, span), 0)
    xt[...] = jnp.zeros_like(xt)
    for q in range(groups):
        block = acc[pl.ds(q * GROUP, GROUP)].reshape(GROUP * feats, span)
        tail = jnp.zeros((16, span), jnp.float32)
        for a in range(GROUP):
            i = q * GROUP + a
            tail = jnp.where(sub == 2 * a, total_hi[i : i + 1, :], tail)
            tail = jnp.where(sub == 2 * a + 1, total_lo[i : i + 1, :], tail)
        lines = pl.ds(q * span, span)
        xt[lines, pl.ds(0, GROUP * feats)] = block.T.astype(jnp.bfloat16)
        xt[lines, pl.ds(GROUP * feats, 16)] = tail.T.astype(jnp.bfloat16)

    x = xt[...]
    stride = GROUP
    for start in range(0, GROUP, stride):
        h = jnp.concatenate(
            [
                silu_half(jnp.dot(x, w_first[a], preferred_element_type=jnp.float32))
                for a in range(start, start + stride)
            ]
        )
        y = later_layers(h, w_mid, w_out)
        for a in range(start, start + stride):
            for q in range(groups):
                at = ((a - start) * groups + q) * span
                ys[pl.ds((q * GROUP + a) * outs, outs), :] = y[:, at : at + span]
    out[pl.ds(0, items * outs), :] = ys[...].astype(jnp.bfloat16)
    out[pl.ds(items * outs, ROWS), :] = codes[...]


def join_kernel(*refs):
    *got, empty, out = refs
    _, n_strip, tile, outs, span = out.shape
    lines = tile * outs
    count = got[0].shape[0] - ROWS
    me = lax.axis_index("strip")
    want = lax.broadcasted_iota(jnp.int32, (lines, count), 0) + me * lines
    chan = lax.broadcasted_iota(jnp.int32, (lines, count), 1) % outs
    filler = jnp.concatenate([empty[...]] * (lines // ROWS))
    ones = jnp.ones((count, span), jnp.bfloat16)
    for k in range(n_strip):
        pos = got[k][pl.ds(count, ROWS), :].astype(jnp.float32)[:1, :count].astype(jnp.int32)
        hit = pos * outs + chan == want
        pick = jnp.where(hit, 1.0, 0.0).astype(jnp.bfloat16)
        blocks = got[k][pl.ds(0, count), :]
        placed = jnp.dot(pick, blocks, preferred_element_type=jnp.float32)
        filled = jnp.dot(pick, ones, preferred_element_type=jnp.float32)
        value = jnp.where(filled > 0.5, placed, filler)
        out[0, me ^ ((k + 1) % n_strip)] = value.reshape(tile, outs, span).astype(jnp.bfloat16)


def compact_device(
    n_slab,
    n_strip,
    colors,
    transmit,
    pair_counts,
    slot_block,
    assign,
    depth_rank,
    w_in,
    trans_weight,
    w_mid,
    w_out,
):
    slots, feats, span = colors.shape[2:]
    items = n_slab * MOST
    outs = w_out.shape[0]
    smem = pl.BlockSpec(memory_space=SMEM)
    vmem = pl.BlockSpec(memory_space=VMEM)
    hbm = pl.BlockSpec(memory_space=pltpu.HBM)
    held = functools.partial(pltpu.with_memory_space_constraint, memory_space=pltpu.HBM)
    small = pltpu.CompilerParams(vmem_limit_bytes=4 * 1024 * 1024)
    message = MOST * feats + ROWS
    sends = pl.pallas_call(
        pack_kernel,
        out_shape=jax.ShapeDtypeStruct((n_slab, message, span), jnp.bfloat16),
        in_specs=[hbm] * 3,
        out_specs=vmem,
        scratch_shapes=[
            pltpu.VMEM(pair_counts.shape, jnp.int32),
            pltpu.VMEM(colors.shape, colors.dtype),
            pltpu.VMEM(transmit.shape, transmit.dtype),
            pltpu.SemaphoreType.DMA((3,)),
        ],
        compiler_params=small,
        name="pack",
    )(held(pair_counts), held(colors), held(transmit))
    group = exchange_order(n_slab)
    got = lax.all_to_all(
        sends, "slab", split_axis=0, concat_axis=0, axis_index_groups=[group], tiled=True
    )
    hidden = w_in.shape[0]
    rough = pl.CostEstimate(flops=10**5, bytes_accessed=10**6, transcendentals=0)
    roomy = pltpu.CompilerParams(vmem_limit_bytes=16 * 1024 * 1024)
    trans_row = trans_weight[None]
    rows, codes = pl.pallas_call(
        functools.partial(plan_kernel, n_slab, slots),
        out_shape=[
            jax.ShapeDtypeStruct((3, items, span), jnp.int32),
            jax.ShapeDtypeStruct((ROWS, span), jnp.bfloat16),
        ],
        in_specs=[smem] * 4,
        out_specs=[vmem] * 2,
        compiler_params=small,
        cost_estimate=rough,
        name="plan",
    )(pair_counts, slot_block, assign, depth_rank)
    w_first, w_last, w_later = pl.pallas_call(
        place_kernel,
        out_shape=[
            jax.ShapeDtypeStruct((GROUP, 2 * GROUP * feats, hidden), jnp.bfloat16),
            jax.ShapeDtypeStruct(w_out.shape, jnp.bfloat16),
            jax.ShapeDtypeStruct(w_mid.shape, jnp.bfloat16),
        ],
        in_specs=[vmem] * 3 + [hbm],
        out_specs=[vmem] * 3,
        scratch_shapes=[
            pltpu.VMEM(w_mid.shape, jnp.bfloat16),
            pltpu.SemaphoreType.DMA((1,)),
        ],
        compiler_params=small,
        cost_estimate=rough,
        name="place",
    )(w_in.T, trans_row, w_out, held(w_mid))
    empty = pl.pallas_call(
        empty_kernel,
        out_shape=jax.ShapeDtypeStruct((ROWS, span), jnp.float32),
        in_specs=[vmem] * 3,
        out_specs=vmem,
        compiler_params=roomy,
        cost_estimate=rough,
        name="empty",
    )(trans_row, w_later, w_last)
    shaded = pl.pallas_call(
        shade_kernel,
        out_shape=jax.ShapeDtypeStruct((items * outs + ROWS, span), jnp.bfloat16),
        in_specs=[vmem] * 6,
        out_specs=vmem,
        scratch_shapes=[
            pltpu.VMEM((items, feats, span), jnp.float32),
            pltpu.VMEM((items // GROUP * span, 2 * GROUP * feats), jnp.bfloat16),
            pltpu.VMEM((items * outs, span), jnp.float32),
        ],
        compiler_params=roomy,
        name="shade",
    )(rows, codes, got, w_first, w_later, w_last)
    tiles = [
        lax.ppermute(shaded, "strip", [(s, s ^ k) for s in range(n_strip)])
        for k in range(1, n_strip)
    ] + [shaded]
    return pl.pallas_call(
        join_kernel,
        out_shape=jax.ShapeDtypeStruct((1, n_strip, LB // n_strip, outs, span), jnp.bfloat16),
        in_specs=[vmem] * (n_strip + 1),
        out_specs=pl.BlockSpec(),
        compiler_params=small,
        name="join",
    )(*tiles, empty)


def solution(mesh):
    n_slab, n_strip = mesh.shape["slab"], mesh.shape["strip"]
    placed = (
        P("slab", "strip", None, None, None),
        P("slab", "strip", None, None),
        P("strip", None, None),
        P("strip", None, None),
        P("strip", None),
        P(),
        P(),
        P(),
        P(),
        P(),
    )
    compact = n_strip & (n_strip - 1) == 0 and 4 * MOST * n_slab <= LB
    return jax.shard_map(
        functools.partial(compact_device, n_slab, n_strip) if compact else dense_device,
        mesh=mesh,
        in_specs=placed,
        out_specs=P("slab", None, "strip", None, None),
        check_vma=False,
    )
```

profile of v0, /device:TPU:0, one launch (start us, length us, event | category | flops | bytes accessed | tf_op | source)
XLA Modules:
  0.0 20.5 jit_solution(12837288554768906693)
XLA Ops:
  0.0 1.7 %pack.1 = bf16[8,72,128]{2,1,0:T(8,128)(2,1)} custom-call(s32[1,8,8]{2,1,0:T(8,128)} %far_counts.1, bf16[1,1,16,32,128]{4,3,2,1,0:T(8,128)(2,1)} %far_colors.1, bf16[1,1,16,128]{3,2,1,0:T(8,128)(2,1)} %far_transmit.1), custom_call_target="tpu_custom_call" | custom-call | tf_op jit(solution)/shard_map/pack/pallas_call | solution.py:313
  1.7 0.0 copy-start
  1.7 0.0 copy-start.2
  1.7 0.0 copy-start.3
  1.7 0.0 copy-start.5
  1.7 0.0 copy-start.6
  1.8 0.0 copy-start.4
  1.8 8.4 %all-to-all-start = ((bf16[8,72,128]{2,1,0:T(8,128)(2,1)}), bf16[8,72,128]{2,1,0:T(8,128)(2,1)S(1)}, u32[]{:S(2)}, u32[]{:S(2)}) async-start(bf16[8,72,128]{2,1,0:T(8,128)(2,1)} %pack.1), calls=%async_computation | async-start | bytes 294912 | tf_op jit(solution)/shard_map/all_to_all | solution.py:328
  10.2 0.0 copy-done
  10.2 0.0 copy-done.2
  10.2 0.0 copy-done.3
  10.2 0.0 copy-done.5
  10.2 0.0 copy-start.1
  10.2 0.9 %plan.1 = (s32[3,16,128]{2,1,0:T(8,128)S(1)}, bf16[8,128]{1,0:T(8,128)(2,1)S(1)}) custom-call(s32[1,8,8]{2,1,0:T(8,128)S(1)} %copy-done, s32[1,8,16]{2,1,0:T(8,128)S(1)} %copy-done.2, s32[1,1024]{1,0:T(1,128)S(1)} %copy-done.3, s32[8]{0:T(128)S(1)} %copy-done.5), custom_call_target="tpu_custom_call" | custom-call | flops 100000 | bytes 1000000 | tf_op jit(solution)/shard_map/plan/pallas_call | solution.py:335
  11.2 0.0 copy-done.6
  11.2 0.0 copy-done.4
  11.2 0.0 copy-done.1
  11.2 1.1 %place.1 = (bf16[4,256,256]{2,1,0:T(8,128)(2,1)S(1)}, bf16[4,256]{1,0:T(4,128)(2,1)S(1)}, bf16[2,256,256]{2,1,0:T(8,128)(2,1)S(1)}) custom-call(bf16[32,256]{1,0:T(8,128)(2,1)S(1)} %bitcast.1, bf16[1,256]{1,0:T(2,128)(2,1)S(1)} %broadcast_in_dim.3.trans_weight, bf16[4,256]{1,0:T(4,128)(2,1)S(1)} %copy-done.4, bf16[2,256,256]{2,1,0:T(8,128)(2,1)} %far_mid.1), custom_call_target="tpu_custom_call" | custom-call | flops 100000 | bytes 1000000 | tf_op jit(solution)/shard_map/place/pallas_call | solution.py:347
  12.3 1.9 %all-to-all-done.got = bf16[8,72,128]{2,1,0:T(8,128)(2,1)S(1)} async-done(((bf16[8,72,128]{2,1,0:T(8,128)(2,1)}), bf16[8,72,128]{2,1,0:T(8,128)(2,1)S(1)}, u32[]{:S(2)}, u32[]{:S(2)}) %all-to-all-start) | async-done | bytes 147488 | tf_op jit(solution)/shard_map/all_to_all | solution.py:328
  14.3 1.6 %shade.1.refs_3_ = bf16[72,128]{1,0:T(8,128)(2,1)S(1)} custom-call(s32[3,16,128]{2,1,0:T(8,128)S(1)} %get-tuple-element.10.rows, bf16[8,128]{1,0:T(8,128)(2,1)S(1)} %get-tuple-element.11.codes, bf16[8,72,128]{2,1,0:T(8,128)(2,1)S(1)} %all-to-all-done.got, bf16[4,256,256]{2,1,0:T(8,128)(2,1)S(1)} %get-tuple-element.12.w_first, ...), custom_call_target="tpu_custom_call" | custom-call | tf_op jit(solution)/shard_map/shade/pallas_call | solution.py:373
  15.8 0.0 collective-permute-start.2
  15.8 1.6 %collective-permute-start.1 = (bf16[72,128]{1,0:T(8,128)(2,1)S(1)}, bf16[72,128]{1,0:T(8,128)(2,1)S(1)}, u32[]{:S(2)}, u32[]{:S(2)}) collective-permute-start(bf16[72,128]{1,0:T(8,128)(2,1)S(1)} %shade.1.refs_3_), channel_id=1, source_target_pairs={{0,2},{1,3},{2,0},{3,1},{4,6},{5,7},{6,4},{7,5},{8,10},{9,11},{10,... | collective-permute-start | bytes 55304 | tf_op jit(solution)/shard_map/ppermute | solution.py:387
  17.4 0.3 %collective-permute-start = (bf16[72,128]{1,0:T(8,128)(2,1)S(1)}, bf16[72,128]{1,0:T(8,128)(2,1)S(1)}, u32[]{:S(2)}, u32[]{:S(2)}) collective-permute-start(bf16[72,128]{1,0:T(8,128)(2,1)S(1)} %shade.1.refs_3_), channel_id=1, source_target_pairs={{0,1},{1,0},{2,3},{3,2},{4,5},{5,4},{6,7},{7,6},{8,9},{9,8},{10,11... | collective-permute-start | bytes 55304 | tf_op jit(solution)/shard_map/ppermute | solution.py:387
  17.7 0.4 %empty.1.refs_4_ = f32[8,128]{1,0:T(8,128)S(1)} custom-call(bf16[1,256]{1,0:T(2,128)(2,1)S(1)} %broadcast_in_dim.3.trans_weight, bf16[2,256,256]{2,1,0:T(8,128)(2,1)S(1)} %get-tuple-element.13.w_mid, bf16[4,256]{1,0:T(4,128)(2,1)S(1)} %get-tuple-element.14.w_out), custom_call_target="tpu_custom_call" | custom-call | flops 100000 | bytes 1000000 | tf_op jit(solution)/shard_map/empty/pallas_call | solution.py:364
  18.1 1.0 %collective-permute-done.2.refs_2_ = bf16[72,128]{1,0:T(8,128)(2,1)S(1)} collective-permute-done((bf16[72,128]{1,0:T(8,128)(2,1)S(1)}, bf16[72,128]{1,0:T(8,128)(2,1)S(1)}, u32[]{:S(2)}, u32[]{:S(2)}) %collective-permute-start.2) | collective-permute-done | bytes 18464 | tf_op jit(solution)/shard_map/ppermute | solution.py:387
  19.2 0.5 %collective-permute-done.1.refs_1_ = bf16[72,128]{1,0:T(8,128)(2,1)S(1)} collective-permute-done((bf16[72,128]{1,0:T(8,128)(2,1)S(1)}, bf16[72,128]{1,0:T(8,128)(2,1)S(1)}, u32[]{:S(2)}, u32[]{:S(2)}) %collective-permute-start.1) | collective-permute-done | bytes 18464 | tf_op jit(solution)/shard_map/ppermute | solution.py:387
  19.6 0.0 collective-permute-done.refs_0_
  19.6 0.9 %join.1 = bf16[1,4,32,4,128]{4,3,2,1,0:T(4,128)(2,1)} custom-call(bf16[72,128]{1,0:T(8,128)(2,1)S(1)} %collective-permute-done.refs_0_, bf16[72,128]{1,0:T(8,128)(2,1)S(1)} %collective-permute-done.1.refs_1_, bf16[72,128]{1,0:T(8,128)(2,1)S(1)} %collective-permute-done.2.refs_2_, bf16[72,128]{1,0:T(8,128)(2,1)S(1)} %shade.1.refs_3_, f32[8,128]{1,0:T(8,128)S(1)} %empty.1.refs_4_), custom_call_target="tpu_custom_call" | custom-call | tf_op jit(solution)/shard_map/join/pallas_call | solution.py:390
  (1 shorter events, 0.0 us)
Async XLA Ops:
  1.7 8.5 %copy-start = (s32[1,8,8]{2,1,0:T(8,128)S(1)}, s32[1,8,8]{2,1,0:T(8,128)}, u32[]{:S(2)}) copy-start(s32[1,8,8]{2,1,0:T(8,128)} %far_counts.1) | copy-start | bytes 772
  1.7 8.5 %copy-start.2 = (s32[1,8,16]{2,1,0:T(8,128)S(1)}, s32[1,8,16]{2,1,0:T(8,128)}, u32[]{:S(2)}) copy-start(s32[1,8,16]{2,1,0:T(8,128)} %refs_1_.1) | copy-start | bytes 1540
  1.7 8.5 %copy-start.3 = (s32[1,1024]{1,0:T(1,128)S(1)}, s32[1,1024]{1,0:T(1,128)}, u32[]{:S(2)}) copy-start(s32[1,1024]{1,0:T(1,128)} %refs_2_.1) | copy-start | bytes 12292
  1.7 8.5 %copy-start.5 = (s32[8]{0:T(128)S(1)}, s32[8]{0:T(128)}, u32[]{:S(2)}) copy-start(s32[8]{0:T(128)} %refs_3_.1) | copy-start | bytes 100
  1.7 9.4 %copy-start.6 = (bf16[256]{0:T(256)(128)(2,1)S(1)}, bf16[256]{0:T(256)(128)(2,1)}, u32[]{:S(2)}) copy-start(bf16[256]{0:T(256)(128)(2,1)} %param.17) | copy-start | bytes 1540
  1.8 9.4 %copy-start.4 = (bf16[4,256]{1,0:T(4,128)(2,1)S(1)}, bf16[4,256]{1,0:T(4,128)(2,1)}, u32[]{:S(2)}) copy-start(bf16[4,256]{1,0:T(4,128)(2,1)} %far_out.1) | copy-start | bytes 6148
  1.8 12.5 %all-to-all-start = ((bf16[8,72,128]{2,1,0:T(8,128)(2,1)}), bf16[8,72,128]{2,1,0:T(8,128)(2,1)S(1)}, u32[]{:S(2)}, u32[]{:S(2)}) async-start(bf16[8,72,128]{2,1,0:T(8,128)(2,1)} %pack.1), calls=%async_computation | async-start | bytes 294912 | tf_op jit(solution)/shard_map/all_to_all | solution.py:328
  10.2 1.0 %copy-start.1 = (bf16[256,32]{0,1:T(8,128)(2,1)S(1)}, bf16[256,32]{0,1:T(8,128)(2,1)}, u32[]{:S(2)}) copy-start(bf16[256,32]{0,1:T(8,128)(2,1)} %param.16) | copy-start | bytes 49156
  15.8 3.4 %collective-permute-start.2 = (bf16[72,128]{1,0:T(8,128)(2,1)S(1)}, bf16[72,128]{1,0:T(8,128)(2,1)S(1)}, u32[]{:S(2)}, u32[]{:S(2)}) collective-permute-start(bf16[72,128]{1,0:T(8,128)(2,1)S(1)} %shade.1.refs_3_), channel_id=1, source_target_pairs={{0,3},{1,2},{2,1},{3,0},{4,7},{5,6},{6,5},{7,4},{8,11},{9,10},{10,... | collective-permute-start | bytes 55304 | tf_op jit(solution)/shard_map/ppermute | solution.py:387
  15.8 3.8 %collective-permute-start.1 = (bf16[72,128]{1,0:T(8,128)(2,1)S(1)}, bf16[72,128]{1,0:T(8,128)(2,1)S(1)}, u32[]{:S(2)}, u32[]{:S(2)}) collective-permute-start(bf16[72,128]{1,0:T(8,128)(2,1)S(1)} %shade.1.refs_3_), channel_id=1, source_target_pairs={{0,2},{1,3},{2,0},{3,1},{4,6},{5,7},{6,4},{7,5},{8,10},{9,11},{10,... | collective-permute-start | bytes 55304 | tf_op jit(solution)/shard_map/ppermute | solution.py:387
  17.4 2.3 %collective-permute-start = (bf16[72,128]{1,0:T(8,128)(2,1)S(1)}, bf16[72,128]{1,0:T(8,128)(2,1)S(1)}, u32[]{:S(2)}, u32[]{:S(2)}) collective-permute-start(bf16[72,128]{1,0:T(8,128)(2,1)S(1)} %shade.1.refs_3_), channel_id=1, source_target_pairs={{0,1},{1,0},{2,3},{3,2},{4,5},{5,4},{6,7},{7,6},{8,9},{9,8},{10,11... | collective-permute-start | bytes 55304 | tf_op jit(solution)/shard_map/ppermute | solution.py:387
where the time goes:
time: 20.8 us; the launch traced here: 20.5 us
  starting transfers between devices  10.3 us (50%)
  Pallas kernels  6.58 us (32%)
  waiting for transfers between devices  3.47 us (17%)
    all_to_all x1, starting transfers between devices, compact_device(): lax.all_to_all(sends, 'slab', split_axis=0, concat_axis=0, axis_index_gro...  8.41 us
    all_to_all x1, waiting for transfers between devices, compact_device(): lax.all_to_all(sends, 'slab', split_axis=0, concat_axis=0, axis_index_gro...  1.94 us
    ppermute x3, starting transfers between devices, compact_device(): lax.ppermute(shaded, 'strip', [(s, s ^ k) for s in range(n_strip)])  1.88 us
    pallas_call x1, Pallas kernels, compact_device(): pl.pallas_call(pack_kernel, out_shape=jax.ShapeDtypeStruct((n_slab, messa...  1.69 us
    pallas_call x1, Pallas kernels, compact_device(): pl.pallas_call(shade_kernel, out_shape=jax.ShapeDtypeStruct((items * outs...  1.55 us
    ppermute x3, waiting for transfers between devices, compact_device(): lax.ppermute(shaded, 'strip', [(s, s ^ k) for s in range(n_strip)])  1.53 us
    pallas_call x1, Pallas kernels, compact_device(): pl.pallas_call(place_kernel, out_shape=[jax.ShapeDtypeStruct((GROUP, 2 *...  1.1 us
    pallas_call x1, Pallas kernels, compact_device(): pl.pallas_call(functools.partial(plan_kernel, n_slab, slots), out_shape=[...  0.93 us
  transfers between devices with their start and end apart: 4, of which 3 were waited for; matrix products, arithmetic and copies ran while one was open for 0% of the time, Pallas kernels for 12%

commit v1 on v0

--- a/solution.py
+++ b/solution.py
@@ -89,9 +89,8 @@
 
 
 def exchange_order(n_slab):
-    half = n_slab // 2
-    flip = 1 if half % 2 == 0 else 0
-    return [s for i in range(half) for s in (half + (i ^ flip), i)]
+    central = n_slab // 2 + 1
+    return [central] + [s for s in reversed(range(n_slab)) if s != central]
 
 
 def pack_kernel(far_counts, far_colors, far_transmit, sends, counts, colors, transmit, sems):

time: 20.8 us -> 21.2 us (1.019)
  waiting for transfers between devices: 3.47 us -> 3.85 us
    all_to_all x1, waiting for transfers between devices: 1.94 us -> 2.32 us  [compact_device(): lax.all_to_all(sends, 'slab', split_axis=0, concat_axis=0, axis_index_gro...]
where the time goes in v1:
time: 21.2 us; the launch traced here: 21 us
  starting transfers between devices  10.3 us (49%)
  Pallas kernels  6.59 us (31%)
  waiting for transfers between devices  3.85 us (18%)
    all_to_all x1, starting transfers between devices, compact_device(): lax.all_to_all(sends, 'slab', split_axis=0, concat_axis=0, axis_index_gro...  8.45 us
    all_to_all x1, waiting for transfers between devices, compact_device(): lax.all_to_all(sends, 'slab', split_axis=0, concat_axis=0, axis_index_gro...  2.32 us
    ppermute x3, starting transfers between devices, compact_device(): lax.ppermute(shaded, 'strip', [(s, s ^ k) for s in range(n_strip)])  1.88 us
    pallas_call x1, Pallas kernels, compact_device(): pl.pallas_call(pack_kernel, out_shape=jax.ShapeDtypeStruct((n_slab, messa...  1.69 us
    pallas_call x1, Pallas kernels, compact_device(): pl.pallas_call(shade_kernel, out_shape=jax.ShapeDtypeStruct((items * outs...  1.55 us
    ppermute x3, waiting for transfers between devices, compact_device(): lax.ppermute(shaded, 'strip', [(s, s ^ k) for s in range(n_strip)])  1.53 us
    pallas_call x1, Pallas kernels, compact_device(): pl.pallas_call(place_kernel, out_shape=[jax.ShapeDtypeStruct((GROUP, 2 *...  1.1 us
    pallas_call x1, Pallas kernels, compact_device(): pl.pallas_call(functools.partial(plan_kernel, n_slab, slots), out_shape=[...  0.93 us
  transfers between devices with their start and end apart: 4, of which 3 were waited for; matrix products, arithmetic and copies ran while one was open for 0% of the time, Pallas kernels for 12%

profile of v1, /device:TPU:0, one launch (start us, length us, event | category | flops | bytes accessed | tf_op | source)
XLA Modules:
  0.0 21.0 jit_solution(16464014942636022310)
XLA Ops:
  0.0 1.7 %pack.1 = bf16[8,72,128]{2,1,0:T(8,128)(2,1)} custom-call(s32[1,8,8]{2,1,0:T(8,128)} %far_counts.1, bf16[1,1,16,32,128]{4,3,2,1,0:T(8,128)(2,1)} %far_colors.1, bf16[1,1,16,128]{3,2,1,0:T(8,128)(2,1)} %far_transmit.1), custom_call_target="tpu_custom_call" | custom-call | tf_op jit(solution)/shard_map/pack/pallas_call | solution.py:312
  1.7 0.0 copy-start
  1.7 0.0 copy-start.2
  1.7 0.0 copy-start.3
  1.7 0.0 copy-start.5
  1.7 0.0 copy-start.6
  1.8 0.0 copy-start.4
  1.8 8.5 %all-to-all-start = ((bf16[8,72,128]{2,1,0:T(8,128)(2,1)}), bf16[8,72,128]{2,1,0:T(8,128)(2,1)S(1)}, u32[]{:S(2)}, u32[]{:S(2)}) async-start(bf16[8,72,128]{2,1,0:T(8,128)(2,1)} %pack.1), calls=%async_computation | async-start | bytes 294912 | tf_op jit(solution)/shard_map/all_to_all | solution.py:327
  10.2 0.0 copy-done
  10.2 0.0 copy-done.2
  10.2 0.0 copy-done.3
  10.2 0.0 copy-done.5
  10.3 0.0 copy-start.1
  10.3 0.9 %plan.1 = (s32[3,16,128]{2,1,0:T(8,128)S(1)}, bf16[8,128]{1,0:T(8,128)(2,1)S(1)}) custom-call(s32[1,8,8]{2,1,0:T(8,128)S(1)} %copy-done, s32[1,8,16]{2,1,0:T(8,128)S(1)} %copy-done.2, s32[1,1024]{1,0:T(1,128)S(1)} %copy-done.3, s32[8]{0:T(128)S(1)} %copy-done.5), custom_call_target="tpu_custom_call" | custom-call | flops 100000 | bytes 1000000 | tf_op jit(solution)/shard_map/plan/pallas_call | solution.py:334
  11.2 0.0 copy-done.6
  11.2 0.0 copy-done.4
  11.2 0.0 copy-done.1
  11.2 1.1 %place.1 = (bf16[4,256,256]{2,1,0:T(8,128)(2,1)S(1)}, bf16[4,256]{1,0:T(4,128)(2,1)S(1)}, bf16[2,256,256]{2,1,0:T(8,128)(2,1)S(1)}) custom-call(bf16[32,256]{1,0:T(8,128)(2,1)S(1)} %bitcast.1, bf16[1,256]{1,0:T(2,128)(2,1)S(1)} %broadcast_in_dim.3.trans_weight, bf16[4,256]{1,0:T(4,128)(2,1)S(1)} %copy-done.4, bf16[2,256,256]{2,1,0:T(8,128)(2,1)} %far_mid.1), custom_call_target="tpu_custom_call" | custom-call | flops 100000 | bytes 1000000 | tf_op jit(solution)/shard_map/place/pallas_call | solution.py:346
  12.4 2.3 %all-to-all-done.got = bf16[8,72,128]{2,1,0:T(8,128)(2,1)S(1)} async-done(((bf16[8,72,128]{2,1,0:T(8,128)(2,1)}), bf16[8,72,128]{2,1,0:T(8,128)(2,1)S(1)}, u32[]{:S(2)}, u32[]{:S(2)}) %all-to-all-start) | async-done | bytes 147488 | tf_op jit(solution)/shard_map/all_to_all | solution.py:327
  14.7 1.6 %shade.1.refs_3_ = bf16[72,128]{1,0:T(8,128)(2,1)S(1)} custom-call(s32[3,16,128]{2,1,0:T(8,128)S(1)} %get-tuple-element.10.rows, bf16[8,128]{1,0:T(8,128)(2,1)S(1)} %get-tuple-element.11.codes, bf16[8,72,128]{2,1,0:T(8,128)(2,1)S(1)} %all-to-all-done.got, bf16[4,256,256]{2,1,0:T(8,128)(2,1)S(1)} %get-tuple-element.12.w_first, ...), custom_call_target="tpu_custom_call" | custom-call | tf_op jit(solution)/shard_map/shade/pallas_call | solution.py:372
  16.2 0.0 collective-permute-start.2
  16.2 1.6 %collective-permute-start.1 = (bf16[72,128]{1,0:T(8,128)(2,1)S(1)}, bf16[72,128]{1,0:T(8,128)(2,1)S(1)}, u32[]{:S(2)}, u32[]{:S(2)}) collective-permute-start(bf16[72,128]{1,0:T(8,128)(2,1)S(1)} %shade.1.refs_3_), channel_id=1, source_target_pairs={{0,2},{1,3},{2,0},{3,1},{4,6},{5,7},{6,4},{7,5},{8,10},{9,11},{10,... | collective-permute-start | bytes 55304 | tf_op jit(solution)/shard_map/ppermute | solution.py:386
  17.8 0.3 %collective-permute-start = (bf16[72,128]{1,0:T(8,128)(2,1)S(1)}, bf16[72,128]{1,0:T(8,128)(2,1)S(1)}, u32[]{:S(2)}, u32[]{:S(2)}) collective-permute-start(bf16[72,128]{1,0:T(8,128)(2,1)S(1)} %shade.1.refs_3_), channel_id=1, source_target_pairs={{0,1},{1,0},{2,3},{3,2},{4,5},{5,4},{6,7},{7,6},{8,9},{9,8},{10,11... | collective-permute-start | bytes 55304 | tf_op jit(solution)/shard_map/ppermute | solution.py:386
  18.1 0.4 %empty.1.refs_4_ = f32[8,128]{1,0:T(8,128)S(1)} custom-call(bf16[1,256]{1,0:T(2,128)(2,1)S(1)} %broadcast_in_dim.3.trans_weight, bf16[2,256,256]{2,1,0:T(8,128)(2,1)S(1)} %get-tuple-element.13.w_mid, bf16[4,256]{1,0:T(4,128)(2,1)S(1)} %get-tuple-element.14.w_out), custom_call_target="tpu_custom_call" | custom-call | flops 100000 | bytes 1000000 | tf_op jit(solution)/shard_map/empty/pallas_call | solution.py:363
  18.5 1.0 %collective-permute-done.2.refs_2_ = bf16[72,128]{1,0:T(8,128)(2,1)S(1)} collective-permute-done((bf16[72,128]{1,0:T(8,128)(2,1)S(1)}, bf16[72,128]{1,0:T(8,128)(2,1)S(1)}, u32[]{:S(2)}, u32[]{:S(2)}) %collective-permute-start.2) | collective-permute-done | bytes 18464 | tf_op jit(solution)/shard_map/ppermute | solution.py:386
  19.6 0.5 %collective-permute-done.1.refs_1_ = bf16[72,128]{1,0:T(8,128)(2,1)S(1)} collective-permute-done((bf16[72,128]{1,0:T(8,128)(2,1)S(1)}, bf16[72,128]{1,0:T(8,128)(2,1)S(1)}, u32[]{:S(2)}, u32[]{:S(2)}) %collective-permute-start.1) | collective-permute-done | bytes 18464 | tf_op jit(solution)/shard_map/ppermute | solution.py:386
  20.1 0.0 collective-permute-done.refs_0_
  20.1 0.9 %join.1 = bf16[1,4,32,4,128]{4,3,2,1,0:T(4,128)(2,1)} custom-call(bf16[72,128]{1,0:T(8,128)(2,1)S(1)} %collective-permute-done.refs_0_, bf16[72,128]{1,0:T(8,128)(2,1)S(1)} %collective-permute-done.1.refs_1_, bf16[72,128]{1,0:T(8,128)(2,1)S(1)} %collective-permute-done.2.refs_2_, bf16[72,128]{1,0:T(8,128)(2,1)S(1)} %shade.1.refs_3_, f32[8,128]{1,0:T(8,128)S(1)} %empty.1.refs_4_), custom_call_target="tpu_custom_call" | custom-call | tf_op jit(solution)/shard_map/join/pallas_call | solution.py:389
  (1 shorter events, 0.0 us)
Async XLA Ops:
  1.7 8.5 %copy-start = (s32[1,8,8]{2,1,0:T(8,128)S(1)}, s32[1,8,8]{2,1,0:T(8,128)}, u32[]{:S(2)}) copy-start(s32[1,8,8]{2,1,0:T(8,128)} %far_counts.1) | copy-start | bytes 772
  1.7 8.5 %copy-start.2 = (s32[1,8,16]{2,1,0:T(8,128)S(1)}, s32[1,8,16]{2,1,0:T(8,128)}, u32[]{:S(2)}) copy-start(s32[1,8,16]{2,1,0:T(8,128)} %refs_1_.1) | copy-start | bytes 1540
  1.7 8.5 %copy-start.3 = (s32[1,1024]{1,0:T(1,128)S(1)}, s32[1,1024]{1,0:T(1,128)}, u32[]{:S(2)}) copy-start(s32[1,1024]{1,0:T(1,128)} %refs_2_.1) | copy-start | bytes 12292
  1.7 8.5 %copy-start.5 = (s32[8]{0:T(128)S(1)}, s32[8]{0:T(128)}, u32[]{:S(2)}) copy-start(s32[8]{0:T(128)} %refs_3_.1) | copy-start | bytes 100
  1.7 9.5 %copy-start.6 = (bf16[256]{0:T(256)(128)(2,1)S(1)}, bf16[256]{0:T(256)(128)(2,1)}, u32[]{:S(2)}) copy-start(bf16[256]{0:T(256)(128)(2,1)} %param.17) | copy-start | bytes 1540
  1.8 9.5 %copy-start.4 = (bf16[4,256]{1,0:T(4,128)(2,1)S(1)}, bf16[4,256]{1,0:T(4,128)(2,1)}, u32[]{:S(2)}) copy-start(bf16[4,256]{1,0:T(4,128)(2,1)} %far_out.1) | copy-start | bytes 6148
  1.8 12.9 %all-to-all-start = ((bf16[8,72,128]{2,1,0:T(8,128)(2,1)}), bf16[8,72,128]{2,1,0:T(8,128)(2,1)S(1)}, u32[]{:S(2)}, u32[]{:S(2)}) async-start(bf16[8,72,128]{2,1,0:T(8,128)(2,1)} %pack.1), calls=%async_computation | async-start | bytes 294912 | tf_op jit(solution)/shard_map/all_to_all | solution.py:327
  10.3 1.0 %copy-start.1 = (bf16[256,32]{0,1:T(8,128)(2,1)S(1)}, bf16[256,32]{0,1:T(8,128)(2,1)}, u32[]{:S(2)}) copy-start(bf16[256,32]{0,1:T(8,128)(2,1)} %param.16) | copy-start | bytes 49156
  16.2 3.4 %collective-permute-start.2 = (bf16[72,128]{1,0:T(8,128)(2,1)S(1)}, bf16[72,128]{1,0:T(8,128)(2,1)S(1)}, u32[]{:S(2)}, u32[]{:S(2)}) collective-permute-start(bf16[72,128]{1,0:T(8,128)(2,1)S(1)} %shade.1.refs_3_), channel_id=1, source_target_pairs={{0,3},{1,2},{2,1},{3,0},{4,7},{5,6},{6,5},{7,4},{8,11},{9,10},{10,... | collective-permute-start | bytes 55304 | tf_op jit(solution)/shard_map/ppermute | solution.py:386
  16.2 3.8 %collective-permute-start.1 = (bf16[72,128]{1,0:T(8,128)(2,1)S(1)}, bf16[72,128]{1,0:T(8,128)(2,1)S(1)}, u32[]{:S(2)}, u32[]{:S(2)}) collective-permute-start(bf16[72,128]{1,0:T(8,128)(2,1)S(1)} %shade.1.refs_3_), channel_id=1, source_target_pairs={{0,2},{1,3},{2,0},{3,1},{4,6},{5,7},{6,4},{7,5},{8,10},{9,11},{10,... | collective-permute-start | bytes 55304 | tf_op jit(solution)/shard_map/ppermute | solution.py:386
  17.8 2.3 %collective-permute-start = (bf16[72,128]{1,0:T(8,128)(2,1)S(1)}, bf16[72,128]{1,0:T(8,128)(2,1)S(1)}, u32[]{:S(2)}, u32[]{:S(2)}) collective-permute-start(bf16[72,128]{1,0:T(8,128)(2,1)S(1)} %shade.1.refs_3_), channel_id=1, source_target_pairs={{0,1},{1,0},{2,3},{3,2},{4,5},{5,4},{6,7},{7,6},{8,9},{9,8},{10,11... | collective-permute-start | bytes 55304 | tf_op jit(solution)/shard_map/ppermute | solution.py:386

commit v2 on v0

--- a/solution.py
+++ b/solution.py
@@ -86,6 +86,7 @@
 VMEM = pltpu.VMEM
 ROWS = 8
 GROUP = 4
+PARTS = 4
 
 
 def exchange_order(n_slab):
@@ -97,13 +98,17 @@
 def pack_kernel(far_counts, far_colors, far_transmit, sends, counts, colors, transmit, sems):
     n_slab = sends.shape[0]
     place = [exchange_order(n_slab).index(c) for c in range(n_slab)]
-    slots, feats, span = colors.shape[2:]
+    slots, feats, span = colors.shape
     me = lax.axis_index("slab")
+    part = slots // PARTS
     copies = [
-        pltpu.make_async_copy(far, near, sems.at[i])
-        for i, (far, near) in enumerate(
-            ((far_counts, counts), (far_transmit, transmit), (far_colors, colors))
+        pltpu.make_async_copy(far_counts, counts, sems.at[0]),
+        pltpu.make_async_copy(far_transmit, transmit, sems.at[1]),
+    ] + [
+        pltpu.make_async_copy(
+            far_colors.at[0, 0, pl.ds(p * part, part)], colors.at[pl.ds(p * part, part)], sems.at[2 + p]
         )
+        for p in range(PARTS)
     ]
     for copy in copies:
         copy.start()
@@ -124,15 +129,20 @@
     for c in range(n_slab):
         tail = tails[c * ROWS : (c + 1) * ROWS]
         sends[place[c], pl.ds(MOST * feats, ROWS), :] = tail.astype(jnp.bfloat16)
-    copies[2].wait()
+    waited = 0
     for c in range(n_slab):
         off = jnp.broadcast_to(offs[c], (feats, span)).astype(jnp.bfloat16)
         for r in range(MOST):
             last = min(MOST * c + r, slots - 1)
-            block = colors[0, 0, last]
+            while waited * part <= last:
+                copies[2 + waited].wait()
+                waited += 1
+            block = colors[last]
             for slot in range(r, last):
-                block = jnp.where(off == slot - r, colors[0, 0, slot], block)
+                block = jnp.where(off == slot - r, colors[slot], block)
             sends[place[c], pl.ds(r * feats, feats), :] = block
+    for copy in copies[2 + waited :]:
+        copy.wait()
 
 
 def plan_kernel(n_slab, slots, *refs):
@@ -267,7 +277,7 @@
 
 
 def join_kernel(*refs):
-    *got, empty, out = refs
+    *got, empty, out, held, sems = refs
     _, n_strip, tile, outs, span = out.shape
     lines = tile * outs
     count = got[0].shape[0] - ROWS
@@ -276,6 +286,7 @@
     chan = lax.broadcasted_iota(jnp.int32, (lines, count), 1) % outs
     filler = jnp.concatenate([empty[...]] * (lines // ROWS))
     ones = jnp.ones((count, span), jnp.bfloat16)
+    copies = []
     for k in range(n_strip):
         pos = got[k][pl.ds(count, ROWS), :].astype(jnp.float32)[:1, :count].astype(jnp.int32)
         hit = pos * outs + chan == want
@@ -284,7 +295,14 @@
         placed = jnp.dot(pick, blocks, preferred_element_type=jnp.float32)
         filled = jnp.dot(pick, ones, preferred_element_type=jnp.float32)
         value = jnp.where(filled > 0.5, placed, filler)
-        out[0, me ^ ((k + 1) % n_strip)] = value.reshape(tile, outs, span).astype(jnp.bfloat16)
+        held[k] = value.reshape(tile, outs, span).astype(jnp.bfloat16)
+        copy = pltpu.make_async_copy(
+            held.at[k], out.at[0, me ^ ((k + 1) % n_strip)], sems.at[k]
+        )
+        copy.start()
+        copies.append(copy)
+    for copy in copies:
+        copy.wait()
 
 
 def compact_device(
@@ -317,9 +335,9 @@
         out_specs=vmem,
         scratch_shapes=[
             pltpu.VMEM(pair_counts.shape, jnp.int32),
-            pltpu.VMEM(colors.shape, colors.dtype),
+            pltpu.VMEM(colors.shape[2:], colors.dtype),
             pltpu.VMEM(transmit.shape, transmit.dtype),
-            pltpu.SemaphoreType.DMA((3,)),
+            pltpu.SemaphoreType.DMA((2 + PARTS,)),
         ],
         compiler_params=small,
         name="pack",
@@ -391,7 +409,11 @@
         join_kernel,
         out_shape=jax.ShapeDtypeStruct((1, n_strip, LB // n_strip, outs, span), jnp.bfloat16),
         in_specs=[vmem] * (n_strip + 1),
-        out_specs=pl.BlockSpec(),
+        out_specs=pl.BlockSpec(memory_space=pl.ANY),
+        scratch_shapes=[
+            pltpu.VMEM((n_strip, LB // n_strip, outs, span), jnp.bfloat16),
+            pltpu.SemaphoreType.DMA((n_strip,)),
+        ],
         compiler_params=small,
         name="join",
     )(*tiles, empty)

time: 20.8 us -> 20.8 us (level)
  no operation moved by 1% of the time
where the time goes in v2:
time: 20.8 us; the launch traced here: 20.5 us
  starting transfers between devices  10.3 us (50%)
  Pallas kernels  6.59 us (32%)
  waiting for transfers between devices  3.47 us (17%)
    all_to_all x1, starting transfers between devices, compact_device(): lax.all_to_all(sends, 'slab', split_axis=0, concat_axis=0, axis_index_gro...  8.41 us
    all_to_all x1, waiting for transfers between devices, compact_device(): lax.all_to_all(sends, 'slab', split_axis=0, concat_axis=0, axis_index_gro...  1.94 us
    ppermute x3, starting transfers between devices, compact_device(): lax.ppermute(shaded, 'strip', [(s, s ^ k) for s in range(n_strip)])  1.88 us
    pallas_call x1, Pallas kernels, compact_device(): pl.pallas_call(pack_kernel, out_shape=jax.ShapeDtypeStruct((n_slab, messa...  1.7 us
    pallas_call x1, Pallas kernels, compact_device(): pl.pallas_call(shade_kernel, out_shape=jax.ShapeDtypeStruct((items * outs...  1.56 us
    ppermute x3, waiting for transfers between devices, compact_device(): lax.ppermute(shaded, 'strip', [(s, s ^ k) for s in range(n_strip)])  1.53 us
    pallas_call x1, Pallas kernels, compact_device(): pl.pallas_call(place_kernel, out_shape=[jax.ShapeDtypeStruct((GROUP, 2 *...  1.1 us
    pallas_call x1, Pallas kernels, compact_device(): pl.pallas_call(functools.partial(plan_kernel, n_slab, slots), out_shape=[...  0.93 us
  transfers between devices with their start and end apart: 4, of which 3 were waited for; matrix products, arithmetic and copies ran while one was open for 0% of the time, Pallas kernels for 12%

profile of v2, /device:TPU:0, one launch (start us, length us, event | category | flops | bytes accessed | tf_op | source)
XLA Modules:
  0.0 20.5 jit_solution(2483649368321851077)
XLA Ops:
  0.0 1.7 %pack.1 = bf16[8,72,128]{2,1,0:T(8,128)(2,1)} custom-call(s32[1,8,8]{2,1,0:T(8,128)} %far_counts.1, bf16[1,1,16,32,128]{4,3,2,1,0:T(8,128)(2,1)} %far_colors.1, bf16[1,1,16,128]{3,2,1,0:T(8,128)(2,1)} %far_transmit.1), custom_call_target="tpu_custom_call" | custom-call | tf_op jit(solution)/shard_map/pack/pallas_call | solution.py:331
  1.7 0.0 copy-start
  1.7 0.0 copy-start.2
  1.7 0.0 copy-start.3
  1.7 0.0 copy-start.5
  1.8 0.0 copy-start.6
  1.8 0.0 copy-start.4
  1.8 8.4 %all-to-all-start = ((bf16[8,72,128]{2,1,0:T(8,128)(2,1)}), bf16[8,72,128]{2,1,0:T(8,128)(2,1)S(1)}, u32[]{:S(2)}, u32[]{:S(2)}) async-start(bf16[8,72,128]{2,1,0:T(8,128)(2,1)} %pack.1), calls=%async_computation | async-start | bytes 294912 | tf_op jit(solution)/shard_map/all_to_all | solution.py:346
  10.2 0.0 copy-done
  10.2 0.0 copy-done.2
  10.2 0.0 copy-done.3
  10.2 0.0 copy-done.5
  10.2 0.0 copy-start.1
  10.2 0.9 %plan.1 = (s32[3,16,128]{2,1,0:T(8,128)S(1)}, bf16[8,128]{1,0:T(8,128)(2,1)S(1)}) custom-call(s32[1,8,8]{2,1,0:T(8,128)S(1)} %copy-done, s32[1,8,16]{2,1,0:T(8,128)S(1)} %copy-done.2, s32[1,1024]{1,0:T(1,128)S(1)} %copy-done.3, s32[8]{0:T(128)S(1)} %copy-done.5), custom_call_target="tpu_custom_call" | custom-call | flops 100000 | bytes 1000000 | tf_op jit(solution)/shard_map/plan/pallas_call | solution.py:353
  11.2 0.0 copy-done.6
  11.2 0.0 copy-done.4
  11.2 0.0 copy-done.1
  11.2 1.1 %place.1 = (bf16[4,256,256]{2,1,0:T(8,128)(2,1)S(1)}, bf16[4,256]{1,0:T(4,128)(2,1)S(1)}, bf16[2,256,256]{2,1,0:T(8,128)(2,1)S(1)}) custom-call(bf16[32,256]{1,0:T(8,128)(2,1)S(1)} %bitcast.1, bf16[1,256]{1,0:T(2,128)(2,1)S(1)} %broadcast_in_dim.3.trans_weight, bf16[4,256]{1,0:T(4,128)(2,1)S(1)} %copy-done.4, bf16[2,256,256]{2,1,0:T(8,128)(2,1)} %far_mid.1), custom_call_target="tpu_custom_call" | custom-call | flops 100000 | bytes 1000000 | tf_op jit(solution)/shard_map/place/pallas_call | solution.py:365
  12.3 1.9 %all-to-all-done.got = bf16[8,72,128]{2,1,0:T(8,128)(2,1)S(1)} async-done(((bf16[8,72,128]{2,1,0:T(8,128)(2,1)}), bf16[8,72,128]{2,1,0:T(8,128)(2,1)S(1)}, u32[]{:S(2)}, u32[]{:S(2)}) %all-to-all-start) | async-done | bytes 147488 | tf_op jit(solution)/shard_map/all_to_all | solution.py:346
  14.3 1.6 %shade.1.refs_3_ = bf16[72,128]{1,0:T(8,128)(2,1)S(1)} custom-call(s32[3,16,128]{2,1,0:T(8,128)S(1)} %get-tuple-element.10.rows, bf16[8,128]{1,0:T(8,128)(2,1)S(1)} %get-tuple-element.11.codes, bf16[8,72,128]{2,1,0:T(8,128)(2,1)S(1)} %all-to-all-done.got, bf16[4,256,256]{2,1,0:T(8,128)(2,1)S(1)} %get-tuple-element.12.w_first, ...), custom_call_target="tpu_custom_call" | custom-call | tf_op jit(solution)/shard_map/shade/pallas_call | solution.py:391
  15.8 0.0 collective-permute-start.2
  15.8 1.6 %collective-permute-start.1 = (bf16[72,128]{1,0:T(8,128)(2,1)S(1)}, bf16[72,128]{1,0:T(8,128)(2,1)S(1)}, u32[]{:S(2)}, u32[]{:S(2)}) collective-permute-start(bf16[72,128]{1,0:T(8,128)(2,1)S(1)} %shade.1.refs_3_), channel_id=1, source_target_pairs={{0,2},{1,3},{2,0},{3,1},{4,6},{5,7},{6,4},{7,5},{8,10},{9,11},{10,... | collective-permute-start | bytes 55304 | tf_op jit(solution)/shard_map/ppermute | solution.py:405
  17.4 0.3 %collective-permute-start = (bf16[72,128]{1,0:T(8,128)(2,1)S(1)}, bf16[72,128]{1,0:T(8,128)(2,1)S(1)}, u32[]{:S(2)}, u32[]{:S(2)}) collective-permute-start(bf16[72,128]{1,0:T(8,128)(2,1)S(1)} %shade.1.refs_3_), channel_id=1, source_target_pairs={{0,1},{1,0},{2,3},{3,2},{4,5},{5,4},{6,7},{7,6},{8,9},{9,8},{10,11... | collective-permute-start | bytes 55304 | tf_op jit(solution)/shard_map/ppermute | solution.py:405
  17.7 0.4 %empty.1.refs_4_ = f32[8,128]{1,0:T(8,128)S(1)} custom-call(bf16[1,256]{1,0:T(2,128)(2,1)S(1)} %broadcast_in_dim.3.trans_weight, bf16[2,256,256]{2,1,0:T(8,128)(2,1)S(1)} %get-tuple-element.13.w_mid, bf16[4,256]{1,0:T(4,128)(2,1)S(1)} %get-tuple-element.14.w_out), custom_call_target="tpu_custom_call" | custom-call | flops 100000 | bytes 1000000 | tf_op jit(solution)/shard_map/empty/pallas_call | solution.py:382
  18.1 1.0 %collective-permute-done.2.refs_2_ = bf16[72,128]{1,0:T(8,128)(2,1)S(1)} collective-permute-done((bf16[72,128]{1,0:T(8,128)(2,1)S(1)}, bf16[72,128]{1,0:T(8,128)(2,1)S(1)}, u32[]{:S(2)}, u32[]{:S(2)}) %collective-permute-start.2) | collective-permute-done | bytes 18464 | tf_op jit(solution)/shard_map/ppermute | solution.py:405
  19.2 0.5 %collective-permute-done.1.refs_1_ = bf16[72,128]{1,0:T(8,128)(2,1)S(1)} collective-permute-done((bf16[72,128]{1,0:T(8,128)(2,1)S(1)}, bf16[72,128]{1,0:T(8,128)(2,1)S(1)}, u32[]{:S(2)}, u32[]{:S(2)}) %collective-permute-start.1) | collective-permute-done | bytes 18464 | tf_op jit(solution)/shard_map/ppermute | solution.py:405
  19.7 0.0 collective-permute-done.refs_0_
  19.7 0.9 %join.1 = bf16[1,4,32,4,128]{4,3,2,1,0:T(4,128)(2,1)} custom-call(bf16[72,128]{1,0:T(8,128)(2,1)S(1)} %collective-permute-done.refs_0_, bf16[72,128]{1,0:T(8,128)(2,1)S(1)} %collective-permute-done.1.refs_1_, bf16[72,128]{1,0:T(8,128)(2,1)S(1)} %collective-permute-done.2.refs_2_, bf16[72,128]{1,0:T(8,128)(2,1)S(1)} %shade.1.refs_3_, f32[8,128]{1,0:T(8,128)S(1)} %empty.1.refs_4_), custom_call_target="tpu_custom_call" | custom-call | tf_op jit(solution)/shard_map/join/pallas_call | solution.py:408
  (1 shorter events, 0.0 us)
Async XLA Ops:
  1.7 8.5 %copy-start = (s32[1,8,8]{2,1,0:T(8,128)S(1)}, s32[1,8,8]{2,1,0:T(8,128)}, u32[]{:S(2)}) copy-start(s32[1,8,8]{2,1,0:T(8,128)} %far_counts.1) | copy-start | bytes 772
  1.7 8.5 %copy-start.2 = (s32[1,8,16]{2,1,0:T(8,128)S(1)}, s32[1,8,16]{2,1,0:T(8,128)}, u32[]{:S(2)}) copy-start(s32[1,8,16]{2,1,0:T(8,128)} %refs_1_.1) | copy-start | bytes 1540
  1.7 8.5 %copy-start.3 = (s32[1,1024]{1,0:T(1,128)S(1)}, s32[1,1024]{1,0:T(1,128)}, u32[]{:S(2)}) copy-start(s32[1,1024]{1,0:T(1,128)} %refs_2_.1) | copy-start | bytes 12292
  1.7 8.5 %copy-start.5 = (s32[8]{0:T(128)S(1)}, s32[8]{0:T(128)}, u32[]{:S(2)}) copy-start(s32[8]{0:T(128)} %refs_3_.1) | copy-start | bytes 100
  1.8 9.4 %copy-start.6 = (bf16[256]{0:T(256)(128)(2,1)S(1)}, bf16[256]{0:T(256)(128)(2,1)}, u32[]{:S(2)}) copy-start(bf16[256]{0:T(256)(128)(2,1)} %param.17) | copy-start | bytes 1540
  1.8 9.4 %copy-start.4 = (bf16[4,256]{1,0:T(4,128)(2,1)S(1)}, bf16[4,256]{1,0:T(4,128)(2,1)}, u32[]{:S(2)}) copy-start(bf16[4,256]{1,0:T(4,128)(2,1)} %far_out.1) | copy-start | bytes 6148
  1.8 12.5 %all-to-all-start = ((bf16[8,72,128]{2,1,0:T(8,128)(2,1)}), bf16[8,72,128]{2,1,0:T(8,128)(2,1)S(1)}, u32[]{:S(2)}, u32[]{:S(2)}) async-start(bf16[8,72,128]{2,1,0:T(8,128)(2,1)} %pack.1), calls=%async_computation | async-start | bytes 294912 | tf_op jit(solution)/shard_map/all_to_all | solution.py:346
  10.2 1.0 %copy-start.1 = (bf16[256,32]{0,1:T(8,128)(2,1)S(1)}, bf16[256,32]{0,1:T(8,128)(2,1)}, u32[]{:S(2)}) copy-start(bf16[256,32]{0,1:T(8,128)(2,1)} %param.16) | copy-start | bytes 49156
  15.8 3.4 %collective-permute-start.2 = (bf16[72,128]{1,0:T(8,128)(2,1)S(1)}, bf16[72,128]{1,0:T(8,128)(2,1)S(1)}, u32[]{:S(2)}, u32[]{:S(2)}) collective-permute-start(bf16[72,128]{1,0:T(8,128)(2,1)S(1)} %shade.1.refs_3_), channel_id=1, source_target_pairs={{0,3},{1,2},{2,1},{3,0},{4,7},{5,6},{6,5},{7,4},{8,11},{9,10},{10,... | collective-permute-start | bytes 55304 | tf_op jit(solution)/shard_map/ppermute | solution.py:405
  15.8 3.8 %collective-permute-start.1 = (bf16[72,128]{1,0:T(8,128)(2,1)S(1)}, bf16[72,128]{1,0:T(8,128)(2,1)S(1)}, u32[]{:S(2)}, u32[]{:S(2)}) collective-permute-start(bf16[72,128]{1,0:T(8,128)(2,1)S(1)} %shade.1.refs_3_), channel_id=1, source_target_pairs={{0,2},{1,3},{2,0},{3,1},{4,6},{5,7},{6,4},{7,5},{8,10},{9,11},{10,... | collective-permute-start | bytes 55304 | tf_op jit(solution)/shard_map/ppermute | solution.py:405
  17.4 2.3 %collective-permute-start = (bf16[72,128]{1,0:T(8,128)(2,1)S(1)}, bf16[72,128]{1,0:T(8,128)(2,1)S(1)}, u32[]{:S(2)}, u32[]{:S(2)}) collective-permute-start(bf16[72,128]{1,0:T(8,128)(2,1)S(1)} %shade.1.refs_3_), channel_id=1, source_target_pairs={{0,1},{1,0},{2,3},{3,2},{4,5},{5,4},{6,7},{7,6},{8,9},{9,8},{10,11... | collective-permute-start | bytes 55304 | tf_op jit(solution)/shard_map/ppermute | solution.py:405

commit v3 on v2

--- a/solution.py
+++ b/solution.py
@@ -203,9 +203,14 @@
     return (u + u * jnp.tanh(u)).astype(jnp.bfloat16)
 
 
-def later_layers(h, w_mid, w_out):
+def silu_half_short(u):
+    u = u.astype(jnp.bfloat16)
+    return u + u * jnp.tanh(u)
+
+
+def later_layers(h, w_mid, w_out, silu):
     for m in range(w_mid.shape[0]):
-        h = silu_half(jnp.dot(h, w_mid[m], preferred_element_type=jnp.float32))
+        h = silu(jnp.dot(h, w_mid[m], preferred_element_type=jnp.float32))
     y = lax.dot_general(
         w_out[...], h, (((1,), (1,)), ((), ())), preferred_element_type=jnp.float32
     )
@@ -215,7 +220,7 @@
 def empty_kernel(trans_weight, w_mid, w_out, out):
     u = trans_weight[...].astype(jnp.float32) * 0.5
     h = silu_half(jnp.broadcast_to(u, (out.shape[1], u.shape[1])))
-    y = later_layers(h, w_mid, w_out)
+    y = later_layers(h, w_mid, w_out, silu_half)
     outs = w_out.shape[0]
     for at in range(0, out.shape[0], outs):
         out[pl.ds(at, outs), :] = y
@@ -263,11 +268,11 @@
     for start in range(0, GROUP, stride):
         h = jnp.concatenate(
             [
-                silu_half(jnp.dot(x, w_first[a], preferred_element_type=jnp.float32))
+                silu_half_short(jnp.dot(x, w_first[a], preferred_element_type=jnp.float32))
                 for a in range(start, start + stride)
             ]
         )
-        y = later_layers(h, w_mid, w_out)
+        y = later_layers(h, w_mid, w_out, silu_half_short)
         for a in range(start, start + stride):
             for q in range(groups):
                 at = ((a - start) * groups + q) * span

time: 20.8 us -> 20.9 us (level)
  no operation moved by 1% of the time
where the time goes in v3:
time: 20.9 us; the launch traced here: 20.6 us
  starting transfers between devices  10.3 us (49%)
  Pallas kernels  6.63 us (32%)
  waiting for transfers between devices  3.47 us (17%)
    all_to_all x1, starting transfers between devices, compact_device(): lax.all_to_all(sends, 'slab', split_axis=0, concat_axis=0, axis_index_gro...  8.41 us
    all_to_all x1, waiting for transfers between devices, compact_device(): lax.all_to_all(sends, 'slab', split_axis=0, concat_axis=0, axis_index_gro...  1.94 us
    ppermute x3, starting transfers between devices, compact_device(): lax.ppermute(shaded, 'strip', [(s, s ^ k) for s in range(n_strip)])  1.88 us
    pallas_call x1, Pallas kernels, compact_device(): pl.pallas_call(pack_kernel, out_shape=jax.ShapeDtypeStruct((n_slab, messa...  1.7 us
    pallas_call x1, Pallas kernels, compact_device(): pl.pallas_call(shade_kernel, out_shape=jax.ShapeDtypeStruct((items * outs...  1.61 us
    ppermute x3, waiting for transfers between devices, compact_device(): lax.ppermute(shaded, 'strip', [(s, s ^ k) for s in range(n_strip)])  1.53 us
    pallas_call x1, Pallas kernels, compact_device(): pl.pallas_call(place_kernel, out_shape=[jax.ShapeDtypeStruct((GROUP, 2 *...  1.1 us
    pallas_call x1, Pallas kernels, compact_device(): pl.pallas_call(functools.partial(plan_kernel, n_slab, slots), out_shape=[...  0.93 us
  transfers between devices with their start and end apart: 4, of which 3 were waited for; matrix products, arithmetic and copies ran while one was open for 0% of the time, Pallas kernels for 12%

profile of v3, /device:TPU:0, one launch (start us, length us, event | category | flops | bytes accessed | tf_op | source)
XLA Modules:
  0.0 20.6 jit_solution(7618326864442545178)
XLA Ops:
  0.0 1.7 %pack.1 = bf16[8,72,128]{2,1,0:T(8,128)(2,1)} custom-call(s32[1,8,8]{2,1,0:T(8,128)} %far_counts.1, bf16[1,1,16,32,128]{4,3,2,1,0:T(8,128)(2,1)} %far_colors.1, bf16[1,1,16,128]{3,2,1,0:T(8,128)(2,1)} %far_transmit.1), custom_call_target="tpu_custom_call" | custom-call | tf_op jit(solution)/shard_map/pack/pallas_call | solution.py:336
  1.7 0.0 copy-start
  1.7 0.0 copy-start.2
  1.7 0.0 copy-start.3
  1.7 0.0 copy-start.5
  1.8 0.0 copy-start.6
  1.8 0.0 copy-start.4
  1.8 8.4 %all-to-all-start = ((bf16[8,72,128]{2,1,0:T(8,128)(2,1)}), bf16[8,72,128]{2,1,0:T(8,128)(2,1)S(1)}, u32[]{:S(2)}, u32[]{:S(2)}) async-start(bf16[8,72,128]{2,1,0:T(8,128)(2,1)} %pack.1), calls=%async_computation | async-start | bytes 294912 | tf_op jit(solution)/shard_map/all_to_all | solution.py:351
  10.2 0.0 copy-done
  10.2 0.0 copy-done.2
  10.2 0.0 copy-done.3
  10.2 0.0 copy-done.5
  10.2 0.0 copy-start.1
  10.2 0.9 %plan.1 = (s32[3,16,128]{2,1,0:T(8,128)S(1)}, bf16[8,128]{1,0:T(8,128)(2,1)S(1)}) custom-call(s32[1,8,8]{2,1,0:T(8,128)S(1)} %copy-done, s32[1,8,16]{2,1,0:T(8,128)S(1)} %copy-done.2, s32[1,1024]{1,0:T(1,128)S(1)} %copy-done.3, s32[8]{0:T(128)S(1)} %copy-done.5), custom_call_target="tpu_custom_call" | custom-call | flops 100000 | bytes 1000000 | tf_op jit(solution)/shard_map/plan/pallas_call | solution.py:358
  11.2 0.0 copy-done.6
  11.2 0.0 copy-done.4
  11.2 0.0 copy-done.1
  11.2 1.1 %place.1 = (bf16[4,256,256]{2,1,0:T(8,128)(2,1)S(1)}, bf16[4,256]{1,0:T(4,128)(2,1)S(1)}, bf16[2,256,256]{2,1,0:T(8,128)(2,1)S(1)}) custom-call(bf16[32,256]{1,0:T(8,128)(2,1)S(1)} %bitcast.1, bf16[1,256]{1,0:T(2,128)(2,1)S(1)} %broadcast_in_dim.3.trans_weight, bf16[4,256]{1,0:T(4,128)(2,1)S(1)} %copy-done.4, bf16[2,256,256]{2,1,0:T(8,128)(2,1)} %far_mid.1), custom_call_target="tpu_custom_call" | custom-call | flops 100000 | bytes 1000000 | tf_op jit(solution)/shard_map/place/pallas_call | solution.py:370
  12.3 1.9 %all-to-all-done.got = bf16[8,72,128]{2,1,0:T(8,128)(2,1)S(1)} async-done(((bf16[8,72,128]{2,1,0:T(8,128)(2,1)}), bf16[8,72,128]{2,1,0:T(8,128)(2,1)S(1)}, u32[]{:S(2)}, u32[]{:S(2)}) %all-to-all-start) | async-done | bytes 147488 | tf_op jit(solution)/shard_map/all_to_all | solution.py:351
  14.3 1.6 %shade.1.refs_3_ = bf16[72,128]{1,0:T(8,128)(2,1)S(1)} custom-call(s32[3,16,128]{2,1,0:T(8,128)S(1)} %get-tuple-element.10.rows, bf16[8,128]{1,0:T(8,128)(2,1)S(1)} %get-tuple-element.11.codes, bf16[8,72,128]{2,1,0:T(8,128)(2,1)S(1)} %all-to-all-done.got, bf16[4,256,256]{2,1,0:T(8,128)(2,1)S(1)} %get-tuple-element.12.w_first, ...), custom_call_target="tpu_custom_call" | custom-call | tf_op jit(solution)/shard_map/shade/pallas_call | solution.py:396
  15.9 0.0 collective-permute-start.2
  15.9 1.6 %collective-permute-start.1 = (bf16[72,128]{1,0:T(8,128)(2,1)S(1)}, bf16[72,128]{1,0:T(8,128)(2,1)S(1)}, u32[]{:S(2)}, u32[]{:S(2)}) collective-permute-start(bf16[72,128]{1,0:T(8,128)(2,1)S(1)} %shade.1.refs_3_), channel_id=1, source_target_pairs={{0,2},{1,3},{2,0},{3,1},{4,6},{5,7},{6,4},{7,5},{8,10},{9,11},{10,... | collective-permute-start | bytes 55304 | tf_op jit(solution)/shard_map/ppermute | solution.py:410
  17.4 0.3 %collective-permute-start = (bf16[72,128]{1,0:T(8,128)(2,1)S(1)}, bf16[72,128]{1,0:T(8,128)(2,1)S(1)}, u32[]{:S(2)}, u32[]{:S(2)}) collective-permute-start(bf16[72,128]{1,0:T(8,128)(2,1)S(1)} %shade.1.refs_3_), channel_id=1, source_target_pairs={{0,1},{1,0},{2,3},{3,2},{4,5},{5,4},{6,7},{7,6},{8,9},{9,8},{10,11... | collective-permute-start | bytes 55304 | tf_op jit(solution)/shard_map/ppermute | solution.py:410
  17.8 0.4 %empty.1.refs_4_ = f32[8,128]{1,0:T(8,128)S(1)} custom-call(bf16[1,256]{1,0:T(2,128)(2,1)S(1)} %broadcast_in_dim.3.trans_weight, bf16[2,256,256]{2,1,0:T(8,128)(2,1)S(1)} %get-tuple-element.13.w_mid, bf16[4,256]{1,0:T(4,128)(2,1)S(1)} %get-tuple-element.14.w_out), custom_call_target="tpu_custom_call" | custom-call | flops 100000 | bytes 1000000 | tf_op jit(solution)/shard_map/empty/pallas_call | solution.py:387
  18.2 1.0 %collective-permute-done.2.refs_2_ = bf16[72,128]{1,0:T(8,128)(2,1)S(1)} collective-permute-done((bf16[72,128]{1,0:T(8,128)(2,1)S(1)}, bf16[72,128]{1,0:T(8,128)(2,1)S(1)}, u32[]{:S(2)}, u32[]{:S(2)}) %collective-permute-start.2) | collective-permute-done | bytes 18464 | tf_op jit(solution)/shard_map/ppermute | solution.py:410
  19.2 0.5 %collective-permute-done.1.refs_1_ = bf16[72,128]{1,0:T(8,128)(2,1)S(1)} collective-permute-done((bf16[72,128]{1,0:T(8,128)(2,1)S(1)}, bf16[72,128]{1,0:T(8,128)(2,1)S(1)}, u32[]{:S(2)}, u32[]{:S(2)}) %collective-permute-start.1) | collective-permute-done | bytes 18464 | tf_op jit(solution)/shard_map/ppermute | solution.py:410
  19.7 0.0 collective-permute-done.refs_0_
  19.7 0.9 %join.1 = bf16[1,4,32,4,128]{4,3,2,1,0:T(4,128)(2,1)} custom-call(bf16[72,128]{1,0:T(8,128)(2,1)S(1)} %collective-permute-done.refs_0_, bf16[72,128]{1,0:T(8,128)(2,1)S(1)} %collective-permute-done.1.refs_1_, bf16[72,128]{1,0:T(8,128)(2,1)S(1)} %collective-permute-done.2.refs_2_, bf16[72,128]{1,0:T(8,128)(2,1)S(1)} %shade.1.refs_3_, f32[8,128]{1,0:T(8,128)S(1)} %empty.1.refs_4_), custom_call_target="tpu_custom_call" | custom-call | tf_op jit(solution)/shard_map/join/pallas_call | solution.py:413
  (1 shorter events, 0.0 us)
Async XLA Ops:
  1.7 8.5 %copy-start = (s32[1,8,8]{2,1,0:T(8,128)S(1)}, s32[1,8,8]{2,1,0:T(8,128)}, u32[]{:S(2)}) copy-start(s32[1,8,8]{2,1,0:T(8,128)} %far_counts.1) | copy-start | bytes 772
  1.7 8.5 %copy-start.2 = (s32[1,8,16]{2,1,0:T(8,128)S(1)}, s32[1,8,16]{2,1,0:T(8,128)}, u32[]{:S(2)}) copy-start(s32[1,8,16]{2,1,0:T(8,128)} %refs_1_.1) | copy-start | bytes 1540
  1.7 8.5 %copy-start.3 = (s32[1,1024]{1,0:T(1,128)S(1)}, s32[1,1024]{1,0:T(1,128)}, u32[]{:S(2)}) copy-start(s32[1,1024]{1,0:T(1,128)} %refs_2_.1) | copy-start | bytes 12292
  1.7 8.5 %copy-start.5 = (s32[8]{0:T(128)S(1)}, s32[8]{0:T(128)}, u32[]{:S(2)}) copy-start(s32[8]{0:T(128)} %refs_3_.1) | copy-start | bytes 100
  1.8 9.4 %copy-start.6 = (bf16[256]{0:T(256)(128)(2,1)S(1)}, bf16[256]{0:T(256)(128)(2,1)}, u32[]{:S(2)}) copy-start(bf16[256]{0:T(256)(128)(2,1)} %param.17) | copy-start | bytes 1540
  1.8 9.4 %copy-start.4 = (bf16[4,256]{1,0:T(4,128)(2,1)S(1)}, bf16[4,256]{1,0:T(4,128)(2,1)}, u32[]{:S(2)}) copy-start(bf16[4,256]{1,0:T(4,128)(2,1)} %far_out.1) | copy-start | bytes 6148
  1.8 12.5 %all-to-all-start = ((bf16[8,72,128]{2,1,0:T(8,128)(2,1)}), bf16[8,72,128]{2,1,0:T(8,128)(2,1)S(1)}, u32[]{:S(2)}, u32[]{:S(2)}) async-start(bf16[8,72,128]{2,1,0:T(8,128)(2,1)} %pack.1), calls=%async_computation | async-start | bytes 294912 | tf_op jit(solution)/shard_map/all_to_all | solution.py:351
  10.2 1.0 %copy-start.1 = (bf16[256,32]{0,1:T(8,128)(2,1)S(1)}, bf16[256,32]{0,1:T(8,128)(2,1)}, u32[]{:S(2)}) copy-start(bf16[256,32]{0,1:T(8,128)(2,1)} %param.16) | copy-start | bytes 49156
  15.9 3.4 %collective-permute-start.2 = (bf16[72,128]{1,0:T(8,128)(2,1)S(1)}, bf16[72,128]{1,0:T(8,128)(2,1)S(1)}, u32[]{:S(2)}, u32[]{:S(2)}) collective-permute-start(bf16[72,128]{1,0:T(8,128)(2,1)S(1)} %shade.1.refs_3_), channel_id=1, source_target_pairs={{0,3},{1,2},{2,1},{3,0},{4,7},{5,6},{6,5},{7,4},{8,11},{9,10},{10,... | collective-permute-start | bytes 55304 | tf_op jit(solution)/shard_map/ppermute | solution.py:410
  15.9 3.8 %collective-permute-start.1 = (bf16[72,128]{1,0:T(8,128)(2,1)S(1)}, bf16[72,128]{1,0:T(8,128)(2,1)S(1)}, u32[]{:S(2)}, u32[]{:S(2)}) collective-permute-start(bf16[72,128]{1,0:T(8,128)(2,1)S(1)} %shade.1.refs_3_), channel_id=1, source_target_pairs={{0,2},{1,3},{2,0},{3,1},{4,6},{5,7},{6,4},{7,5},{8,10},{9,11},{10,... | collective-permute-start | bytes 55304 | tf_op jit(solution)/shard_map/ppermute | solution.py:410
  17.4 2.3 %collective-permute-start = (bf16[72,128]{1,0:T(8,128)(2,1)S(1)}, bf16[72,128]{1,0:T(8,128)(2,1)S(1)}, u32[]{:S(2)}, u32[]{:S(2)}) collective-permute-start(bf16[72,128]{1,0:T(8,128)(2,1)S(1)} %shade.1.refs_3_), channel_id=1, source_target_pairs={{0,1},{1,0},{2,3},{3,2},{4,5},{5,4},{6,7},{7,6},{8,9},{9,8},{10,11... | collective-permute-start | bytes 55304 | tf_op jit(solution)/shard_map/ppermute | solution.py:410

commit v4 on v2

--- a/solution.py
+++ b/solution.py
@@ -92,7 +92,9 @@
 def exchange_order(n_slab):
     half = n_slab // 2
     flip = 1 if half % 2 == 0 else 0
-    return [s for i in range(half) for s in (half + (i ^ flip), i)]
+    ring = [s for i in range(half) for s in (half + (i ^ flip), i)]
+    at = ring.index(n_slab - 1)
+    return ring[at:] + ring[:at]
 
 
 def pack_kernel(far_counts, far_colors, far_transmit, sends, counts, colors, transmit, sems):

time: 20.8 us -> 22.6 us (1.087)
  starting transfers between devices: 10.3 us -> 11.3 us
  waiting for transfers between devices: 3.47 us -> 4.17 us
    all_to_all x1, starting transfers between devices: 8.41 us -> 9.45 us  [compact_device(): lax.all_to_all(sends, 'slab', split_axis=0, concat_axis=0, axis_index_gro...]
    ppermute x3, waiting for transfers between devices: 1.53 us -> 2.23 us  [compact_device(): lax.ppermute(shaded, 'strip', [(s, s ^ k) for s in range(n_strip)])]
  transfers between devices with their start and end apart: 4 -> 4, of which waited for: 3 -> 3; matrix products, arithmetic and copies ran while one was open for 0% -> 0% of each run, Pallas kernels for 12% -> 11%
where the time goes in v4:
time: 22.6 us; the launch traced here: 22.3 us
  starting transfers between devices  11.3 us (50%)
  Pallas kernels  6.58 us (29%)
  waiting for transfers between devices  4.17 us (18%)
    all_to_all x1, starting transfers between devices, compact_device(): lax.all_to_all(sends, 'slab', split_axis=0, concat_axis=0, axis_index_gro...  9.45 us
    ppermute x3, waiting for transfers between devices, compact_device(): lax.ppermute(shaded, 'strip', [(s, s ^ k) for s in range(n_strip)])  2.23 us
    all_to_all x1, waiting for transfers between devices, compact_device(): lax.all_to_all(sends, 'slab', split_axis=0, concat_axis=0, axis_index_gro...  1.94 us
    ppermute x3, starting transfers between devices, compact_device(): lax.ppermute(shaded, 'strip', [(s, s ^ k) for s in range(n_strip)])  1.88 us
    pallas_call x1, Pallas kernels, compact_device(): pl.pallas_call(pack_kernel, out_shape=jax.ShapeDtypeStruct((n_slab, messa...  1.7 us
    pallas_call x1, Pallas kernels, compact_device(): pl.pallas_call(shade_kernel, out_shape=jax.ShapeDtypeStruct((items * outs...  1.55 us
    pallas_call x1, Pallas kernels, compact_device(): pl.pallas_call(place_kernel, out_shape=[jax.ShapeDtypeStruct((GROUP, 2 *...  1.1 us
    pallas_call x1, Pallas kernels, compact_device(): pl.pallas_call(functools.partial(plan_kernel, n_slab, slots), out_shape=[...  0.93 us
  transfers between devices with their start and end apart: 4, of which 3 were waited for; matrix products, arithmetic and copies ran while one was open for 0% of the time, Pallas kernels for 11%

profile of v4, /device:TPU:0, one launch (start us, length us, event | category | flops | bytes accessed | tf_op | source)
XLA Modules:
  0.0 22.3 jit_solution(8142095529153747969)
XLA Ops:
  0.0 1.7 %pack.1 = bf16[8,72,128]{2,1,0:T(8,128)(2,1)} custom-call(s32[1,8,8]{2,1,0:T(8,128)} %far_counts.1, bf16[1,1,16,32,128]{4,3,2,1,0:T(8,128)(2,1)} %far_colors.1, bf16[1,1,16,128]{3,2,1,0:T(8,128)(2,1)} %far_transmit.1), custom_call_target="tpu_custom_call" | custom-call | tf_op jit(solution)/shard_map/pack/pallas_call | solution.py:333
  1.7 0.0 copy-start
  1.7 0.0 copy-start.2
  1.7 0.0 copy-start.3
  1.7 0.0 copy-start.5
  1.8 0.0 copy-start.6
  1.8 0.0 copy-start.4
  1.8 9.5 %all-to-all-start = ((bf16[8,72,128]{2,1,0:T(8,128)(2,1)}), bf16[8,72,128]{2,1,0:T(8,128)(2,1)S(1)}, u32[]{:S(2)}, u32[]{:S(2)}) async-start(bf16[8,72,128]{2,1,0:T(8,128)(2,1)} %pack.1), calls=%async_computation | async-start | bytes 294912 | tf_op jit(solution)/shard_map/all_to_all | solution.py:348
  11.2 0.0 copy-done
  11.2 0.0 copy-done.2
  11.2 0.0 copy-done.3
  11.2 0.0 copy-done.5
  11.3 0.0 copy-start.1
  11.3 0.9 %plan.1 = (s32[3,16,128]{2,1,0:T(8,128)S(1)}, bf16[8,128]{1,0:T(8,128)(2,1)S(1)}) custom-call(s32[1,8,8]{2,1,0:T(8,128)S(1)} %copy-done, s32[1,8,16]{2,1,0:T(8,128)S(1)} %copy-done.2, s32[1,1024]{1,0:T(1,128)S(1)} %copy-done.3, s32[8]{0:T(128)S(1)} %copy-done.5), custom_call_target="tpu_custom_call" | custom-call | flops 100000 | bytes 1000000 | tf_op jit(solution)/shard_map/plan/pallas_call | solution.py:355
  12.2 0.0 copy-done.6
  12.2 0.0 copy-done.4
  12.2 0.0 copy-done.1
  12.3 1.1 %place.1 = (bf16[4,256,256]{2,1,0:T(8,128)(2,1)S(1)}, bf16[4,256]{1,0:T(4,128)(2,1)S(1)}, bf16[2,256,256]{2,1,0:T(8,128)(2,1)S(1)}) custom-call(bf16[32,256]{1,0:T(8,128)(2,1)S(1)} %bitcast.1, bf16[1,256]{1,0:T(2,128)(2,1)S(1)} %broadcast_in_dim.3.trans_weight, bf16[4,256]{1,0:T(4,128)(2,1)S(1)} %copy-done.4, bf16[2,256,256]{2,1,0:T(8,128)(2,1)} %far_mid.1), custom_call_target="tpu_custom_call" | custom-call | flops 100000 | bytes 1000000 | tf_op jit(solution)/shard_map/place/pallas_call | solution.py:367
  13.4 1.9 %all-to-all-done.got = bf16[8,72,128]{2,1,0:T(8,128)(2,1)S(1)} async-done(((bf16[8,72,128]{2,1,0:T(8,128)(2,1)}), bf16[8,72,128]{2,1,0:T(8,128)(2,1)S(1)}, u32[]{:S(2)}, u32[]{:S(2)}) %all-to-all-start) | async-done | bytes 147488 | tf_op jit(solution)/shard_map/all_to_all | solution.py:348
  15.3 1.6 %shade.1.refs_3_ = bf16[72,128]{1,0:T(8,128)(2,1)S(1)} custom-call(s32[3,16,128]{2,1,0:T(8,128)S(1)} %get-tuple-element.10.rows, bf16[8,128]{1,0:T(8,128)(2,1)S(1)} %get-tuple-element.11.codes, bf16[8,72,128]{2,1,0:T(8,128)(2,1)S(1)} %all-to-all-done.got, bf16[4,256,256]{2,1,0:T(8,128)(2,1)S(1)} %get-tuple-element.12.w_first, ...), custom_call_target="tpu_custom_call" | custom-call | tf_op jit(solution)/shard_map/shade/pallas_call | solution.py:393
  16.9 0.6 %collective-permute-start.2 = (bf16[72,128]{1,0:T(8,128)(2,1)S(1)}, bf16[72,128]{1,0:T(8,128)(2,1)S(1)}, u32[]{:S(2)}, u32[]{:S(2)}) collective-permute-start(bf16[72,128]{1,0:T(8,128)(2,1)S(1)} %shade.1.refs_3_), channel_id=1, source_target_pairs={{0,3},{1,2},{2,1},{3,0},{4,7},{5,6},{6,5},{7,4},{8,11},{9,10},{10,... | collective-permute-start | bytes 55304 | tf_op jit(solution)/shard_map/ppermute | solution.py:407
  17.5 0.9 %collective-permute-start.1 = (bf16[72,128]{1,0:T(8,128)(2,1)S(1)}, bf16[72,128]{1,0:T(8,128)(2,1)S(1)}, u32[]{:S(2)}, u32[]{:S(2)}) collective-permute-start(bf16[72,128]{1,0:T(8,128)(2,1)S(1)} %shade.1.refs_3_), channel_id=1, source_target_pairs={{0,2},{1,3},{2,0},{3,1},{4,6},{5,7},{6,4},{7,5},{8,10},{9,11},{10,... | collective-permute-start | bytes 55304 | tf_op jit(solution)/shard_map/ppermute | solution.py:407
  18.4 0.3 %collective-permute-start = (bf16[72,128]{1,0:T(8,128)(2,1)S(1)}, bf16[72,128]{1,0:T(8,128)(2,1)S(1)}, u32[]{:S(2)}, u32[]{:S(2)}) collective-permute-start(bf16[72,128]{1,0:T(8,128)(2,1)S(1)} %shade.1.refs_3_), channel_id=1, source_target_pairs={{0,1},{1,0},{2,3},{3,2},{4,5},{5,4},{6,7},{7,6},{8,9},{9,8},{10,11... | collective-permute-start | bytes 55304 | tf_op jit(solution)/shard_map/ppermute | solution.py:407
  18.7 0.4 %empty.1.refs_4_ = f32[8,128]{1,0:T(8,128)S(1)} custom-call(bf16[1,256]{1,0:T(2,128)(2,1)S(1)} %broadcast_in_dim.3.trans_weight, bf16[2,256,256]{2,1,0:T(8,128)(2,1)S(1)} %get-tuple-element.13.w_mid, bf16[4,256]{1,0:T(4,128)(2,1)S(1)} %get-tuple-element.14.w_out), custom_call_target="tpu_custom_call" | custom-call | flops 100000 | bytes 1000000 | tf_op jit(solution)/shard_map/empty/pallas_call | solution.py:384
  19.2 1.0 %collective-permute-done.2.refs_2_ = bf16[72,128]{1,0:T(8,128)(2,1)S(1)} collective-permute-done((bf16[72,128]{1,0:T(8,128)(2,1)S(1)}, bf16[72,128]{1,0:T(8,128)(2,1)S(1)}, u32[]{:S(2)}, u32[]{:S(2)}) %collective-permute-start.2) | collective-permute-done | bytes 18464 | tf_op jit(solution)/shard_map/ppermute | solution.py:407
  20.2 1.2 %collective-permute-done.1.refs_1_ = bf16[72,128]{1,0:T(8,128)(2,1)S(1)} collective-permute-done((bf16[72,128]{1,0:T(8,128)(2,1)S(1)}, bf16[72,128]{1,0:T(8,128)(2,1)S(1)}, u32[]{:S(2)}, u32[]{:S(2)}) %collective-permute-start.1) | collective-permute-done | bytes 18464 | tf_op jit(solution)/shard_map/ppermute | solution.py:407
  21.4 0.0 collective-permute-done.refs_0_
  21.4 0.9 %join.1 = bf16[1,4,32,4,128]{4,3,2,1,0:T(4,128)(2,1)} custom-call(bf16[72,128]{1,0:T(8,128)(2,1)S(1)} %collective-permute-done.refs_0_, bf16[72,128]{1,0:T(8,128)(2,1)S(1)} %collective-permute-done.1.refs_1_, bf16[72,128]{1,0:T(8,128)(2,1)S(1)} %collective-permute-done.2.refs_2_, bf16[72,128]{1,0:T(8,128)(2,1)S(1)} %shade.1.refs_3_, f32[8,128]{1,0:T(8,128)S(1)} %empty.1.refs_4_), custom_call_target="tpu_custom_call" | custom-call | tf_op jit(solution)/shard_map/join/pallas_call | solution.py:410
  (1 shorter events, 0.0 us)
Async XLA Ops:
  1.7 9.5 %copy-start = (s32[1,8,8]{2,1,0:T(8,128)S(1)}, s32[1,8,8]{2,1,0:T(8,128)}, u32[]{:S(2)}) copy-start(s32[1,8,8]{2,1,0:T(8,128)} %far_counts.1) | copy-start | bytes 772
  1.7 9.5 %copy-start.2 = (s32[1,8,16]{2,1,0:T(8,128)S(1)}, s32[1,8,16]{2,1,0:T(8,128)}, u32[]{:S(2)}) copy-start(s32[1,8,16]{2,1,0:T(8,128)} %refs_1_.1) | copy-start | bytes 1540
  1.7 9.5 %copy-start.3 = (s32[1,1024]{1,0:T(1,128)S(1)}, s32[1,1024]{1,0:T(1,128)}, u32[]{:S(2)}) copy-start(s32[1,1024]{1,0:T(1,128)} %refs_2_.1) | copy-start | bytes 12292
  1.7 9.5 %copy-start.5 = (s32[8]{0:T(128)S(1)}, s32[8]{0:T(128)}, u32[]{:S(2)}) copy-start(s32[8]{0:T(128)} %refs_3_.1) | copy-start | bytes 100
  1.8 10.5 %copy-start.6 = (bf16[256]{0:T(256)(128)(2,1)S(1)}, bf16[256]{0:T(256)(128)(2,1)}, u32[]{:S(2)}) copy-start(bf16[256]{0:T(256)(128)(2,1)} %param.17) | copy-start | bytes 1540
  1.8 10.5 %copy-start.4 = (bf16[4,256]{1,0:T(4,128)(2,1)S(1)}, bf16[4,256]{1,0:T(4,128)(2,1)}, u32[]{:S(2)}) copy-start(bf16[4,256]{1,0:T(4,128)(2,1)} %far_out.1) | copy-start | bytes 6148
  1.8 13.5 %all-to-all-start = ((bf16[8,72,128]{2,1,0:T(8,128)(2,1)}), bf16[8,72,128]{2,1,0:T(8,128)(2,1)S(1)}, u32[]{:S(2)}, u32[]{:S(2)}) async-start(bf16[8,72,128]{2,1,0:T(8,128)(2,1)} %pack.1), calls=%async_computation | async-start | bytes 294912 | tf_op jit(solution)/shard_map/all_to_all | solution.py:348
  11.3 1.0 %copy-start.1 = (bf16[256,32]{0,1:T(8,128)(2,1)S(1)}, bf16[256,32]{0,1:T(8,128)(2,1)}, u32[]{:S(2)}) copy-start(bf16[256,32]{0,1:T(8,128)(2,1)} %param.16) | copy-start | bytes 49156
  16.9 3.4 %collective-permute-start.2 = (bf16[72,128]{1,0:T(8,128)(2,1)S(1)}, bf16[72,128]{1,0:T(8,128)(2,1)S(1)}, u32[]{:S(2)}, u32[]{:S(2)}) collective-permute-start(bf16[72,128]{1,0:T(8,128)(2,1)S(1)} %shade.1.refs_3_), channel_id=1, source_target_pairs={{0,3},{1,2},{2,1},{3,0},{4,7},{5,6},{6,5},{7,4},{8,11},{9,10},{10,... | collective-permute-start | bytes 55304 | tf_op jit(solution)/shard_map/ppermute | solution.py:407
  17.5 3.9 %collective-permute-start.1 = (bf16[72,128]{1,0:T(8,128)(2,1)S(1)}, bf16[72,128]{1,0:T(8,128)(2,1)S(1)}, u32[]{:S(2)}, u32[]{:S(2)}) collective-permute-start(bf16[72,128]{1,0:T(8,128)(2,1)S(1)} %shade.1.refs_3_), channel_id=1, source_target_pairs={{0,2},{1,3},{2,0},{3,1},{4,6},{5,7},{6,4},{7,5},{8,10},{9,11},{10,... | collective-permute-start | bytes 55304 | tf_op jit(solution)/shard_map/ppermute | solution.py:407
  18.4 3.0 %collective-permute-start = (bf16[72,128]{1,0:T(8,128)(2,1)S(1)}, bf16[72,128]{1,0:T(8,128)(2,1)S(1)}, u32[]{:S(2)}, u32[]{:S(2)}) collective-permute-start(bf16[72,128]{1,0:T(8,128)(2,1)S(1)} %shade.1.refs_3_), channel_id=1, source_target_pairs={{0,1},{1,0},{2,3},{3,2},{4,5},{5,4},{6,7},{7,6},{8,9},{9,8},{10,11... | collective-permute-start | bytes 55304 | tf_op jit(solution)/shard_map/ppermute | solution.py:407

commit v5 on v2

--- a/solution.py
+++ b/solution.py
@@ -86,7 +86,12 @@
 VMEM = pltpu.VMEM
 ROWS = 8
 GROUP = 4
-PARTS = 4
+
+
+def exchange_place(n_slab, c):
+    half = n_slab // 2
+    flip = 1 if half % 2 == 0 else 0
+    return jnp.where(c < half, 2 * c + 1, 2 * ((c - half) ^ flip))
 
 
 def exchange_order(n_slab):
@@ -95,54 +100,39 @@
     return [s for i in range(half) for s in (half + (i ^ flip), i)]
 
 
-def pack_kernel(far_counts, far_colors, far_transmit, sends, counts, colors, transmit, sems):
+def pack_kernel(far_counts, far_colors, far_transmit, sends, counts, colors, transmit, tall, sems):
     n_slab = sends.shape[0]
-    place = [exchange_order(n_slab).index(c) for c in range(n_slab)]
     slots, feats, span = colors.shape
     me = lax.axis_index("slab")
-    part = slots // PARTS
     copies = [
-        pltpu.make_async_copy(far_counts, counts, sems.at[0]),
-        pltpu.make_async_copy(far_transmit, transmit, sems.at[1]),
-    ] + [
-        pltpu.make_async_copy(
-            far_colors.at[0, 0, pl.ds(p * part, part)], colors.at[pl.ds(p * part, part)], sems.at[2 + p]
+        pltpu.make_async_copy(far, near, sems.at[i])
+        for i, (far, near) in enumerate(
+            (
+                (far_counts, counts),
+                (far_transmit.at[0, 0], transmit),
+                (far_colors.at[0, 0], colors),
+            )
         )
-        for p in range(PARTS)
     ]
     for copy in copies:
         copy.start()
+    row = lax.broadcasted_iota(jnp.int32, (ROWS, span), 0)
+    copies[1].wait()
+    tall[...] = transmit[...].astype(jnp.float32)
     copies[0].wait()
-    mine = counts[0, pl.ds(me, 1), :].astype(jnp.float32)
-    before = lax.broadcasted_iota(jnp.int32, mine.shape, 1)
-    row = lax.broadcasted_iota(jnp.int32, (ROWS, slots), 0).astype(jnp.float32)
-    lane = lax.broadcasted_iota(jnp.int32, (ROWS, slots), 1).astype(jnp.float32)
-    offs, picks = [], []
-    for c in range(n_slab):
-        off = jnp.sum(jnp.where(before < c, mine, 0.0), axis=1, keepdims=True)
-        offs.append(off)
-        hit = (row < MOST) & (lane - row == off)
-        picks.append(jnp.where(hit, 1.0, 0.0))
-    pick = jnp.concatenate(picks).astype(jnp.bfloat16)
-    copies[1].wait()
-    tails = jnp.dot(pick, transmit[0, 0], preferred_element_type=jnp.float32)
-    for c in range(n_slab):
-        tail = tails[c * ROWS : (c + 1) * ROWS]
-        sends[place[c], pl.ds(MOST * feats, ROWS), :] = tail.astype(jnp.bfloat16)
-    waited = 0
-    for c in range(n_slab):
-        off = jnp.broadcast_to(offs[c], (feats, span)).astype(jnp.bfloat16)
+    copies[2].wait()
+
+    def fill(c, off):
+        tail = jnp.ones((ROWS, span), jnp.float32)
+        at = exchange_place(n_slab, c)
         for r in range(MOST):
-            last = min(MOST * c + r, slots - 1)
-            while waited * part <= last:
-                copies[2 + waited].wait()
-                waited += 1
-            block = colors[last]
-            for slot in range(r, last):
-                block = jnp.where(off == slot - r, colors[slot], block)
-            sends[place[c], pl.ds(r * feats, feats), :] = block
-    for copy in copies[2 + waited :]:
-        copy.wait()
+            slot = jnp.minimum(off + r, slots - 1)
+            sends[at, pl.ds(r * feats, feats), :] = colors[slot]
+            tail = jnp.where(row == r, tall[pl.ds(slot, 1), :], tail)
+        sends[at, pl.ds(MOST * feats, ROWS), :] = tail.astype(jnp.bfloat16)
+        return off + counts[0, me, c]
+
+    lax.fori_loop(0, n_slab, fill, jnp.int32(0))
 
 
 def plan_kernel(n_slab, slots, *refs):
@@ -334,10 +324,11 @@
         in_specs=[hbm] * 3,
         out_specs=vmem,
         scratch_shapes=[
-            pltpu.VMEM(pair_counts.shape, jnp.int32),
+            pltpu.SMEM(pair_counts.shape, jnp.int32),
             pltpu.VMEM(colors.shape[2:], colors.dtype),
-            pltpu.VMEM(transmit.shape, transmit.dtype),
-            pltpu.SemaphoreType.DMA((2 + PARTS,)),
+            pltpu.VMEM(transmit.shape[2:], transmit.dtype),
+            pltpu.VMEM(transmit.shape[2:], jnp.float32),
+            pltpu.SemaphoreType.DMA((3,)),
         ],
         compiler_params=small,
         name="pack",

time: 20.8 us -> 20.8 us (level)
  no operation moved by 1% of the time
where the time goes in v5:
time: 20.8 us; the launch traced here: 20.5 us
  starting transfers between devices  10.3 us (50%)
  Pallas kernels  6.56 us (32%)
  waiting for transfers between devices  3.47 us (17%)
    all_to_all x1, starting transfers between devices, compact_device(): lax.all_to_all(sends, 'slab', split_axis=0, concat_axis=0, axis_index_gro...  8.41 us
    all_to_all x1, waiting for transfers between devices, compact_device(): lax.all_to_all(sends, 'slab', split_axis=0, concat_axis=0, axis_index_gro...  1.94 us
    ppermute x3, starting transfers between devices, compact_device(): lax.ppermute(shaded, 'strip', [(s, s ^ k) for s in range(n_strip)])  1.88 us
    pallas_call x1, Pallas kernels, compact_device(): pl.pallas_call(pack_kernel, out_shape=jax.ShapeDtypeStruct((n_slab, messa...  1.68 us
    pallas_call x1, Pallas kernels, compact_device(): pl.pallas_call(shade_kernel, out_shape=jax.ShapeDtypeStruct((items * outs...  1.55 us
    ppermute x3, waiting for transfers between devices, compact_device(): lax.ppermute(shaded, 'strip', [(s, s ^ k) for s in range(n_strip)])  1.53 us
    pallas_call x1, Pallas kernels, compact_device(): pl.pallas_call(place_kernel, out_shape=[jax.ShapeDtypeStruct((GROUP, 2 *...  1.1 us
    pallas_call x1, Pallas kernels, compact_device(): pl.pallas_call(functools.partial(plan_kernel, n_slab, slots), out_shape=[...  0.93 us
  transfers between devices with their start and end apart: 4, of which 3 were waited for; matrix products, arithmetic and copies ran while one was open for 0% of the time, Pallas kernels for 12%

profile of v5, /device:TPU:0, one launch (start us, length us, event | category | flops | bytes accessed | tf_op | source)
XLA Modules:
  0.0 20.5 jit_solution(6349819151101423747)
XLA Ops:
  0.0 1.7 %pack.1 = bf16[8,72,128]{2,1,0:T(8,128)(2,1)} custom-call(s32[1,8,8]{2,1,0:T(8,128)} %far_counts.1, bf16[1,1,16,32,128]{4,3,2,1,0:T(8,128)(2,1)} %far_colors.1, bf16[1,1,16,128]{3,2,1,0:T(8,128)(2,1)} %far_transmit.1), custom_call_target="tpu_custom_call" | custom-call | tf_op jit(solution)/shard_map/pack/pallas_call | solution.py:321
  1.7 0.0 copy-start
  1.7 0.0 copy-start.2
  1.7 0.0 copy-start.3
  1.7 0.0 copy-start.5
  1.7 0.0 copy-start.6
  1.7 0.0 copy-start.4
  1.8 8.4 %all-to-all-start = ((bf16[8,72,128]{2,1,0:T(8,128)(2,1)}), bf16[8,72,128]{2,1,0:T(8,128)(2,1)S(1)}, u32[]{:S(2)}, u32[]{:S(2)}) async-start(bf16[8,72,128]{2,1,0:T(8,128)(2,1)} %pack.1), calls=%async_computation | async-start | bytes 294912 | tf_op jit(solution)/shard_map/all_to_all | solution.py:337
  10.2 0.0 copy-done
  10.2 0.0 copy-done.2
  10.2 0.0 copy-done.3
  10.2 0.0 copy-done.5
  10.2 0.0 copy-start.1
  10.2 0.9 %plan.1 = (s32[3,16,128]{2,1,0:T(8,128)S(1)}, bf16[8,128]{1,0:T(8,128)(2,1)S(1)}) custom-call(s32[1,8,8]{2,1,0:T(8,128)S(1)} %copy-done, s32[1,8,16]{2,1,0:T(8,128)S(1)} %copy-done.2, s32[1,1024]{1,0:T(1,128)S(1)} %copy-done.3, s32[8]{0:T(128)S(1)} %copy-done.5), custom_call_target="tpu_custom_call" | custom-call | flops 100000 | bytes 1000000 | tf_op jit(solution)/shard_map/plan/pallas_call | solution.py:344
  11.2 0.0 copy-done.6
  11.2 0.0 copy-done.4
  11.2 0.0 copy-done.1
  11.2 1.1 %place.1 = (bf16[4,256,256]{2,1,0:T(8,128)(2,1)S(1)}, bf16[4,256]{1,0:T(4,128)(2,1)S(1)}, bf16[2,256,256]{2,1,0:T(8,128)(2,1)S(1)}) custom-call(bf16[32,256]{1,0:T(8,128)(2,1)S(1)} %bitcast.1, bf16[1,256]{1,0:T(2,128)(2,1)S(1)} %broadcast_in_dim.3.trans_weight, bf16[4,256]{1,0:T(4,128)(2,1)S(1)} %copy-done.4, bf16[2,256,256]{2,1,0:T(8,128)(2,1)} %far_mid.1), custom_call_target="tpu_custom_call" | custom-call | flops 100000 | bytes 1000000 | tf_op jit(solution)/shard_map/place/pallas_call | solution.py:356
  12.3 1.9 %all-to-all-done.got = bf16[8,72,128]{2,1,0:T(8,128)(2,1)S(1)} async-done(((bf16[8,72,128]{2,1,0:T(8,128)(2,1)}), bf16[8,72,128]{2,1,0:T(8,128)(2,1)S(1)}, u32[]{:S(2)}, u32[]{:S(2)}) %all-to-all-start) | async-done | bytes 147488 | tf_op jit(solution)/shard_map/all_to_all | solution.py:337
  14.2 1.6 %shade.1.refs_3_ = bf16[72,128]{1,0:T(8,128)(2,1)S(1)} custom-call(s32[3,16,128]{2,1,0:T(8,128)S(1)} %get-tuple-element.10.rows, bf16[8,128]{1,0:T(8,128)(2,1)S(1)} %get-tuple-element.11.codes, bf16[8,72,128]{2,1,0:T(8,128)(2,1)S(1)} %all-to-all-done.got, bf16[4,256,256]{2,1,0:T(8,128)(2,1)S(1)} %get-tuple-element.12.w_first, ...), custom_call_target="tpu_custom_call" | custom-call | tf_op jit(solution)/shard_map/shade/pallas_call | solution.py:382
  15.8 0.0 collective-permute-start.2
  15.8 1.6 %collective-permute-start.1 = (bf16[72,128]{1,0:T(8,128)(2,1)S(1)}, bf16[72,128]{1,0:T(8,128)(2,1)S(1)}, u32[]{:S(2)}, u32[]{:S(2)}) collective-permute-start(bf16[72,128]{1,0:T(8,128)(2,1)S(1)} %shade.1.refs_3_), channel_id=1, source_target_pairs={{0,2},{1,3},{2,0},{3,1},{4,6},{5,7},{6,4},{7,5},{8,10},{9,11},{10,... | collective-permute-start | bytes 55304 | tf_op jit(solution)/shard_map/ppermute | solution.py:396
  17.4 0.3 %collective-permute-start = (bf16[72,128]{1,0:T(8,128)(2,1)S(1)}, bf16[72,128]{1,0:T(8,128)(2,1)S(1)}, u32[]{:S(2)}, u32[]{:S(2)}) collective-permute-start(bf16[72,128]{1,0:T(8,128)(2,1)S(1)} %shade.1.refs_3_), channel_id=1, source_target_pairs={{0,1},{1,0},{2,3},{3,2},{4,5},{5,4},{6,7},{7,6},{8,9},{9,8},{10,11... | collective-permute-start | bytes 55304 | tf_op jit(solution)/shard_map/ppermute | solution.py:396
  17.7 0.4 %empty.1.refs_4_ = f32[8,128]{1,0:T(8,128)S(1)} custom-call(bf16[1,256]{1,0:T(2,128)(2,1)S(1)} %broadcast_in_dim.3.trans_weight, bf16[2,256,256]{2,1,0:T(8,128)(2,1)S(1)} %get-tuple-element.13.w_mid, bf16[4,256]{1,0:T(4,128)(2,1)S(1)} %get-tuple-element.14.w_out), custom_call_target="tpu_custom_call" | custom-call | flops 100000 | bytes 1000000 | tf_op jit(solution)/shard_map/empty/pallas_call | solution.py:373
  18.1 1.0 %collective-permute-done.2.refs_2_ = bf16[72,128]{1,0:T(8,128)(2,1)S(1)} collective-permute-done((bf16[72,128]{1,0:T(8,128)(2,1)S(1)}, bf16[72,128]{1,0:T(8,128)(2,1)S(1)}, u32[]{:S(2)}, u32[]{:S(2)}) %collective-permute-start.2) | collective-permute-done | bytes 18464 | tf_op jit(solution)/shard_map/ppermute | solution.py:396
  19.2 0.5 %collective-permute-done.1.refs_1_ = bf16[72,128]{1,0:T(8,128)(2,1)S(1)} collective-permute-done((bf16[72,128]{1,0:T(8,128)(2,1)S(1)}, bf16[72,128]{1,0:T(8,128)(2,1)S(1)}, u32[]{:S(2)}, u32[]{:S(2)}) %collective-permute-start.1) | collective-permute-done | bytes 18464 | tf_op jit(solution)/shard_map/ppermute | solution.py:396
  19.6 0.0 collective-permute-done.refs_0_
  19.6 0.9 %join.1 = bf16[1,4,32,4,128]{4,3,2,1,0:T(4,128)(2,1)} custom-call(bf16[72,128]{1,0:T(8,128)(2,1)S(1)} %collective-permute-done.refs_0_, bf16[72,128]{1,0:T(8,128)(2,1)S(1)} %collective-permute-done.1.refs_1_, bf16[72,128]{1,0:T(8,128)(2,1)S(1)} %collective-permute-done.2.refs_2_, bf16[72,128]{1,0:T(8,128)(2,1)S(1)} %shade.1.refs_3_, f32[8,128]{1,0:T(8,128)S(1)} %empty.1.refs_4_), custom_call_target="tpu_custom_call" | custom-call | tf_op jit(solution)/shard_map/join/pallas_call | solution.py:399
  (1 shorter events, 0.0 us)
Async XLA Ops:
  1.7 8.5 %copy-start = (s32[1,8,8]{2,1,0:T(8,128)S(1)}, s32[1,8,8]{2,1,0:T(8,128)}, u32[]{:S(2)}) copy-start(s32[1,8,8]{2,1,0:T(8,128)} %far_counts.1) | copy-start | bytes 772
  1.7 8.5 %copy-start.2 = (s32[1,8,16]{2,1,0:T(8,128)S(1)}, s32[1,8,16]{2,1,0:T(8,128)}, u32[]{:S(2)}) copy-start(s32[1,8,16]{2,1,0:T(8,128)} %refs_1_.1) | copy-start | bytes 1540
  1.7 8.5 %copy-start.3 = (s32[1,1024]{1,0:T(1,128)S(1)}, s32[1,1024]{1,0:T(1,128)}, u32[]{:S(2)}) copy-start(s32[1,1024]{1,0:T(1,128)} %refs_2_.1) | copy-start | bytes 12292
  1.7 8.5 %copy-start.5 = (s32[8]{0:T(128)S(1)}, s32[8]{0:T(128)}, u32[]{:S(2)}) copy-start(s32[8]{0:T(128)} %refs_3_.1) | copy-start | bytes 100
  1.7 9.4 %copy-start.6 = (bf16[256]{0:T(256)(128)(2,1)S(1)}, bf16[256]{0:T(256)(128)(2,1)}, u32[]{:S(2)}) copy-start(bf16[256]{0:T(256)(128)(2,1)} %param.17) | copy-start | bytes 1540
  1.7 9.4 %copy-start.4 = (bf16[4,256]{1,0:T(4,128)(2,1)S(1)}, bf16[4,256]{1,0:T(4,128)(2,1)}, u32[]{:S(2)}) copy-start(bf16[4,256]{1,0:T(4,128)(2,1)} %far_out.1) | copy-start | bytes 6148
  1.8 12.5 %all-to-all-start = ((bf16[8,72,128]{2,1,0:T(8,128)(2,1)}), bf16[8,72,128]{2,1,0:T(8,128)(2,1)S(1)}, u32[]{:S(2)}, u32[]{:S(2)}) async-start(bf16[8,72,128]{2,1,0:T(8,128)(2,1)} %pack.1), calls=%async_computation | async-start | bytes 294912 | tf_op jit(solution)/shard_map/all_to_all | solution.py:337
  10.2 1.0 %copy-start.1 = (bf16[256,32]{0,1:T(8,128)(2,1)S(1)}, bf16[256,32]{0,1:T(8,128)(2,1)}, u32[]{:S(2)}) copy-start(bf16[256,32]{0,1:T(8,128)(2,1)} %param.16) | copy-start | bytes 49156
  15.8 3.4 %collective-permute-start.2 = (bf16[72,128]{1,0:T(8,128)(2,1)S(1)}, bf16[72,128]{1,0:T(8,128)(2,1)S(1)}, u32[]{:S(2)}, u32[]{:S(2)}) collective-permute-start(bf16[72,128]{1,0:T(8,128)(2,1)S(1)} %shade.1.refs_3_), channel_id=1, source_target_pairs={{0,3},{1,2},{2,1},{3,0},{4,7},{5,6},{6,5},{7,4},{8,11},{9,10},{10,... | collective-permute-start | bytes 55304 | tf_op jit(solution)/shard_map/ppermute | solution.py:396
  15.8 3.8 %collective-permute-start.1 = (bf16[72,128]{1,0:T(8,128)(2,1)S(1)}, bf16[72,128]{1,0:T(8,128)(2,1)S(1)}, u32[]{:S(2)}, u32[]{:S(2)}) collective-permute-start(bf16[72,128]{1,0:T(8,128)(2,1)S(1)} %shade.1.refs_3_), channel_id=1, source_target_pairs={{0,2},{1,3},{2,0},{3,1},{4,6},{5,7},{6,4},{7,5},{8,10},{9,11},{10,... | collective-permute-start | bytes 55304 | tf_op jit(solution)/shard_map/ppermute | solution.py:396
  17.4 2.3 %collective-permute-start = (bf16[72,128]{1,0:T(8,128)(2,1)S(1)}, bf16[72,128]{1,0:T(8,128)(2,1)S(1)}, u32[]{:S(2)}, u32[]{:S(2)}) collective-permute-start(bf16[72,128]{1,0:T(8,128)(2,1)S(1)} %shade.1.refs_3_), channel_id=1, source_target_pairs={{0,1},{1,0},{2,3},{3,2},{4,5},{5,4},{6,7},{7,6},{8,9},{9,8},{10,11... | collective-permute-start | bytes 55304 | tf_op jit(solution)/shard_map/ppermute | solution.py:396

commit v6 on v2

--- a/solution.py
+++ b/solution.py
@@ -99,7 +99,6 @@
     n_slab = sends.shape[0]
     place = [exchange_order(n_slab).index(c) for c in range(n_slab)]
     slots, feats, span = colors.shape
-    me = lax.axis_index("slab")
     part = slots // PARTS
     copies = [
         pltpu.make_async_copy(far_counts, counts, sems.at[0]),
@@ -112,6 +111,7 @@
     ]
     for copy in copies:
         copy.start()
+    me = lax.axis_index("slab")
     copies[0].wait()
     mine = counts[0, pl.ds(me, 1), :].astype(jnp.float32)
     before = lax.broadcasted_iota(jnp.int32, mine.shape, 1)
@@ -146,7 +146,8 @@
 
 
 def plan_kernel(n_slab, slots, *refs):
-    (counts, blocks, assign, depth), (rows, codes) = refs[:4], refs[4:]
+    (counts, blocks, assign, depth), (rows, codes, strip) = refs[:4], refs[4:]
+    strip[...] = jnp.full(strip.shape, lax.axis_index("strip"), jnp.int32)
     items = n_slab * MOST
     outs = codes.shape[1] // (2 * items)
     me = lax.axis_index("slab")
@@ -277,12 +278,12 @@
 
 
 def join_kernel(*refs):
-    *got, empty, out, held, sems = refs
+    *got, empty, strip, out, held, sems = refs
     _, n_strip, tile, outs, span = out.shape
     lines = tile * outs
     count = got[0].shape[0] - ROWS
-    me = lax.axis_index("strip")
-    want = lax.broadcasted_iota(jnp.int32, (lines, count), 0) + me * lines
+    me = strip[0, 0]
+    want = lax.broadcasted_iota(jnp.int32, (lines, count), 0) + strip[:1, :count] * lines
     chan = lax.broadcasted_iota(jnp.int32, (lines, count), 1) % outs
     filler = jnp.concatenate([empty[...]] * (lines // ROWS))
     ones = jnp.ones((count, span), jnp.bfloat16)
@@ -350,14 +351,15 @@
     rough = pl.CostEstimate(flops=10**5, bytes_accessed=10**6, transcendentals=0)
     roomy = pltpu.CompilerParams(vmem_limit_bytes=16 * 1024 * 1024)
     trans_row = trans_weight[None]
-    rows, codes = pl.pallas_call(
+    rows, codes, strip = pl.pallas_call(
         functools.partial(plan_kernel, n_slab, slots),
         out_shape=[
             jax.ShapeDtypeStruct((3, items, span), jnp.int32),
             jax.ShapeDtypeStruct((ROWS, span), jnp.bfloat16),
+            jax.ShapeDtypeStruct((ROWS, span), jnp.int32),
         ],
         in_specs=[smem] * 4,
-        out_specs=[vmem] * 2,
+        out_specs=[vmem] * 3,
         compiler_params=small,
         cost_estimate=rough,
         name="plan",
@@ -408,7 +410,7 @@
     return pl.pallas_call(
         join_kernel,
         out_shape=jax.ShapeDtypeStruct((1, n_strip, LB // n_strip, outs, span), jnp.bfloat16),
-        in_specs=[vmem] * (n_strip + 1),
+        in_specs=[vmem] * (n_strip + 2),
         out_specs=pl.BlockSpec(memory_space=pl.ANY),
         scratch_shapes=[
             pltpu.VMEM((n_strip, LB // n_strip, outs, span), jnp.bfloat16),
@@ -416,7 +418,7 @@
         ],
         compiler_params=small,
         name="join",
-    )(*tiles, empty)
+    )(*tiles, empty, strip)
 
 
 def solution(mesh):

time: 20.8 us -> 20.8 us (level)
  no operation moved by 1% of the time
where the time goes in v6:
time: 20.8 us; the launch traced here: 20.5 us
  starting transfers between devices  10.3 us (50%)
  Pallas kernels  6.58 us (32%)
  waiting for transfers between devices  3.46 us (17%)
    all_to_all x1, starting transfers between devices, compact_device(): lax.all_to_all(sends, 'slab', split_axis=0, concat_axis=0, axis_index_gro...  8.41 us
    all_to_all x1, waiting for transfers between devices, compact_device(): lax.all_to_all(sends, 'slab', split_axis=0, concat_axis=0, axis_index_gro...  1.93 us
    ppermute x3, starting transfers between devices, compact_device(): lax.ppermute(shaded, 'strip', [(s, s ^ k) for s in range(n_strip)])  1.88 us
    pallas_call x1, Pallas kernels, compact_device(): pl.pallas_call(pack_kernel, out_shape=jax.ShapeDtypeStruct((n_slab, messa...  1.7 us
    pallas_call x1, Pallas kernels, compact_device(): pl.pallas_call(shade_kernel, out_shape=jax.ShapeDtypeStruct((items * outs...  1.56 us
    ppermute x3, waiting for transfers between devices, compact_device(): lax.ppermute(shaded, 'strip', [(s, s ^ k) for s in range(n_strip)])  1.53 us
    pallas_call x1, Pallas kernels, compact_device(): pl.pallas_call(place_kernel, out_shape=[jax.ShapeDtypeStruct((GROUP, 2 *...  1.1 us
    pallas_call x1, Pallas kernels, compact_device(): pl.pallas_call(functools.partial(plan_kernel, n_slab, slots), out_shape=[...  0.94 us
  transfers between devices with their start and end apart: 4, of which 3 were waited for; matrix products, arithmetic and copies ran while one was open for 0% of the time, Pallas kernels for 12%

profile of v6, /device:TPU:0, one launch (start us, length us, event | category | flops | bytes accessed | tf_op | source)
XLA Modules:
  0.0 20.5 jit_solution(4725730332076264057)
XLA Ops:
  0.0 1.7 %pack.1 = bf16[8,72,128]{2,1,0:T(8,128)(2,1)} custom-call(s32[1,8,8]{2,1,0:T(8,128)} %far_counts.1, bf16[1,1,16,32,128]{4,3,2,1,0:T(8,128)(2,1)} %far_colors.1, bf16[1,1,16,128]{3,2,1,0:T(8,128)(2,1)} %far_transmit.1), custom_call_target="tpu_custom_call" | custom-call | tf_op jit(solution)/shard_map/pack/pallas_call | solution.py:332
  1.7 0.0 copy-start
  1.7 0.0 copy-start.2
  1.7 0.0 copy-start.3
  1.7 0.0 copy-start.5
  1.8 0.0 copy-start.6
  1.8 0.0 copy-start.4
  1.8 8.4 %all-to-all-start = ((bf16[8,72,128]{2,1,0:T(8,128)(2,1)}), bf16[8,72,128]{2,1,0:T(8,128)(2,1)S(1)}, u32[]{:S(2)}, u32[]{:S(2)}) async-start(bf16[8,72,128]{2,1,0:T(8,128)(2,1)} %pack.1), calls=%async_computation | async-start | bytes 294912 | tf_op jit(solution)/shard_map/all_to_all | solution.py:347
  10.2 0.0 copy-done
  10.2 0.0 copy-done.2
  10.2 0.0 copy-done.3
  10.2 0.0 copy-done.5
  10.2 0.0 copy-start.1
  10.2 0.9 %plan.1 = (s32[3,16,128]{2,1,0:T(8,128)S(1)}, bf16[8,128]{1,0:T(8,128)(2,1)S(1)}, s32[8,128]{1,0:T(8,128)S(1)}) custom-call(s32[1,8,8]{2,1,0:T(8,128)S(1)} %copy-done, s32[1,8,16]{2,1,0:T(8,128)S(1)} %copy-done.2, s32[1,1024]{1,0:T(1,128)S(1)} %copy-done.3, s32[8]{0:T(128)S(1)} %copy-done.5), custom_call_target="tpu_custom_call" | custom-call | flops 100000 | bytes 1000000 | tf_op jit(solution)/shard_map/plan/pallas_call | solution.py:354
  11.2 0.0 copy-done.6
  11.2 0.0 copy-done.4
  11.2 0.0 copy-done.1
  11.2 1.1 %place.1 = (bf16[4,256,256]{2,1,0:T(8,128)(2,1)S(1)}, bf16[4,256]{1,0:T(4,128)(2,1)S(1)}, bf16[2,256,256]{2,1,0:T(8,128)(2,1)S(1)}) custom-call(bf16[32,256]{1,0:T(8,128)(2,1)S(1)} %bitcast.1, bf16[1,256]{1,0:T(2,128)(2,1)S(1)} %broadcast_in_dim.3.trans_weight, bf16[4,256]{1,0:T(4,128)(2,1)S(1)} %copy-done.4, bf16[2,256,256]{2,1,0:T(8,128)(2,1)} %far_mid.1), custom_call_target="tpu_custom_call" | custom-call | flops 100000 | bytes 1000000 | tf_op jit(solution)/shard_map/place/pallas_call | solution.py:367
  12.3 1.9 %all-to-all-done.got = bf16[8,72,128]{2,1,0:T(8,128)(2,1)S(1)} async-done(((bf16[8,72,128]{2,1,0:T(8,128)(2,1)}), bf16[8,72,128]{2,1,0:T(8,128)(2,1)S(1)}, u32[]{:S(2)}, u32[]{:S(2)}) %all-to-all-start) | async-done | bytes 147488 | tf_op jit(solution)/shard_map/all_to_all | solution.py:347
  14.3 1.6 %shade.1.refs_3_ = bf16[72,128]{1,0:T(8,128)(2,1)S(1)} custom-call(s32[3,16,128]{2,1,0:T(8,128)S(1)} %get-tuple-element.11.rows, bf16[8,128]{1,0:T(8,128)(2,1)S(1)} %get-tuple-element.12.codes, bf16[8,72,128]{2,1,0:T(8,128)(2,1)S(1)} %all-to-all-done.got, bf16[4,256,256]{2,1,0:T(8,128)(2,1)S(1)} %get-tuple-element.13.w_first, ...), custom_call_target="tpu_custom_call" | custom-call | tf_op jit(solution)/shard_map/shade/pallas_call | solution.py:393
  15.8 0.0 collective-permute-start.2
  15.8 1.6 %collective-permute-start.1 = (bf16[72,128]{1,0:T(8,128)(2,1)S(1)}, bf16[72,128]{1,0:T(8,128)(2,1)S(1)}, u32[]{:S(2)}, u32[]{:S(2)}) collective-permute-start(bf16[72,128]{1,0:T(8,128)(2,1)S(1)} %shade.1.refs_3_), channel_id=1, source_target_pairs={{0,2},{1,3},{2,0},{3,1},{4,6},{5,7},{6,4},{7,5},{8,10},{9,11},{10,... | collective-permute-start | bytes 55304 | tf_op jit(solution)/shard_map/ppermute | solution.py:407
  17.4 0.3 %collective-permute-start = (bf16[72,128]{1,0:T(8,128)(2,1)S(1)}, bf16[72,128]{1,0:T(8,128)(2,1)S(1)}, u32[]{:S(2)}, u32[]{:S(2)}) collective-permute-start(bf16[72,128]{1,0:T(8,128)(2,1)S(1)} %shade.1.refs_3_), channel_id=1, source_target_pairs={{0,1},{1,0},{2,3},{3,2},{4,5},{5,4},{6,7},{7,6},{8,9},{9,8},{10,11... | collective-permute-start | bytes 55304 | tf_op jit(solution)/shard_map/ppermute | solution.py:407
  17.7 0.4 %empty.1.refs_4_ = f32[8,128]{1,0:T(8,128)S(1)} custom-call(bf16[1,256]{1,0:T(2,128)(2,1)S(1)} %broadcast_in_dim.3.trans_weight, bf16[2,256,256]{2,1,0:T(8,128)(2,1)S(1)} %get-tuple-element.14.w_mid, bf16[4,256]{1,0:T(4,128)(2,1)S(1)} %get-tuple-element.15.w_out), custom_call_target="tpu_custom_call" | custom-call | flops 100000 | bytes 1000000 | tf_op jit(solution)/shard_map/empty/pallas_call | solution.py:384
  18.1 1.0 %collective-permute-done.2.refs_2_ = bf16[72,128]{1,0:T(8,128)(2,1)S(1)} collective-permute-done((bf16[72,128]{1,0:T(8,128)(2,1)S(1)}, bf16[72,128]{1,0:T(8,128)(2,1)S(1)}, u32[]{:S(2)}, u32[]{:S(2)}) %collective-permute-start.2) | collective-permute-done | bytes 18464 | tf_op jit(solution)/shard_map/ppermute | solution.py:407
  19.2 0.5 %collective-permute-done.1.refs_1_ = bf16[72,128]{1,0:T(8,128)(2,1)S(1)} collective-permute-done((bf16[72,128]{1,0:T(8,128)(2,1)S(1)}, bf16[72,128]{1,0:T(8,128)(2,1)S(1)}, u32[]{:S(2)}, u32[]{:S(2)}) %collective-permute-start.1) | collective-permute-done | bytes 18464 | tf_op jit(solution)/shard_map/ppermute | solution.py:407
  19.7 0.0 collective-permute-done.refs_0_
  19.7 0.9 %join.1 = bf16[1,4,32,4,128]{4,3,2,1,0:T(4,128)(2,1)} custom-call(bf16[72,128]{1,0:T(8,128)(2,1)S(1)} %collective-permute-done.refs_0_, bf16[72,128]{1,0:T(8,128)(2,1)S(1)} %collective-permute-done.1.refs_1_, bf16[72,128]{1,0:T(8,128)(2,1)S(1)} %collective-permute-done.2.refs_2_, bf16[72,128]{1,0:T(8,128)(2,1)S(1)} %shade.1.refs_3_, ...), custom_call_target="tpu_custom_call" | custom-call | tf_op jit(solution)/shard_map/join/pallas_call | solution.py:410
  (1 shorter events, 0.0 us)
Async XLA Ops:
  1.7 8.5 %copy-start = (s32[1,8,8]{2,1,0:T(8,128)S(1)}, s32[1,8,8]{2,1,0:T(8,128)}, u32[]{:S(2)}) copy-start(s32[1,8,8]{2,1,0:T(8,128)} %far_counts.1) | copy-start | bytes 772
  1.7 8.5 %copy-start.2 = (s32[1,8,16]{2,1,0:T(8,128)S(1)}, s32[1,8,16]{2,1,0:T(8,128)}, u32[]{:S(2)}) copy-start(s32[1,8,16]{2,1,0:T(8,128)} %refs_1_.1) | copy-start | bytes 1540
  1.7 8.5 %copy-start.3 = (s32[1,1024]{1,0:T(1,128)S(1)}, s32[1,1024]{1,0:T(1,128)}, u32[]{:S(2)}) copy-start(s32[1,1024]{1,0:T(1,128)} %refs_2_.1) | copy-start | bytes 12292
  1.7 8.5 %copy-start.5 = (s32[8]{0:T(128)S(1)}, s32[8]{0:T(128)}, u32[]{:S(2)}) copy-start(s32[8]{0:T(128)} %refs_3_.1) | copy-start | bytes 100
  1.8 9.4 %copy-start.6 = (bf16[256]{0:T(256)(128)(2,1)S(1)}, bf16[256]{0:T(256)(128)(2,1)}, u32[]{:S(2)}) copy-start(bf16[256]{0:T(256)(128)(2,1)} %param.17) | copy-start | bytes 1540
  1.8 9.4 %copy-start.4 = (bf16[4,256]{1,0:T(4,128)(2,1)S(1)}, bf16[4,256]{1,0:T(4,128)(2,1)}, u32[]{:S(2)}) copy-start(bf16[4,256]{1,0:T(4,128)(2,1)} %far_out.1) | copy-start | bytes 6148
  1.8 12.5 %all-to-all-start = ((bf16[8,72,128]{2,1,0:T(8,128)(2,1)}), bf16[8,72,128]{2,1,0:T(8,128)(2,1)S(1)}, u32[]{:S(2)}, u32[]{:S(2)}) async-start(bf16[8,72,128]{2,1,0:T(8,128)(2,1)} %pack.1), calls=%async_computation | async-start | bytes 294912 | tf_op jit(solution)/shard_map/all_to_all | solution.py:347
  10.2 1.0 %copy-start.1 = (bf16[256,32]{0,1:T(8,128)(2,1)S(1)}, bf16[256,32]{0,1:T(8,128)(2,1)}, u32[]{:S(2)}) copy-start(bf16[256,32]{0,1:T(8,128)(2,1)} %param.16) | copy-start | bytes 49156
  15.8 3.3 %collective-permute-start.2 = (bf16[72,128]{1,0:T(8,128)(2,1)S(1)}, bf16[72,128]{1,0:T(8,128)(2,1)S(1)}, u32[]{:S(2)}, u32[]{:S(2)}) collective-permute-start(bf16[72,128]{1,0:T(8,128)(2,1)S(1)} %shade.1.refs_3_), channel_id=1, source_target_pairs={{0,3},{1,2},{2,1},{3,0},{4,7},{5,6},{6,5},{7,4},{8,11},{9,10},{10,... | collective-permute-start | bytes 55304 | tf_op jit(solution)/shard_map/ppermute | solution.py:407
  15.8 3.8 %collective-permute-start.1 = (bf16[72,128]{1,0:T(8,128)(2,1)S(1)}, bf16[72,128]{1,0:T(8,128)(2,1)S(1)}, u32[]{:S(2)}, u32[]{:S(2)}) collective-permute-start(bf16[72,128]{1,0:T(8,128)(2,1)S(1)} %shade.1.refs_3_), channel_id=1, source_target_pairs={{0,2},{1,3},{2,0},{3,1},{4,6},{5,7},{6,4},{7,5},{8,10},{9,11},{10,... | collective-permute-start | bytes 55304 | tf_op jit(solution)/shard_map/ppermute | solution.py:407
  17.4 2.3 %collective-permute-start = (bf16[72,128]{1,0:T(8,128)(2,1)S(1)}, bf16[72,128]{1,0:T(8,128)(2,1)S(1)}, u32[]{:S(2)}, u32[]{:S(2)}) collective-permute-start(bf16[72,128]{1,0:T(8,128)(2,1)S(1)} %shade.1.refs_3_), channel_id=1, source_target_pairs={{0,1},{1,0},{2,3},{3,2},{4,5},{5,4},{6,7},{7,6},{8,9},{9,8},{10,11... | collective-permute-start | bytes 55304 | tf_op jit(solution)/shard_map/ppermute | solution.py:407

commit v7 on v6

--- a/solution.py
+++ b/solution.py
@@ -92,7 +92,7 @@
 def exchange_order(n_slab):
     half = n_slab // 2
     flip = 1 if half % 2 == 0 else 0
-    return [s for i in range(half) for s in (half + (i ^ flip), i)]
+    return [s for i in range(half) for s in (half + (i ^ flip), half - 1 - i)]
 
 
 def pack_kernel(far_counts, far_colors, far_transmit, sends, counts, colors, transmit, sems):

time: 20.8 us -> 21.1 us (1.014)
  no operation moved by 1% of the time
where the time goes in v7:
time: 21.1 us; the launch traced here: 20.8 us
  starting transfers between devices  10.3 us (49%)
  Pallas kernels  6.58 us (31%)
  waiting for transfers between devices  3.67 us (17%)
    all_to_all x1, starting transfers between devices, compact_device(): lax.all_to_all(sends, 'slab', split_axis=0, concat_axis=0, axis_index_gro...  8.45 us
    all_to_all x1, waiting for transfers between devices, compact_device(): lax.all_to_all(sends, 'slab', split_axis=0, concat_axis=0, axis_index_gro...  2.14 us
    ppermute x3, starting transfers between devices, compact_device(): lax.ppermute(shaded, 'strip', [(s, s ^ k) for s in range(n_strip)])  1.88 us
    pallas_call x1, Pallas kernels, compact_device(): pl.pallas_call(pack_kernel, out_shape=jax.ShapeDtypeStruct((n_slab, messa...  1.7 us
    pallas_call x1, Pallas kernels, compact_device(): pl.pallas_call(shade_kernel, out_shape=jax.ShapeDtypeStruct((items * outs...  1.56 us
    ppermute x3, waiting for transfers between devices, compact_device(): lax.ppermute(shaded, 'strip', [(s, s ^ k) for s in range(n_strip)])  1.53 us
    pallas_call x1, Pallas kernels, compact_device(): pl.pallas_call(place_kernel, out_shape=[jax.ShapeDtypeStruct((GROUP, 2 *...  1.1 us
    pallas_call x1, Pallas kernels, compact_device(): pl.pallas_call(functools.partial(plan_kernel, n_slab, slots), out_shape=[...  0.93 us
  transfers between devices with their start and end apart: 4, of which 3 were waited for; matrix products, arithmetic and copies ran while one was open for 0% of the time, Pallas kernels for 12%

profile of v7, /device:TPU:0, one launch (start us, length us, event | category | flops | bytes accessed | tf_op | source)
XLA Modules:
  0.0 20.8 jit_solution(7576316360032019712)
XLA Ops:
  0.0 1.7 %pack.1 = bf16[8,72,128]{2,1,0:T(8,128)(2,1)} custom-call(s32[1,8,8]{2,1,0:T(8,128)} %far_counts.1, bf16[1,1,16,32,128]{4,3,2,1,0:T(8,128)(2,1)} %far_colors.1, bf16[1,1,16,128]{3,2,1,0:T(8,128)(2,1)} %far_transmit.1), custom_call_target="tpu_custom_call" | custom-call | tf_op jit(solution)/shard_map/pack/pallas_call | solution.py:332
  1.7 0.0 copy-start
  1.7 0.0 copy-start.2
  1.7 0.0 copy-start.3
  1.7 0.0 copy-start.5
  1.8 0.0 copy-start.6
  1.8 0.0 copy-start.4
  1.8 8.5 %all-to-all-start = ((bf16[8,72,128]{2,1,0:T(8,128)(2,1)}), bf16[8,72,128]{2,1,0:T(8,128)(2,1)S(1)}, u32[]{:S(2)}, u32[]{:S(2)}) async-start(bf16[8,72,128]{2,1,0:T(8,128)(2,1)} %pack.1), calls=%async_computation | async-start | bytes 294912 | tf_op jit(solution)/shard_map/all_to_all | solution.py:347
  10.2 0.0 copy-done
  10.2 0.0 copy-done.2
  10.2 0.0 copy-done.3
  10.3 0.0 copy-done.5
  10.3 0.0 copy-start.1
  10.3 0.9 %plan.1 = (s32[3,16,128]{2,1,0:T(8,128)S(1)}, bf16[8,128]{1,0:T(8,128)(2,1)S(1)}, s32[8,128]{1,0:T(8,128)S(1)}) custom-call(s32[1,8,8]{2,1,0:T(8,128)S(1)} %copy-done, s32[1,8,16]{2,1,0:T(8,128)S(1)} %copy-done.2, s32[1,1024]{1,0:T(1,128)S(1)} %copy-done.3, s32[8]{0:T(128)S(1)} %copy-done.5), custom_call_target="tpu_custom_call" | custom-call | flops 100000 | bytes 1000000 | tf_op jit(solution)/shard_map/plan/pallas_call | solution.py:354
  11.2 0.0 copy-done.6
  11.2 0.0 copy-done.4
  11.2 0.0 copy-done.1
  11.3 1.1 %place.1 = (bf16[4,256,256]{2,1,0:T(8,128)(2,1)S(1)}, bf16[4,256]{1,0:T(4,128)(2,1)S(1)}, bf16[2,256,256]{2,1,0:T(8,128)(2,1)S(1)}) custom-call(bf16[32,256]{1,0:T(8,128)(2,1)S(1)} %bitcast.1, bf16[1,256]{1,0:T(2,128)(2,1)S(1)} %broadcast_in_dim.3.trans_weight, bf16[4,256]{1,0:T(4,128)(2,1)S(1)} %copy-done.4, bf16[2,256,256]{2,1,0:T(8,128)(2,1)} %far_mid.1), custom_call_target="tpu_custom_call" | custom-call | flops 100000 | bytes 1000000 | tf_op jit(solution)/shard_map/place/pallas_call | solution.py:367
  12.4 2.1 %all-to-all-done.got = bf16[8,72,128]{2,1,0:T(8,128)(2,1)S(1)} async-done(((bf16[8,72,128]{2,1,0:T(8,128)(2,1)}), bf16[8,72,128]{2,1,0:T(8,128)(2,1)S(1)}, u32[]{:S(2)}, u32[]{:S(2)}) %all-to-all-start) | async-done | bytes 147488 | tf_op jit(solution)/shard_map/all_to_all | solution.py:347
  14.5 1.6 %shade.1.refs_3_ = bf16[72,128]{1,0:T(8,128)(2,1)S(1)} custom-call(s32[3,16,128]{2,1,0:T(8,128)S(1)} %get-tuple-element.11.rows, bf16[8,128]{1,0:T(8,128)(2,1)S(1)} %get-tuple-element.12.codes, bf16[8,72,128]{2,1,0:T(8,128)(2,1)S(1)} %all-to-all-done.got, bf16[4,256,256]{2,1,0:T(8,128)(2,1)S(1)} %get-tuple-element.13.w_first, ...), custom_call_target="tpu_custom_call" | custom-call | tf_op jit(solution)/shard_map/shade/pallas_call | solution.py:393
  16.1 0.0 collective-permute-start.2
  16.1 1.6 %collective-permute-start.1 = (bf16[72,128]{1,0:T(8,128)(2,1)S(1)}, bf16[72,128]{1,0:T(8,128)(2,1)S(1)}, u32[]{:S(2)}, u32[]{:S(2)}) collective-permute-start(bf16[72,128]{1,0:T(8,128)(2,1)S(1)} %shade.1.refs_3_), channel_id=1, source_target_pairs={{0,2},{1,3},{2,0},{3,1},{4,6},{5,7},{6,4},{7,5},{8,10},{9,11},{10,... | collective-permute-start | bytes 55304 | tf_op jit(solution)/shard_map/ppermute | solution.py:407
  17.6 0.3 %collective-permute-start = (bf16[72,128]{1,0:T(8,128)(2,1)S(1)}, bf16[72,128]{1,0:T(8,128)(2,1)S(1)}, u32[]{:S(2)}, u32[]{:S(2)}) collective-permute-start(bf16[72,128]{1,0:T(8,128)(2,1)S(1)} %shade.1.refs_3_), channel_id=1, source_target_pairs={{0,1},{1,0},{2,3},{3,2},{4,5},{5,4},{6,7},{7,6},{8,9},{9,8},{10,11... | collective-permute-start | bytes 55304 | tf_op jit(solution)/shard_map/ppermute | solution.py:407
  17.9 0.4 %empty.1.refs_4_ = f32[8,128]{1,0:T(8,128)S(1)} custom-call(bf16[1,256]{1,0:T(2,128)(2,1)S(1)} %broadcast_in_dim.3.trans_weight, bf16[2,256,256]{2,1,0:T(8,128)(2,1)S(1)} %get-tuple-element.14.w_mid, bf16[4,256]{1,0:T(4,128)(2,1)S(1)} %get-tuple-element.15.w_out), custom_call_target="tpu_custom_call" | custom-call | flops 100000 | bytes 1000000 | tf_op jit(solution)/shard_map/empty/pallas_call | solution.py:384
  18.4 1.1 %collective-permute-done.2.refs_2_ = bf16[72,128]{1,0:T(8,128)(2,1)S(1)} collective-permute-done((bf16[72,128]{1,0:T(8,128)(2,1)S(1)}, bf16[72,128]{1,0:T(8,128)(2,1)S(1)}, u32[]{:S(2)}, u32[]{:S(2)}) %collective-permute-start.2) | collective-permute-done | bytes 18464 | tf_op jit(solution)/shard_map/ppermute | solution.py:407
  19.4 0.5 %collective-permute-done.1.refs_1_ = bf16[72,128]{1,0:T(8,128)(2,1)S(1)} collective-permute-done((bf16[72,128]{1,0:T(8,128)(2,1)S(1)}, bf16[72,128]{1,0:T(8,128)(2,1)S(1)}, u32[]{:S(2)}, u32[]{:S(2)}) %collective-permute-start.1) | collective-permute-done | bytes 18464 | tf_op jit(solution)/shard_map/ppermute | solution.py:407
  19.9 0.0 collective-permute-done.refs_0_
  19.9 0.9 %join.1 = bf16[1,4,32,4,128]{4,3,2,1,0:T(4,128)(2,1)} custom-call(bf16[72,128]{1,0:T(8,128)(2,1)S(1)} %collective-permute-done.refs_0_, bf16[72,128]{1,0:T(8,128)(2,1)S(1)} %collective-permute-done.1.refs_1_, bf16[72,128]{1,0:T(8,128)(2,1)S(1)} %collective-permute-done.2.refs_2_, bf16[72,128]{1,0:T(8,128)(2,1)S(1)} %shade.1.refs_3_, ...), custom_call_target="tpu_custom_call" | custom-call | tf_op jit(solution)/shard_map/join/pallas_call | solution.py:410
  (1 shorter events, 0.0 us)
Async XLA Ops:
  1.7 8.5 %copy-start = (s32[1,8,8]{2,1,0:T(8,128)S(1)}, s32[1,8,8]{2,1,0:T(8,128)}, u32[]{:S(2)}) copy-start(s32[1,8,8]{2,1,0:T(8,128)} %far_counts.1) | copy-start | bytes 772
  1.7 8.5 %copy-start.2 = (s32[1,8,16]{2,1,0:T(8,128)S(1)}, s32[1,8,16]{2,1,0:T(8,128)}, u32[]{:S(2)}) copy-start(s32[1,8,16]{2,1,0:T(8,128)} %refs_1_.1) | copy-start | bytes 1540
  1.7 8.5 %copy-start.3 = (s32[1,1024]{1,0:T(1,128)S(1)}, s32[1,1024]{1,0:T(1,128)}, u32[]{:S(2)}) copy-start(s32[1,1024]{1,0:T(1,128)} %refs_2_.1) | copy-start | bytes 12292
  1.7 8.5 %copy-start.5 = (s32[8]{0:T(128)S(1)}, s32[8]{0:T(128)}, u32[]{:S(2)}) copy-start(s32[8]{0:T(128)} %refs_3_.1) | copy-start | bytes 100
  1.8 9.5 %copy-start.6 = (bf16[256]{0:T(256)(128)(2,1)S(1)}, bf16[256]{0:T(256)(128)(2,1)}, u32[]{:S(2)}) copy-start(bf16[256]{0:T(256)(128)(2,1)} %param.17) | copy-start | bytes 1540
  1.8 9.5 %copy-start.4 = (bf16[4,256]{1,0:T(4,128)(2,1)S(1)}, bf16[4,256]{1,0:T(4,128)(2,1)}, u32[]{:S(2)}) copy-start(bf16[4,256]{1,0:T(4,128)(2,1)} %far_out.1) | copy-start | bytes 6148
  1.8 12.7 %all-to-all-start = ((bf16[8,72,128]{2,1,0:T(8,128)(2,1)}), bf16[8,72,128]{2,1,0:T(8,128)(2,1)S(1)}, u32[]{:S(2)}, u32[]{:S(2)}) async-start(bf16[8,72,128]{2,1,0:T(8,128)(2,1)} %pack.1), calls=%async_computation | async-start | bytes 294912 | tf_op jit(solution)/shard_map/all_to_all | solution.py:347
  10.3 1.0 %copy-start.1 = (bf16[256,32]{0,1:T(8,128)(2,1)S(1)}, bf16[256,32]{0,1:T(8,128)(2,1)}, u32[]{:S(2)}) copy-start(bf16[256,32]{0,1:T(8,128)(2,1)} %param.16) | copy-start | bytes 49156
  16.1 3.4 %collective-permute-start.2 = (bf16[72,128]{1,0:T(8,128)(2,1)S(1)}, bf16[72,128]{1,0:T(8,128)(2,1)S(1)}, u32[]{:S(2)}, u32[]{:S(2)}) collective-permute-start(bf16[72,128]{1,0:T(8,128)(2,1)S(1)} %shade.1.refs_3_), channel_id=1, source_target_pairs={{0,3},{1,2},{2,1},{3,0},{4,7},{5,6},{6,5},{7,4},{8,11},{9,10},{10,... | collective-permute-start | bytes 55304 | tf_op jit(solution)/shard_map/ppermute | solution.py:407
  16.1 3.8 %collective-permute-start.1 = (bf16[72,128]{1,0:T(8,128)(2,1)S(1)}, bf16[72,128]{1,0:T(8,128)(2,1)S(1)}, u32[]{:S(2)}, u32[]{:S(2)}) collective-permute-start(bf16[72,128]{1,0:T(8,128)(2,1)S(1)} %shade.1.refs_3_), channel_id=1, source_target_pairs={{0,2},{1,3},{2,0},{3,1},{4,6},{5,7},{6,4},{7,5},{8,10},{9,11},{10,... | collective-permute-start | bytes 55304 | tf_op jit(solution)/shard_map/ppermute | solution.py:407
  17.6 2.3 %collective-permute-start = (bf16[72,128]{1,0:T(8,128)(2,1)S(1)}, bf16[72,128]{1,0:T(8,128)(2,1)S(1)}, u32[]{:S(2)}, u32[]{:S(2)}) collective-permute-start(bf16[72,128]{1,0:T(8,128)(2,1)S(1)} %shade.1.refs_3_), channel_id=1, source_target_pairs={{0,1},{1,0},{2,3},{3,2},{4,5},{5,4},{6,7},{7,6},{8,9},{9,8},{10,11... | collective-permute-start | bytes 55304 | tf_op jit(solution)/shard_map/ppermute | solution.py:407

commit v8 on v7

--- a/solution.py
+++ b/solution.py
@@ -91,8 +91,7 @@
 
 def exchange_order(n_slab):
     half = n_slab // 2
-    flip = 1 if half % 2 == 0 else 0
-    return [s for i in range(half) for s in (half + (i ^ flip), half - 1 - i)]
+    return [s for i in range(half) for s in (half + (i + 1) % half, i)]
 
 
 def pack_kernel(far_counts, far_colors, far_transmit, sends, counts, colors, transmit, sems):

time: 21.1 us -> 20.8 us (0.986)
  no operation moved by 1% of the time
where the time goes in v8:
time: 20.8 us; the launch traced here: 20.5 us
  starting transfers between devices  10.3 us (50%)
  Pallas kernels  6.58 us (32%)
  waiting for transfers between devices  3.46 us (17%)
    all_to_all x1, starting transfers between devices, compact_device(): lax.all_to_all(sends, 'slab', split_axis=0, concat_axis=0, axis_index_gro...  8.41 us
    all_to_all x1, waiting for transfers between devices, compact_device(): lax.all_to_all(sends, 'slab', split_axis=0, concat_axis=0, axis_index_gro...  1.93 us
    ppermute x3, starting transfers between devices, compact_device(): lax.ppermute(shaded, 'strip', [(s, s ^ k) for s in range(n_strip)])  1.88 us
    pallas_call x1, Pallas kernels, compact_device(): pl.pallas_call(pack_kernel, out_shape=jax.ShapeDtypeStruct((n_slab, messa...  1.7 us
    pallas_call x1, Pallas kernels, compact_device(): pl.pallas_call(shade_kernel, out_shape=jax.ShapeDtypeStruct((items * outs...  1.56 us
    ppermute x3, waiting for transfers between devices, compact_device(): lax.ppermute(shaded, 'strip', [(s, s ^ k) for s in range(n_strip)])  1.53 us
    pallas_call x1, Pallas kernels, compact_device(): pl.pallas_call(place_kernel, out_shape=[jax.ShapeDtypeStruct((GROUP, 2 *...  1.1 us
    pallas_call x1, Pallas kernels, compact_device(): pl.pallas_call(functools.partial(plan_kernel, n_slab, slots), out_shape=[...  0.94 us
  transfers between devices with their start and end apart: 4, of which 3 were waited for; matrix products, arithmetic and copies ran while one was open for 0% of the time, Pallas kernels for 12%

profile of v8, /device:TPU:0, one launch (start us, length us, event | category | flops | bytes accessed | tf_op | source)
XLA Modules:
  0.0 20.5 jit_solution(17855897151068707382)
XLA Ops:
  0.0 1.7 %pack.1 = bf16[8,72,128]{2,1,0:T(8,128)(2,1)} custom-call(s32[1,8,8]{2,1,0:T(8,128)} %far_counts.1, bf16[1,1,16,32,128]{4,3,2,1,0:T(8,128)(2,1)} %far_colors.1, bf16[1,1,16,128]{3,2,1,0:T(8,128)(2,1)} %far_transmit.1), custom_call_target="tpu_custom_call" | custom-call | tf_op jit(solution)/shard_map/pack/pallas_call | solution.py:331
  1.7 0.0 copy-start
  1.7 0.0 copy-start.2
  1.7 0.0 copy-start.3
  1.7 0.0 copy-start.5
  1.8 0.0 copy-start.6
  1.8 0.0 copy-start.4
  1.8 8.4 %all-to-all-start = ((bf16[8,72,128]{2,1,0:T(8,128)(2,1)}), bf16[8,72,128]{2,1,0:T(8,128)(2,1)S(1)}, u32[]{:S(2)}, u32[]{:S(2)}) async-start(bf16[8,72,128]{2,1,0:T(8,128)(2,1)} %pack.1), calls=%async_computation | async-start | bytes 294912 | tf_op jit(solution)/shard_map/all_to_all | solution.py:346
  10.2 0.0 copy-done
  10.2 0.0 copy-done.2
  10.2 0.0 copy-done.3
  10.2 0.0 copy-done.5
  10.2 0.0 copy-start.1
  10.2 0.9 %plan.1 = (s32[3,16,128]{2,1,0:T(8,128)S(1)}, bf16[8,128]{1,0:T(8,128)(2,1)S(1)}, s32[8,128]{1,0:T(8,128)S(1)}) custom-call(s32[1,8,8]{2,1,0:T(8,128)S(1)} %copy-done, s32[1,8,16]{2,1,0:T(8,128)S(1)} %copy-done.2, s32[1,1024]{1,0:T(1,128)S(1)} %copy-done.3, s32[8]{0:T(128)S(1)} %copy-done.5), custom_call_target="tpu_custom_call" | custom-call | flops 100000 | bytes 1000000 | tf_op jit(solution)/shard_map/plan/pallas_call | solution.py:353
  11.2 0.0 copy-done.6
  11.2 0.0 copy-done.4
  11.2 0.0 copy-done.1
  11.2 1.1 %place.1 = (bf16[4,256,256]{2,1,0:T(8,128)(2,1)S(1)}, bf16[4,256]{1,0:T(4,128)(2,1)S(1)}, bf16[2,256,256]{2,1,0:T(8,128)(2,1)S(1)}) custom-call(bf16[32,256]{1,0:T(8,128)(2,1)S(1)} %bitcast.1, bf16[1,256]{1,0:T(2,128)(2,1)S(1)} %broadcast_in_dim.3.trans_weight, bf16[4,256]{1,0:T(4,128)(2,1)S(1)} %copy-done.4, bf16[2,256,256]{2,1,0:T(8,128)(2,1)} %far_mid.1), custom_call_target="tpu_custom_call" | custom-call | flops 100000 | bytes 1000000 | tf_op jit(solution)/shard_map/place/pallas_call | solution.py:366
  12.3 1.9 %all-to-all-done.got = bf16[8,72,128]{2,1,0:T(8,128)(2,1)S(1)} async-done(((bf16[8,72,128]{2,1,0:T(8,128)(2,1)}), bf16[8,72,128]{2,1,0:T(8,128)(2,1)S(1)}, u32[]{:S(2)}, u32[]{:S(2)}) %all-to-all-start) | async-done | bytes 147488 | tf_op jit(solution)/shard_map/all_to_all | solution.py:346
  14.3 1.6 %shade.1.refs_3_ = bf16[72,128]{1,0:T(8,128)(2,1)S(1)} custom-call(s32[3,16,128]{2,1,0:T(8,128)S(1)} %get-tuple-element.11.rows, bf16[8,128]{1,0:T(8,128)(2,1)S(1)} %get-tuple-element.12.codes, bf16[8,72,128]{2,1,0:T(8,128)(2,1)S(1)} %all-to-all-done.got, bf16[4,256,256]{2,1,0:T(8,128)(2,1)S(1)} %get-tuple-element.13.w_first, ...), custom_call_target="tpu_custom_call" | custom-call | tf_op jit(solution)/shard_map/shade/pallas_call | solution.py:392
  15.8 0.0 collective-permute-start.2
  15.8 1.6 %collective-permute-start.1 = (bf16[72,128]{1,0:T(8,128)(2,1)S(1)}, bf16[72,128]{1,0:T(8,128)(2,1)S(1)}, u32[]{:S(2)}, u32[]{:S(2)}) collective-permute-start(bf16[72,128]{1,0:T(8,128)(2,1)S(1)} %shade.1.refs_3_), channel_id=1, source_target_pairs={{0,2},{1,3},{2,0},{3,1},{4,6},{5,7},{6,4},{7,5},{8,10},{9,11},{10,... | collective-permute-start | bytes 55304 | tf_op jit(solution)/shard_map/ppermute | solution.py:406
  17.4 0.3 %collective-permute-start = (bf16[72,128]{1,0:T(8,128)(2,1)S(1)}, bf16[72,128]{1,0:T(8,128)(2,1)S(1)}, u32[]{:S(2)}, u32[]{:S(2)}) collective-permute-start(bf16[72,128]{1,0:T(8,128)(2,1)S(1)} %shade.1.refs_3_), channel_id=1, source_target_pairs={{0,1},{1,0},{2,3},{3,2},{4,5},{5,4},{6,7},{7,6},{8,9},{9,8},{10,11... | collective-permute-start | bytes 55304 | tf_op jit(solution)/shard_map/ppermute | solution.py:406
  17.7 0.4 %empty.1.refs_4_ = f32[8,128]{1,0:T(8,128)S(1)} custom-call(bf16[1,256]{1,0:T(2,128)(2,1)S(1)} %broadcast_in_dim.3.trans_weight, bf16[2,256,256]{2,1,0:T(8,128)(2,1)S(1)} %get-tuple-element.14.w_mid, bf16[4,256]{1,0:T(4,128)(2,1)S(1)} %get-tuple-element.15.w_out), custom_call_target="tpu_custom_call" | custom-call | flops 100000 | bytes 1000000 | tf_op jit(solution)/shard_map/empty/pallas_call | solution.py:383
  18.1 1.0 %collective-permute-done.2.refs_2_ = bf16[72,128]{1,0:T(8,128)(2,1)S(1)} collective-permute-done((bf16[72,128]{1,0:T(8,128)(2,1)S(1)}, bf16[72,128]{1,0:T(8,128)(2,1)S(1)}, u32[]{:S(2)}, u32[]{:S(2)}) %collective-permute-start.2) | collective-permute-done | bytes 18464 | tf_op jit(solution)/shard_map/ppermute | solution.py:406
  19.2 0.5 %collective-permute-done.1.refs_1_ = bf16[72,128]{1,0:T(8,128)(2,1)S(1)} collective-permute-done((bf16[72,128]{1,0:T(8,128)(2,1)S(1)}, bf16[72,128]{1,0:T(8,128)(2,1)S(1)}, u32[]{:S(2)}, u32[]{:S(2)}) %collective-permute-start.1) | collective-permute-done | bytes 18464 | tf_op jit(solution)/shard_map/ppermute | solution.py:406
  19.7 0.0 collective-permute-done.refs_0_
  19.7 0.9 %join.1 = bf16[1,4,32,4,128]{4,3,2,1,0:T(4,128)(2,1)} custom-call(bf16[72,128]{1,0:T(8,128)(2,1)S(1)} %collective-permute-done.refs_0_, bf16[72,128]{1,0:T(8,128)(2,1)S(1)} %collective-permute-done.1.refs_1_, bf16[72,128]{1,0:T(8,128)(2,1)S(1)} %collective-permute-done.2.refs_2_, bf16[72,128]{1,0:T(8,128)(2,1)S(1)} %shade.1.refs_3_, ...), custom_call_target="tpu_custom_call" | custom-call | tf_op jit(solution)/shard_map/join/pallas_call | solution.py:409
  (1 shorter events, 0.0 us)
Async XLA Ops:
  1.7 8.5 %copy-start = (s32[1,8,8]{2,1,0:T(8,128)S(1)}, s32[1,8,8]{2,1,0:T(8,128)}, u32[]{:S(2)}) copy-start(s32[1,8,8]{2,1,0:T(8,128)} %far_counts.1) | copy-start | bytes 772
  1.7 8.5 %copy-start.2 = (s32[1,8,16]{2,1,0:T(8,128)S(1)}, s32[1,8,16]{2,1,0:T(8,128)}, u32[]{:S(2)}) copy-start(s32[1,8,16]{2,1,0:T(8,128)} %refs_1_.1) | copy-start | bytes 1540
  1.7 8.5 %copy-start.3 = (s32[1,1024]{1,0:T(1,128)S(1)}, s32[1,1024]{1,0:T(1,128)}, u32[]{:S(2)}) copy-start(s32[1,1024]{1,0:T(1,128)} %refs_2_.1) | copy-start | bytes 12292
  1.7 8.5 %copy-start.5 = (s32[8]{0:T(128)S(1)}, s32[8]{0:T(128)}, u32[]{:S(2)}) copy-start(s32[8]{0:T(128)} %refs_3_.1) | copy-start | bytes 100
  1.8 9.4 %copy-start.6 = (bf16[256]{0:T(256)(128)(2,1)S(1)}, bf16[256]{0:T(256)(128)(2,1)}, u32[]{:S(2)}) copy-start(bf16[256]{0:T(256)(128)(2,1)} %param.17) | copy-start | bytes 1540
  1.8 9.4 %copy-start.4 = (bf16[4,256]{1,0:T(4,128)(2,1)S(1)}, bf16[4,256]{1,0:T(4,128)(2,1)}, u32[]{:S(2)}) copy-start(bf16[4,256]{1,0:T(4,128)(2,1)} %far_out.1) | copy-start | bytes 6148
  1.8 12.5 %all-to-all-start = ((bf16[8,72,128]{2,1,0:T(8,128)(2,1)}), bf16[8,72,128]{2,1,0:T(8,128)(2,1)S(1)}, u32[]{:S(2)}, u32[]{:S(2)}) async-start(bf16[8,72,128]{2,1,0:T(8,128)(2,1)} %pack.1), calls=%async_computation | async-start | bytes 294912 | tf_op jit(solution)/shard_map/all_to_all | solution.py:346
  10.2 1.0 %copy-start.1 = (bf16[256,32]{0,1:T(8,128)(2,1)S(1)}, bf16[256,32]{0,1:T(8,128)(2,1)}, u32[]{:S(2)}) copy-start(bf16[256,32]{0,1:T(8,128)(2,1)} %param.16) | copy-start | bytes 49156
  15.8 3.3 %collective-permute-start.2 = (bf16[72,128]{1,0:T(8,128)(2,1)S(1)}, bf16[72,128]{1,0:T(8,128)(2,1)S(1)}, u32[]{:S(2)}, u32[]{:S(2)}) collective-permute-start(bf16[72,128]{1,0:T(8,128)(2,1)S(1)} %shade.1.refs_3_), channel_id=1, source_target_pairs={{0,3},{1,2},{2,1},{3,0},{4,7},{5,6},{6,5},{7,4},{8,11},{9,10},{10,... | collective-permute-start | bytes 55304 | tf_op jit(solution)/shard_map/ppermute | solution.py:406
  15.8 3.8 %collective-permute-start.1 = (bf16[72,128]{1,0:T(8,128)(2,1)S(1)}, bf16[72,128]{1,0:T(8,128)(2,1)S(1)}, u32[]{:S(2)}, u32[]{:S(2)}) collective-permute-start(bf16[72,128]{1,0:T(8,128)(2,1)S(1)} %shade.1.refs_3_), channel_id=1, source_target_pairs={{0,2},{1,3},{2,0},{3,1},{4,6},{5,7},{6,4},{7,5},{8,10},{9,11},{10,... | collective-permute-start | bytes 55304 | tf_op jit(solution)/shard_map/ppermute | solution.py:406
  17.4 2.3 %collective-permute-start = (bf16[72,128]{1,0:T(8,128)(2,1)S(1)}, bf16[72,128]{1,0:T(8,128)(2,1)S(1)}, u32[]{:S(2)}, u32[]{:S(2)}) collective-permute-start(bf16[72,128]{1,0:T(8,128)(2,1)S(1)} %shade.1.refs_3_), channel_id=1, source_target_pairs={{0,1},{1,0},{2,3},{3,2},{4,5},{5,4},{6,7},{7,6},{8,9},{9,8},{10,11... | collective-permute-start | bytes 55304 | tf_op jit(solution)/shard_map/ppermute | solution.py:406

commit v9 on v5

--- a/solution.py
+++ b/solution.py
@@ -88,55 +88,43 @@
 GROUP = 4
 
 
-def exchange_place(n_slab, c):
-    half = n_slab // 2
-    flip = 1 if half % 2 == 0 else 0
-    return jnp.where(c < half, 2 * c + 1, 2 * ((c - half) ^ flip))
-
-
 def exchange_order(n_slab):
     half = n_slab // 2
-    flip = 1 if half % 2 == 0 else 0
-    return [s for i in range(half) for s in (half + (i ^ flip), i)]
+    return [s for i in range(half) for s in (half + (i + 1) % half, i)]
 
 
 def pack_kernel(far_counts, far_colors, far_transmit, sends, counts, colors, transmit, tall, sems):
     n_slab = sends.shape[0]
-    slots, feats, span = colors.shape
-    me = lax.axis_index("slab")
+    order = exchange_order(n_slab)
+    slots, feats, span = colors.shape[2:]
     copies = [
         pltpu.make_async_copy(far, near, sems.at[i])
         for i, (far, near) in enumerate(
-            (
-                (far_counts, counts),
-                (far_transmit.at[0, 0], transmit),
-                (far_colors.at[0, 0], colors),
-            )
+            ((far_counts, counts), (far_colors, colors), (far_transmit, transmit))
         )
     ]
     for copy in copies:
         copy.start()
+    me = lax.axis_index("slab")
+    for copy in copies:
+        copy.wait()
+    tall[...] = transmit[0, 0].astype(jnp.float32)
     row = lax.broadcasted_iota(jnp.int32, (ROWS, span), 0)
-    copies[1].wait()
-    tall[...] = transmit[...].astype(jnp.float32)
-    copies[0].wait()
-    copies[2].wait()
-
-    def fill(c, off):
+    off = jnp.int32(0)
+    for c in range(n_slab):
+        at = order.index(c)
         tail = jnp.ones((ROWS, span), jnp.float32)
-        at = exchange_place(n_slab, c)
         for r in range(MOST):
             slot = jnp.minimum(off + r, slots - 1)
-            sends[at, pl.ds(r * feats, feats), :] = colors[slot]
+            sends[at, pl.ds(r * feats, feats), :] = colors[0, 0, slot]
             tail = jnp.where(row == r, tall[pl.ds(slot, 1), :], tail)
         sends[at, pl.ds(MOST * feats, ROWS), :] = tail.astype(jnp.bfloat16)
-        return off + counts[0, me, c]
-
-    lax.fori_loop(0, n_slab, fill, jnp.int32(0))
+        off = off + counts[0, me, c]
 
 
 def plan_kernel(n_slab, slots, *refs):
-    (counts, blocks, assign, depth), (rows, codes) = refs[:4], refs[4:]
+    (counts, blocks, assign, depth), (rows, codes, strip) = refs[:4], refs[4:]
+    strip[...] = jnp.full(strip.shape, lax.axis_index("strip"), jnp.int32)
     items = n_slab * MOST
     outs = codes.shape[1] // (2 * items)
     me = lax.axis_index("slab")
@@ -267,12 +255,12 @@
 
 
 def join_kernel(*refs):
-    *got, empty, out, held, sems = refs
+    *got, empty, strip, out, held, sems = refs
     _, n_strip, tile, outs, span = out.shape
     lines = tile * outs
     count = got[0].shape[0] - ROWS
-    me = lax.axis_index("strip")
-    want = lax.broadcasted_iota(jnp.int32, (lines, count), 0) + me * lines
+    me = strip[0, 0]
+    want = lax.broadcasted_iota(jnp.int32, (lines, count), 0) + strip[:1, :count] * lines
     chan = lax.broadcasted_iota(jnp.int32, (lines, count), 1) % outs
     filler = jnp.concatenate([empty[...]] * (lines // ROWS))
     ones = jnp.ones((count, span), jnp.bfloat16)
@@ -325,8 +313,8 @@
         out_specs=vmem,
         scratch_shapes=[
             pltpu.SMEM(pair_counts.shape, jnp.int32),
-            pltpu.VMEM(colors.shape[2:], colors.dtype),
-            pltpu.VMEM(transmit.shape[2:], transmit.dtype),
+            pltpu.VMEM(colors.shape, colors.dtype),
+            pltpu.VMEM(transmit.shape, transmit.dtype),
             pltpu.VMEM(transmit.shape[2:], jnp.float32),
             pltpu.SemaphoreType.DMA((3,)),
         ],
@@ -341,14 +329,15 @@
     rough = pl.CostEstimate(flops=10**5, bytes_accessed=10**6, transcendentals=0)
     roomy = pltpu.CompilerParams(vmem_limit_bytes=16 * 1024 * 1024)
     trans_row = trans_weight[None]
-    rows, codes = pl.pallas_call(
+    rows, codes, strip = pl.pallas_call(
         functools.partial(plan_kernel, n_slab, slots),
         out_shape=[
             jax.ShapeDtypeStruct((3, items, span), jnp.int32),
             jax.ShapeDtypeStruct((ROWS, span), jnp.bfloat16),
+            jax.ShapeDtypeStruct((ROWS, span), jnp.int32),
         ],
         in_specs=[smem] * 4,
-        out_specs=[vmem] * 2,
+        out_specs=[vmem] * 3,
         compiler_params=small,
         cost_estimate=rough,
         name="plan",
@@ -399,7 +388,7 @@
     return pl.pallas_call(
         join_kernel,
         out_shape=jax.ShapeDtypeStruct((1, n_strip, LB // n_strip, outs, span), jnp.bfloat16),
-        in_specs=[vmem] * (n_strip + 1),
+        in_specs=[vmem] * (n_strip + 2),
         out_specs=pl.BlockSpec(memory_space=pl.ANY),
         scratch_shapes=[
             pltpu.VMEM((n_strip, LB // n_strip, outs, span), jnp.bfloat16),
@@ -407,7 +396,7 @@
         ],
         compiler_params=small,
         name="join",
-    )(*tiles, empty)
+    )(*tiles, empty, strip)
 
 
 def solution(mesh):

time: 20.8 us -> 20.7 us (level)
  no operation moved by 1% of the time
where the time goes in v9:
time: 20.7 us; the launch traced here: 20.4 us
  starting transfers between devices  10.3 us (50%)
  Pallas kernels  6.51 us (31%)
  waiting for transfers between devices  3.46 us (17%)
    all_to_all x1, starting transfers between devices, compact_device(): lax.all_to_all(sends, 'slab', split_axis=0, concat_axis=0, axis_index_gro...  8.41 us
    all_to_all x1, waiting for transfers between devices, compact_device(): lax.all_to_all(sends, 'slab', split_axis=0, concat_axis=0, axis_index_gro...  1.93 us
    ppermute x3, starting transfers between devices, compact_device(): lax.ppermute(shaded, 'strip', [(s, s ^ k) for s in range(n_strip)])  1.88 us
    pallas_call x1, Pallas kernels, compact_device(): pl.pallas_call(pack_kernel, out_shape=jax.ShapeDtypeStruct((n_slab, messa...  1.62 us
    pallas_call x1, Pallas kernels, compact_device(): pl.pallas_call(shade_kernel, out_shape=jax.ShapeDtypeStruct((items * outs...  1.56 us
    ppermute x3, waiting for transfers between devices, compact_device(): lax.ppermute(shaded, 'strip', [(s, s ^ k) for s in range(n_strip)])  1.53 us
    pallas_call x1, Pallas kernels, compact_device(): pl.pallas_call(place_kernel, out_shape=[jax.ShapeDtypeStruct((GROUP, 2 *...  1.1 us
    pallas_call x1, Pallas kernels, compact_device(): pl.pallas_call(functools.partial(plan_kernel, n_slab, slots), out_shape=[...  0.94 us
  transfers between devices with their start and end apart: 4, of which 3 were waited for; matrix products, arithmetic and copies ran while one was open for 0% of the time, Pallas kernels for 12%

profile of v9, /device:TPU:0, one launch (start us, length us, event | category | flops | bytes accessed | tf_op | source)
XLA Modules:
  0.0 20.4 jit_solution(18196359262206966235)
XLA Ops:
  0.0 1.6 %pack.1 = bf16[8,72,128]{2,1,0:T(8,128)(2,1)} custom-call(s32[1,8,8]{2,1,0:T(8,128)} %far_counts.1, bf16[1,1,16,32,128]{4,3,2,1,0:T(8,128)(2,1)} %far_colors.1, bf16[1,1,16,128]{3,2,1,0:T(8,128)(2,1)} %far_transmit.1), custom_call_target="tpu_custom_call" | custom-call | tf_op jit(solution)/shard_map/pack/pallas_call | solution.py:309
  1.6 0.0 copy-start
  1.6 0.0 copy-start.2
  1.7 0.0 copy-start.3
  1.7 0.0 copy-start.5
  1.7 0.0 copy-start.6
  1.7 0.0 copy-start.4
  1.7 8.4 %all-to-all-start = ((bf16[8,72,128]{2,1,0:T(8,128)(2,1)}), bf16[8,72,128]{2,1,0:T(8,128)(2,1)S(1)}, u32[]{:S(2)}, u32[]{:S(2)}) async-start(bf16[8,72,128]{2,1,0:T(8,128)(2,1)} %pack.1), calls=%async_computation | async-start | bytes 294912 | tf_op jit(solution)/shard_map/all_to_all | solution.py:325
  10.1 0.0 copy-done
  10.1 0.0 copy-done.2
  10.1 0.0 copy-done.3
  10.1 0.0 copy-done.5
  10.1 0.0 copy-start.1
  10.2 0.9 %plan.1 = (s32[3,16,128]{2,1,0:T(8,128)S(1)}, bf16[8,128]{1,0:T(8,128)(2,1)S(1)}, s32[8,128]{1,0:T(8,128)S(1)}) custom-call(s32[1,8,8]{2,1,0:T(8,128)S(1)} %copy-done, s32[1,8,16]{2,1,0:T(8,128)S(1)} %copy-done.2, s32[1,1024]{1,0:T(1,128)S(1)} %copy-done.3, s32[8]{0:T(128)S(1)} %copy-done.5), custom_call_target="tpu_custom_call" | custom-call | flops 100000 | bytes 1000000 | tf_op jit(solution)/shard_map/plan/pallas_call | solution.py:332
  11.1 0.0 copy-done.6
  11.1 0.0 copy-done.4
  11.1 0.0 copy-done.1
  11.1 1.1 %place.1 = (bf16[4,256,256]{2,1,0:T(8,128)(2,1)S(1)}, bf16[4,256]{1,0:T(4,128)(2,1)S(1)}, bf16[2,256,256]{2,1,0:T(8,128)(2,1)S(1)}) custom-call(bf16[32,256]{1,0:T(8,128)(2,1)S(1)} %bitcast.1, bf16[1,256]{1,0:T(2,128)(2,1)S(1)} %broadcast_in_dim.3.trans_weight, bf16[4,256]{1,0:T(4,128)(2,1)S(1)} %copy-done.4, bf16[2,256,256]{2,1,0:T(8,128)(2,1)} %far_mid.1), custom_call_target="tpu_custom_call" | custom-call | flops 100000 | bytes 1000000 | tf_op jit(solution)/shard_map/place/pallas_call | solution.py:345
  12.2 1.9 %all-to-all-done.got = bf16[8,72,128]{2,1,0:T(8,128)(2,1)S(1)} async-done(((bf16[8,72,128]{2,1,0:T(8,128)(2,1)}), bf16[8,72,128]{2,1,0:T(8,128)(2,1)S(1)}, u32[]{:S(2)}, u32[]{:S(2)}) %all-to-all-start) | async-done | bytes 147488 | tf_op jit(solution)/shard_map/all_to_all | solution.py:325
  14.2 1.6 %shade.1.refs_3_ = bf16[72,128]{1,0:T(8,128)(2,1)S(1)} custom-call(s32[3,16,128]{2,1,0:T(8,128)S(1)} %get-tuple-element.11.rows, bf16[8,128]{1,0:T(8,128)(2,1)S(1)} %get-tuple-element.12.codes, bf16[8,72,128]{2,1,0:T(8,128)(2,1)S(1)} %all-to-all-done.got, bf16[4,256,256]{2,1,0:T(8,128)(2,1)S(1)} %get-tuple-element.13.w_first, ...), custom_call_target="tpu_custom_call" | custom-call | tf_op jit(solution)/shard_map/shade/pallas_call | solution.py:371
  15.7 0.0 collective-permute-start.2
  15.7 1.6 %collective-permute-start.1 = (bf16[72,128]{1,0:T(8,128)(2,1)S(1)}, bf16[72,128]{1,0:T(8,128)(2,1)S(1)}, u32[]{:S(2)}, u32[]{:S(2)}) collective-permute-start(bf16[72,128]{1,0:T(8,128)(2,1)S(1)} %shade.1.refs_3_), channel_id=1, source_target_pairs={{0,2},{1,3},{2,0},{3,1},{4,6},{5,7},{6,4},{7,5},{8,10},{9,11},{10,... | collective-permute-start | bytes 55304 | tf_op jit(solution)/shard_map/ppermute | solution.py:385
  17.3 0.3 %collective-permute-start = (bf16[72,128]{1,0:T(8,128)(2,1)S(1)}, bf16[72,128]{1,0:T(8,128)(2,1)S(1)}, u32[]{:S(2)}, u32[]{:S(2)}) collective-permute-start(bf16[72,128]{1,0:T(8,128)(2,1)S(1)} %shade.1.refs_3_), channel_id=1, source_target_pairs={{0,1},{1,0},{2,3},{3,2},{4,5},{5,4},{6,7},{7,6},{8,9},{9,8},{10,11... | collective-permute-start | bytes 55304 | tf_op jit(solution)/shard_map/ppermute | solution.py:385
  17.6 0.4 %empty.1.refs_4_ = f32[8,128]{1,0:T(8,128)S(1)} custom-call(bf16[1,256]{1,0:T(2,128)(2,1)S(1)} %broadcast_in_dim.3.trans_weight, bf16[2,256,256]{2,1,0:T(8,128)(2,1)S(1)} %get-tuple-element.14.w_mid, bf16[4,256]{1,0:T(4,128)(2,1)S(1)} %get-tuple-element.15.w_out), custom_call_target="tpu_custom_call" | custom-call | flops 100000 | bytes 1000000 | tf_op jit(solution)/shard_map/empty/pallas_call | solution.py:362
  18.1 1.0 %collective-permute-done.2.refs_2_ = bf16[72,128]{1,0:T(8,128)(2,1)S(1)} collective-permute-done((bf16[72,128]{1,0:T(8,128)(2,1)S(1)}, bf16[72,128]{1,0:T(8,128)(2,1)S(1)}, u32[]{:S(2)}, u32[]{:S(2)}) %collective-permute-start.2) | collective-permute-done | bytes 18464 | tf_op jit(solution)/shard_map/ppermute | solution.py:385
  19.1 0.5 %collective-permute-done.1.refs_1_ = bf16[72,128]{1,0:T(8,128)(2,1)S(1)} collective-permute-done((bf16[72,128]{1,0:T(8,128)(2,1)S(1)}, bf16[72,128]{1,0:T(8,128)(2,1)S(1)}, u32[]{:S(2)}, u32[]{:S(2)}) %collective-permute-start.1) | collective-permute-done | bytes 18464 | tf_op jit(solution)/shard_map/ppermute | solution.py:385
  19.6 0.0 collective-permute-done.refs_0_
  19.6 0.9 %join.1 = bf16[1,4,32,4,128]{4,3,2,1,0:T(4,128)(2,1)} custom-call(bf16[72,128]{1,0:T(8,128)(2,1)S(1)} %collective-permute-done.refs_0_, bf16[72,128]{1,0:T(8,128)(2,1)S(1)} %collective-permute-done.1.refs_1_, bf16[72,128]{1,0:T(8,128)(2,1)S(1)} %collective-permute-done.2.refs_2_, bf16[72,128]{1,0:T(8,128)(2,1)S(1)} %shade.1.refs_3_, ...), custom_call_target="tpu_custom_call" | custom-call | tf_op jit(solution)/shard_map/join/pallas_call | solution.py:388
  (1 shorter events, 0.0 us)
Async XLA Ops:
  1.6 8.5 %copy-start = (s32[1,8,8]{2,1,0:T(8,128)S(1)}, s32[1,8,8]{2,1,0:T(8,128)}, u32[]{:S(2)}) copy-start(s32[1,8,8]{2,1,0:T(8,128)} %far_counts.1) | copy-start | bytes 772
  1.6 8.5 %copy-start.2 = (s32[1,8,16]{2,1,0:T(8,128)S(1)}, s32[1,8,16]{2,1,0:T(8,128)}, u32[]{:S(2)}) copy-start(s32[1,8,16]{2,1,0:T(8,128)} %refs_1_.1) | copy-start | bytes 1540
  1.7 8.5 %copy-start.3 = (s32[1,1024]{1,0:T(1,128)S(1)}, s32[1,1024]{1,0:T(1,128)}, u32[]{:S(2)}) copy-start(s32[1,1024]{1,0:T(1,128)} %refs_2_.1) | copy-start | bytes 12292
  1.7 8.5 %copy-start.5 = (s32[8]{0:T(128)S(1)}, s32[8]{0:T(128)}, u32[]{:S(2)}) copy-start(s32[8]{0:T(128)} %refs_3_.1) | copy-start | bytes 100
  1.7 9.4 %copy-start.6 = (bf16[256]{0:T(256)(128)(2,1)S(1)}, bf16[256]{0:T(256)(128)(2,1)}, u32[]{:S(2)}) copy-start(bf16[256]{0:T(256)(128)(2,1)} %param.17) | copy-start | bytes 1540
  1.7 9.4 %copy-start.4 = (bf16[4,256]{1,0:T(4,128)(2,1)S(1)}, bf16[4,256]{1,0:T(4,128)(2,1)}, u32[]{:S(2)}) copy-start(bf16[4,256]{1,0:T(4,128)(2,1)} %far_out.1) | copy-start | bytes 6148
  1.7 12.5 %all-to-all-start = ((bf16[8,72,128]{2,1,0:T(8,128)(2,1)}), bf16[8,72,128]{2,1,0:T(8,128)(2,1)S(1)}, u32[]{:S(2)}, u32[]{:S(2)}) async-start(bf16[8,72,128]{2,1,0:T(8,128)(2,1)} %pack.1), calls=%async_computation | async-start | bytes 294912 | tf_op jit(solution)/shard_map/all_to_all | solution.py:325
  10.1 1.0 %copy-start.1 = (bf16[256,32]{0,1:T(8,128)(2,1)S(1)}, bf16[256,32]{0,1:T(8,128)(2,1)}, u32[]{:S(2)}) copy-start(bf16[256,32]{0,1:T(8,128)(2,1)} %param.16) | copy-start | bytes 49156
  15.7 3.3 %collective-permute-start.2 = (bf16[72,128]{1,0:T(8,128)(2,1)S(1)}, bf16[72,128]{1,0:T(8,128)(2,1)S(1)}, u32[]{:S(2)}, u32[]{:S(2)}) collective-permute-start(bf16[72,128]{1,0:T(8,128)(2,1)S(1)} %shade.1.refs_3_), channel_id=1, source_target_pairs={{0,3},{1,2},{2,1},{3,0},{4,7},{5,6},{6,5},{7,4},{8,11},{9,10},{10,... | collective-permute-start | bytes 55304 | tf_op jit(solution)/shard_map/ppermute | solution.py:385
  15.7 3.8 %collective-permute-start.1 = (bf16[72,128]{1,0:T(8,128)(2,1)S(1)}, bf16[72,128]{1,0:T(8,128)(2,1)S(1)}, u32[]{:S(2)}, u32[]{:S(2)}) collective-permute-start(bf16[72,128]{1,0:T(8,128)(2,1)S(1)} %shade.1.refs_3_), channel_id=1, source_target_pairs={{0,2},{1,3},{2,0},{3,1},{4,6},{5,7},{6,4},{7,5},{8,10},{9,11},{10,... | collective-permute-start | bytes 55304 | tf_op jit(solution)/shard_map/ppermute | solution.py:385
  17.3 2.3 %collective-permute-start = (bf16[72,128]{1,0:T(8,128)(2,1)S(1)}, bf16[72,128]{1,0:T(8,128)(2,1)S(1)}, u32[]{:S(2)}, u32[]{:S(2)}) collective-permute-start(bf16[72,128]{1,0:T(8,128)(2,1)S(1)} %shade.1.refs_3_), channel_id=1, source_target_pairs={{0,1},{1,0},{2,3},{3,2},{4,5},{5,4},{6,7},{7,6},{8,9},{9,8},{10,11... | collective-permute-start | bytes 55304 | tf_op jit(solution)/shard_map/ppermute | solution.py:385

commit v10 on v9

--- a/solution.py
+++ b/solution.py
@@ -90,7 +90,9 @@
 
 def exchange_order(n_slab):
     half = n_slab // 2
-    return [s for i in range(half) for s in (half + (i + 1) % half, i)]
+    back = [half] + list(range(n_slab - 1, half, -1))
+    front = list(range(half - 2)) + [half - 1, half - 2] if half > 1 else [0]
+    return [s for pair in zip(back, front) for s in pair]
 
 
 def pack_kernel(far_counts, far_colors, far_transmit, sends, counts, colors, transmit, tall, sems):

time: 20.7 us -> 20.5 us (level)
  starting transfers between devices: 10.3 us -> 9.86 us
  waiting for transfers between devices: 3.46 us -> 3.7 us
    all_to_all x1, starting transfers between devices: 8.41 us -> 7.98 us  [compact_device(): lax.all_to_all(sends, 'slab', split_axis=0, concat_axis=0, axis_index_gro...]
    all_to_all x1, waiting for transfers between devices: 1.93 us -> 2.17 us  [compact_device(): lax.all_to_all(sends, 'slab', split_axis=0, concat_axis=0, axis_index_gro...]
where the time goes in v10:
time: 20.5 us; the launch traced here: 20.3 us
  starting transfers between devices  9.86 us (48%)
  Pallas kernels  6.5 us (32%)
  waiting for transfers between devices  3.7 us (18%)
    all_to_all x1, starting transfers between devices, compact_device(): lax.all_to_all(sends, 'slab', split_axis=0, concat_axis=0, axis_index_gro...  7.98 us
    all_to_all x1, waiting for transfers between devices, compact_device(): lax.all_to_all(sends, 'slab', split_axis=0, concat_axis=0, axis_index_gro...  2.17 us
    ppermute x3, starting transfers between devices, compact_device(): lax.ppermute(shaded, 'strip', [(s, s ^ k) for s in range(n_strip)])  1.88 us
    pallas_call x1, Pallas kernels, compact_device(): pl.pallas_call(pack_kernel, out_shape=jax.ShapeDtypeStruct((n_slab, messa...  1.62 us
    pallas_call x1, Pallas kernels, compact_device(): pl.pallas_call(shade_kernel, out_shape=jax.ShapeDtypeStruct((items * outs...  1.55 us
    ppermute x3, waiting for transfers between devices, compact_device(): lax.ppermute(shaded, 'strip', [(s, s ^ k) for s in range(n_strip)])  1.53 us
    pallas_call x1, Pallas kernels, compact_device(): pl.pallas_call(place_kernel, out_shape=[jax.ShapeDtypeStruct((GROUP, 2 *...  1.1 us
    pallas_call x1, Pallas kernels, compact_device(): pl.pallas_call(functools.partial(plan_kernel, n_slab, slots), out_shape=[...  0.94 us
  transfers between devices with their start and end apart: 4, of which 3 were waited for; matrix products, arithmetic and copies ran while one was open for 0% of the time, Pallas kernels for 12%

profile of v10, /device:TPU:0, one launch (start us, length us, event | category | flops | bytes accessed | tf_op | source)
XLA Modules:
  0.0 20.3 jit_solution(13194900369372578121)
XLA Ops:
  0.0 1.6 %pack.1 = bf16[8,72,128]{2,1,0:T(8,128)(2,1)} custom-call(s32[1,8,8]{2,1,0:T(8,128)} %far_counts.1, bf16[1,1,16,32,128]{4,3,2,1,0:T(8,128)(2,1)} %far_colors.1, bf16[1,1,16,128]{3,2,1,0:T(8,128)(2,1)} %far_transmit.1), custom_call_target="tpu_custom_call" | custom-call | tf_op jit(solution)/shard_map/pack/pallas_call | solution.py:311
  1.6 0.0 copy-start
  1.6 0.0 copy-start.2
  1.7 0.0 copy-start.3
  1.7 0.0 copy-start.5
  1.7 0.0 copy-start.6
  1.7 0.0 copy-start.4
  1.7 8.0 %all-to-all-start = ((bf16[8,72,128]{2,1,0:T(8,128)(2,1)}), bf16[8,72,128]{2,1,0:T(8,128)(2,1)S(1)}, u32[]{:S(2)}, u32[]{:S(2)}) async-start(bf16[8,72,128]{2,1,0:T(8,128)(2,1)} %pack.1), calls=%async_computation | async-start | bytes 294912 | tf_op jit(solution)/shard_map/all_to_all | solution.py:327
  9.7 0.0 copy-done
  9.7 0.0 copy-done.2
  9.7 0.0 copy-done.3
  9.7 0.0 copy-done.5
  9.7 0.0 copy-start.1
  9.7 0.9 %plan.1 = (s32[3,16,128]{2,1,0:T(8,128)S(1)}, bf16[8,128]{1,0:T(8,128)(2,1)S(1)}, s32[8,128]{1,0:T(8,128)S(1)}) custom-call(s32[1,8,8]{2,1,0:T(8,128)S(1)} %copy-done, s32[1,8,16]{2,1,0:T(8,128)S(1)} %copy-done.2, s32[1,1024]{1,0:T(1,128)S(1)} %copy-done.3, s32[8]{0:T(128)S(1)} %copy-done.5), custom_call_target="tpu_custom_call" | custom-call | flops 100000 | bytes 1000000 | tf_op jit(solution)/shard_map/plan/pallas_call | solution.py:334
  10.7 0.0 copy-done.6
  10.7 0.0 copy-done.4
  10.7 0.0 copy-done.1
  10.7 1.1 %place.1 = (bf16[4,256,256]{2,1,0:T(8,128)(2,1)S(1)}, bf16[4,256]{1,0:T(4,128)(2,1)S(1)}, bf16[2,256,256]{2,1,0:T(8,128)(2,1)S(1)}) custom-call(bf16[32,256]{1,0:T(8,128)(2,1)S(1)} %bitcast.1, bf16[1,256]{1,0:T(2,128)(2,1)S(1)} %broadcast_in_dim.3.trans_weight, bf16[4,256]{1,0:T(4,128)(2,1)S(1)} %copy-done.4, bf16[2,256,256]{2,1,0:T(8,128)(2,1)} %far_mid.1), custom_call_target="tpu_custom_call" | custom-call | flops 100000 | bytes 1000000 | tf_op jit(solution)/shard_map/place/pallas_call | solution.py:347
  11.8 2.2 %all-to-all-done.got = bf16[8,72,128]{2,1,0:T(8,128)(2,1)S(1)} async-done(((bf16[8,72,128]{2,1,0:T(8,128)(2,1)}), bf16[8,72,128]{2,1,0:T(8,128)(2,1)S(1)}, u32[]{:S(2)}, u32[]{:S(2)}) %all-to-all-start) | async-done | bytes 147488 | tf_op jit(solution)/shard_map/all_to_all | solution.py:327
  14.0 1.6 %shade.1.refs_3_ = bf16[72,128]{1,0:T(8,128)(2,1)S(1)} custom-call(s32[3,16,128]{2,1,0:T(8,128)S(1)} %get-tuple-element.11.rows, bf16[8,128]{1,0:T(8,128)(2,1)S(1)} %get-tuple-element.12.codes, bf16[8,72,128]{2,1,0:T(8,128)(2,1)S(1)} %all-to-all-done.got, bf16[4,256,256]{2,1,0:T(8,128)(2,1)S(1)} %get-tuple-element.13.w_first, ...), custom_call_target="tpu_custom_call" | custom-call | tf_op jit(solution)/shard_map/shade/pallas_call | solution.py:373
  15.5 0.0 collective-permute-start.2
  15.6 1.6 %collective-permute-start.1 = (bf16[72,128]{1,0:T(8,128)(2,1)S(1)}, bf16[72,128]{1,0:T(8,128)(2,1)S(1)}, u32[]{:S(2)}, u32[]{:S(2)}) collective-permute-start(bf16[72,128]{1,0:T(8,128)(2,1)S(1)} %shade.1.refs_3_), channel_id=1, source_target_pairs={{0,2},{1,3},{2,0},{3,1},{4,6},{5,7},{6,4},{7,5},{8,10},{9,11},{10,... | collective-permute-start | bytes 55304 | tf_op jit(solution)/shard_map/ppermute | solution.py:387
  17.1 0.3 %collective-permute-start = (bf16[72,128]{1,0:T(8,128)(2,1)S(1)}, bf16[72,128]{1,0:T(8,128)(2,1)S(1)}, u32[]{:S(2)}, u32[]{:S(2)}) collective-permute-start(bf16[72,128]{1,0:T(8,128)(2,1)S(1)} %shade.1.refs_3_), channel_id=1, source_target_pairs={{0,1},{1,0},{2,3},{3,2},{4,5},{5,4},{6,7},{7,6},{8,9},{9,8},{10,11... | collective-permute-start | bytes 55304 | tf_op jit(solution)/shard_map/ppermute | solution.py:387
  17.4 0.4 %empty.1.refs_4_ = f32[8,128]{1,0:T(8,128)S(1)} custom-call(bf16[1,256]{1,0:T(2,128)(2,1)S(1)} %broadcast_in_dim.3.trans_weight, bf16[2,256,256]{2,1,0:T(8,128)(2,1)S(1)} %get-tuple-element.14.w_mid, bf16[4,256]{1,0:T(4,128)(2,1)S(1)} %get-tuple-element.15.w_out), custom_call_target="tpu_custom_call" | custom-call | flops 100000 | bytes 1000000 | tf_op jit(solution)/shard_map/empty/pallas_call | solution.py:364
  17.9 1.0 %collective-permute-done.2.refs_2_ = bf16[72,128]{1,0:T(8,128)(2,1)S(1)} collective-permute-done((bf16[72,128]{1,0:T(8,128)(2,1)S(1)}, bf16[72,128]{1,0:T(8,128)(2,1)S(1)}, u32[]{:S(2)}, u32[]{:S(2)}) %collective-permute-start.2) | collective-permute-done | bytes 18464 | tf_op jit(solution)/shard_map/ppermute | solution.py:387
  18.9 0.5 %collective-permute-done.1.refs_1_ = bf16[72,128]{1,0:T(8,128)(2,1)S(1)} collective-permute-done((bf16[72,128]{1,0:T(8,128)(2,1)S(1)}, bf16[72,128]{1,0:T(8,128)(2,1)S(1)}, u32[]{:S(2)}, u32[]{:S(2)}) %collective-permute-start.1) | collective-permute-done | bytes 18464 | tf_op jit(solution)/shard_map/ppermute | solution.py:387
  19.4 0.0 collective-permute-done.refs_0_
  19.4 0.9 %join.1 = bf16[1,4,32,4,128]{4,3,2,1,0:T(4,128)(2,1)} custom-call(bf16[72,128]{1,0:T(8,128)(2,1)S(1)} %collective-permute-done.refs_0_, bf16[72,128]{1,0:T(8,128)(2,1)S(1)} %collective-permute-done.1.refs_1_, bf16[72,128]{1,0:T(8,128)(2,1)S(1)} %collective-permute-done.2.refs_2_, bf16[72,128]{1,0:T(8,128)(2,1)S(1)} %shade.1.refs_3_, ...), custom_call_target="tpu_custom_call" | custom-call | tf_op jit(solution)/shard_map/join/pallas_call | solution.py:390
  (1 shorter events, 0.0 us)
Async XLA Ops:
  1.6 8.1 %copy-start = (s32[1,8,8]{2,1,0:T(8,128)S(1)}, s32[1,8,8]{2,1,0:T(8,128)}, u32[]{:S(2)}) copy-start(s32[1,8,8]{2,1,0:T(8,128)} %far_counts.1) | copy-start | bytes 772
  1.6 8.0 %copy-start.2 = (s32[1,8,16]{2,1,0:T(8,128)S(1)}, s32[1,8,16]{2,1,0:T(8,128)}, u32[]{:S(2)}) copy-start(s32[1,8,16]{2,1,0:T(8,128)} %refs_1_.1) | copy-start | bytes 1540
  1.7 8.0 %copy-start.3 = (s32[1,1024]{1,0:T(1,128)S(1)}, s32[1,1024]{1,0:T(1,128)}, u32[]{:S(2)}) copy-start(s32[1,1024]{1,0:T(1,128)} %refs_2_.1) | copy-start | bytes 12292
  1.7 8.0 %copy-start.5 = (s32[8]{0:T(128)S(1)}, s32[8]{0:T(128)}, u32[]{:S(2)}) copy-start(s32[8]{0:T(128)} %refs_3_.1) | copy-start | bytes 100
  1.7 9.0 %copy-start.6 = (bf16[256]{0:T(256)(128)(2,1)S(1)}, bf16[256]{0:T(256)(128)(2,1)}, u32[]{:S(2)}) copy-start(bf16[256]{0:T(256)(128)(2,1)} %param.17) | copy-start | bytes 1540
  1.7 9.0 %copy-start.4 = (bf16[4,256]{1,0:T(4,128)(2,1)S(1)}, bf16[4,256]{1,0:T(4,128)(2,1)}, u32[]{:S(2)}) copy-start(bf16[4,256]{1,0:T(4,128)(2,1)} %far_out.1) | copy-start | bytes 6148
  1.7 12.3 %all-to-all-start = ((bf16[8,72,128]{2,1,0:T(8,128)(2,1)}), bf16[8,72,128]{2,1,0:T(8,128)(2,1)S(1)}, u32[]{:S(2)}, u32[]{:S(2)}) async-start(bf16[8,72,128]{2,1,0:T(8,128)(2,1)} %pack.1), calls=%async_computation | async-start | bytes 294912 | tf_op jit(solution)/shard_map/all_to_all | solution.py:327
  9.7 1.0 %copy-start.1 = (bf16[256,32]{0,1:T(8,128)(2,1)S(1)}, bf16[256,32]{0,1:T(8,128)(2,1)}, u32[]{:S(2)}) copy-start(bf16[256,32]{0,1:T(8,128)(2,1)} %param.16) | copy-start | bytes 49156
  15.5 3.4 %collective-permute-start.2 = (bf16[72,128]{1,0:T(8,128)(2,1)S(1)}, bf16[72,128]{1,0:T(8,128)(2,1)S(1)}, u32[]{:S(2)}, u32[]{:S(2)}) collective-permute-start(bf16[72,128]{1,0:T(8,128)(2,1)S(1)} %shade.1.refs_3_), channel_id=1, source_target_pairs={{0,3},{1,2},{2,1},{3,0},{4,7},{5,6},{6,5},{7,4},{8,11},{9,10},{10,... | collective-permute-start | bytes 55304 | tf_op jit(solution)/shard_map/ppermute | solution.py:387
  15.6 3.8 %collective-permute-start.1 = (bf16[72,128]{1,0:T(8,128)(2,1)S(1)}, bf16[72,128]{1,0:T(8,128)(2,1)S(1)}, u32[]{:S(2)}, u32[]{:S(2)}) collective-permute-start(bf16[72,128]{1,0:T(8,128)(2,1)S(1)} %shade.1.refs_3_), channel_id=1, source_target_pairs={{0,2},{1,3},{2,0},{3,1},{4,6},{5,7},{6,4},{7,5},{8,10},{9,11},{10,... | collective-permute-start | bytes 55304 | tf_op jit(solution)/shard_map/ppermute | solution.py:387
  17.1 2.3 %collective-permute-start = (bf16[72,128]{1,0:T(8,128)(2,1)S(1)}, bf16[72,128]{1,0:T(8,128)(2,1)S(1)}, u32[]{:S(2)}, u32[]{:S(2)}) collective-permute-start(bf16[72,128]{1,0:T(8,128)(2,1)S(1)} %shade.1.refs_3_), channel_id=1, source_target_pairs={{0,1},{1,0},{2,3},{3,2},{4,5},{5,4},{6,7},{7,6},{8,9},{9,8},{10,11... | collective-permute-start | bytes 55304 | tf_op jit(solution)/shard_map/ppermute | solution.py:387

commit v11 on v10

--- a/solution.py
+++ b/solution.py
@@ -216,17 +216,23 @@
             same = posv == posv[j : j + 1, :]
             total = jnp.where(same, total * trans_j, total)
             front = jnp.where(same & (depthv > depthv[j : j + 1, :]), front * trans_j, front)
-    acc[...] = jnp.zeros_like(acc)
-    for j in range(items):
-        k, r = divmod(j, MOST)
-        color = got[k, pl.ds(r * feats, feats), :].astype(jnp.float32)
-        at = rows[2, j, 0]
-        acc[at] = acc[at] + front[j : j + 1, :] * color
+    acc[pl.ds(MOST, items - MOST)] = jnp.zeros((items - MOST, feats, span), jnp.float32)
+    for k in range(items // MOST):
+        places = [k * MOST + r if k == 0 else rows[2, k * MOST + r, 0] for r in range(MOST)]
+        sums = []
+        for r in range(MOST):
+            j = k * MOST + r
+            color = got[k, pl.ds(r * feats, feats), :].astype(jnp.float32)
+            share = front[j : j + 1, :] * color
+            sums.append(share if k == 0 else acc[places[r]] + share)
+        for r in range(MOST):
+            acc[places[r]] = sums[r]
     total_hi = total.astype(jnp.bfloat16).astype(jnp.float32)
     total_lo = total - total_hi
     groups = items // GROUP
     sub = lax.broadcasted_iota(jnp.int32, (16, span), 0)
-    xt[...] = jnp.zeros_like(xt)
+    used = GROUP * feats
+    xt[:, pl.ds(used, used)] = jnp.zeros((xt.shape[0], used), jnp.bfloat16)
     for q in range(groups):
         block = acc[pl.ds(q * GROUP, GROUP)].reshape(GROUP * feats, span)
         tail = jnp.zeros((16, span), jnp.float32)

time: 20.5 us -> 20.5 us (level)
  no operation moved by 1% of the time
where the time goes in v11:
time: 20.5 us; the launch traced here: 20.2 us
  starting transfers between devices  9.86 us (48%)
  Pallas kernels  6.48 us (32%)
  waiting for transfers between devices  3.7 us (18%)
    all_to_all x1, starting transfers between devices, compact_device(): lax.all_to_all(sends, 'slab', split_axis=0, concat_axis=0, axis_index_gro...  7.98 us
    all_to_all x1, waiting for transfers between devices, compact_device(): lax.all_to_all(sends, 'slab', split_axis=0, concat_axis=0, axis_index_gro...  2.17 us
    ppermute x3, starting transfers between devices, compact_device(): lax.ppermute(shaded, 'strip', [(s, s ^ k) for s in range(n_strip)])  1.88 us
    pallas_call x1, Pallas kernels, compact_device(): pl.pallas_call(pack_kernel, out_shape=jax.ShapeDtypeStruct((n_slab, messa...  1.62 us
    ppermute x3, waiting for transfers between devices, compact_device(): lax.ppermute(shaded, 'strip', [(s, s ^ k) for s in range(n_strip)])  1.53 us
    pallas_call x1, Pallas kernels, compact_device(): pl.pallas_call(shade_kernel, out_shape=jax.ShapeDtypeStruct((items * outs...  1.53 us
    pallas_call x1, Pallas kernels, compact_device(): pl.pallas_call(place_kernel, out_shape=[jax.ShapeDtypeStruct((GROUP, 2 *...  1.1 us
    pallas_call x1, Pallas kernels, compact_device(): pl.pallas_call(functools.partial(plan_kernel, n_slab, slots), out_shape=[...  0.94 us
  transfers between devices with their start and end apart: 4, of which 3 were waited for; matrix products, arithmetic and copies ran while one was open for 0% of the time, Pallas kernels for 12%

profile of v11, /device:TPU:0, one launch (start us, length us, event | category | flops | bytes accessed | tf_op | source)
XLA Modules:
  0.0 20.2 jit_solution(14977021057865695104)
XLA Ops:
  0.0 1.6 %pack.1 = bf16[8,72,128]{2,1,0:T(8,128)(2,1)} custom-call(s32[1,8,8]{2,1,0:T(8,128)} %far_counts.1, bf16[1,1,16,32,128]{4,3,2,1,0:T(8,128)(2,1)} %far_colors.1, bf16[1,1,16,128]{3,2,1,0:T(8,128)(2,1)} %far_transmit.1), custom_call_target="tpu_custom_call" | custom-call | tf_op jit(solution)/shard_map/pack/pallas_call | solution.py:317
  1.6 0.0 copy-start
  1.6 0.0 copy-start.2
  1.7 0.0 copy-start.3
  1.7 0.0 copy-start.5
  1.7 0.0 copy-start.6
  1.7 0.0 copy-start.4
  1.7 8.0 %all-to-all-start = ((bf16[8,72,128]{2,1,0:T(8,128)(2,1)}), bf16[8,72,128]{2,1,0:T(8,128)(2,1)S(1)}, u32[]{:S(2)}, u32[]{:S(2)}) async-start(bf16[8,72,128]{2,1,0:T(8,128)(2,1)} %pack.1), calls=%async_computation | async-start | bytes 294912 | tf_op jit(solution)/shard_map/all_to_all | solution.py:333
  9.7 0.0 copy-done
  9.7 0.0 copy-done.2
  9.7 0.0 copy-done.3
  9.7 0.0 copy-done.5
  9.7 0.0 copy-start.1
  9.7 0.9 %plan.1 = (s32[3,16,128]{2,1,0:T(8,128)S(1)}, bf16[8,128]{1,0:T(8,128)(2,1)S(1)}, s32[8,128]{1,0:T(8,128)S(1)}) custom-call(s32[1,8,8]{2,1,0:T(8,128)S(1)} %copy-done, s32[1,8,16]{2,1,0:T(8,128)S(1)} %copy-done.2, s32[1,1024]{1,0:T(1,128)S(1)} %copy-done.3, s32[8]{0:T(128)S(1)} %copy-done.5), custom_call_target="tpu_custom_call" | custom-call | flops 100000 | bytes 1000000 | tf_op jit(solution)/shard_map/plan/pallas_call | solution.py:340
  10.7 0.0 copy-done.6
  10.7 0.0 copy-done.4
  10.7 0.0 copy-done.1
  10.7 1.1 %place.1 = (bf16[4,256,256]{2,1,0:T(8,128)(2,1)S(1)}, bf16[4,256]{1,0:T(4,128)(2,1)S(1)}, bf16[2,256,256]{2,1,0:T(8,128)(2,1)S(1)}) custom-call(bf16[32,256]{1,0:T(8,128)(2,1)S(1)} %bitcast.1, bf16[1,256]{1,0:T(2,128)(2,1)S(1)} %broadcast_in_dim.3.trans_weight, bf16[4,256]{1,0:T(4,128)(2,1)S(1)} %copy-done.4, bf16[2,256,256]{2,1,0:T(8,128)(2,1)} %far_mid.1), custom_call_target="tpu_custom_call" | custom-call | flops 100000 | bytes 1000000 | tf_op jit(solution)/shard_map/place/pallas_call | solution.py:353
  11.8 2.2 %all-to-all-done.got = bf16[8,72,128]{2,1,0:T(8,128)(2,1)S(1)} async-done(((bf16[8,72,128]{2,1,0:T(8,128)(2,1)}), bf16[8,72,128]{2,1,0:T(8,128)(2,1)S(1)}, u32[]{:S(2)}, u32[]{:S(2)}) %all-to-all-start) | async-done | bytes 147488 | tf_op jit(solution)/shard_map/all_to_all | solution.py:333
  14.0 1.5 %shade.1.refs_3_ = bf16[72,128]{1,0:T(8,128)(2,1)S(1)} custom-call(s32[3,16,128]{2,1,0:T(8,128)S(1)} %get-tuple-element.11.rows, bf16[8,128]{1,0:T(8,128)(2,1)S(1)} %get-tuple-element.12.codes, bf16[8,72,128]{2,1,0:T(8,128)(2,1)S(1)} %all-to-all-done.got, bf16[4,256,256]{2,1,0:T(8,128)(2,1)S(1)} %get-tuple-element.13.w_first, ...), custom_call_target="tpu_custom_call" | custom-call | tf_op jit(solution)/shard_map/shade/pallas_call | solution.py:379
  15.5 0.0 collective-permute-start.2
  15.5 1.6 %collective-permute-start.1 = (bf16[72,128]{1,0:T(8,128)(2,1)S(1)}, bf16[72,128]{1,0:T(8,128)(2,1)S(1)}, u32[]{:S(2)}, u32[]{:S(2)}) collective-permute-start(bf16[72,128]{1,0:T(8,128)(2,1)S(1)} %shade.1.refs_3_), channel_id=1, source_target_pairs={{0,2},{1,3},{2,0},{3,1},{4,6},{5,7},{6,4},{7,5},{8,10},{9,11},{10,... | collective-permute-start | bytes 55304 | tf_op jit(solution)/shard_map/ppermute | solution.py:393
  17.1 0.3 %collective-permute-start = (bf16[72,128]{1,0:T(8,128)(2,1)S(1)}, bf16[72,128]{1,0:T(8,128)(2,1)S(1)}, u32[]{:S(2)}, u32[]{:S(2)}) collective-permute-start(bf16[72,128]{1,0:T(8,128)(2,1)S(1)} %shade.1.refs_3_), channel_id=1, source_target_pairs={{0,1},{1,0},{2,3},{3,2},{4,5},{5,4},{6,7},{7,6},{8,9},{9,8},{10,11... | collective-permute-start | bytes 55304 | tf_op jit(solution)/shard_map/ppermute | solution.py:393
  17.4 0.4 %empty.1.refs_4_ = f32[8,128]{1,0:T(8,128)S(1)} custom-call(bf16[1,256]{1,0:T(2,128)(2,1)S(1)} %broadcast_in_dim.3.trans_weight, bf16[2,256,256]{2,1,0:T(8,128)(2,1)S(1)} %get-tuple-element.14.w_mid, bf16[4,256]{1,0:T(4,128)(2,1)S(1)} %get-tuple-element.15.w_out), custom_call_target="tpu_custom_call" | custom-call | flops 100000 | bytes 1000000 | tf_op jit(solution)/shard_map/empty/pallas_call | solution.py:370
  17.8 1.0 %collective-permute-done.2.refs_2_ = bf16[72,128]{1,0:T(8,128)(2,1)S(1)} collective-permute-done((bf16[72,128]{1,0:T(8,128)(2,1)S(1)}, bf16[72,128]{1,0:T(8,128)(2,1)S(1)}, u32[]{:S(2)}, u32[]{:S(2)}) %collective-permute-start.2) | collective-permute-done | bytes 18464 | tf_op jit(solution)/shard_map/ppermute | solution.py:393
  18.9 0.5 %collective-permute-done.1.refs_1_ = bf16[72,128]{1,0:T(8,128)(2,1)S(1)} collective-permute-done((bf16[72,128]{1,0:T(8,128)(2,1)S(1)}, bf16[72,128]{1,0:T(8,128)(2,1)S(1)}, u32[]{:S(2)}, u32[]{:S(2)}) %collective-permute-start.1) | collective-permute-done | bytes 18464 | tf_op jit(solution)/shard_map/ppermute | solution.py:393
  19.4 0.0 collective-permute-done.refs_0_
  19.4 0.9 %join.1 = bf16[1,4,32,4,128]{4,3,2,1,0:T(4,128)(2,1)} custom-call(bf16[72,128]{1,0:T(8,128)(2,1)S(1)} %collective-permute-done.refs_0_, bf16[72,128]{1,0:T(8,128)(2,1)S(1)} %collective-permute-done.1.refs_1_, bf16[72,128]{1,0:T(8,128)(2,1)S(1)} %collective-permute-done.2.refs_2_, bf16[72,128]{1,0:T(8,128)(2,1)S(1)} %shade.1.refs_3_, ...), custom_call_target="tpu_custom_call" | custom-call | tf_op jit(solution)/shard_map/join/pallas_call | solution.py:396
  (1 shorter events, 0.0 us)
Async XLA Ops:
  1.6 8.1 %copy-start = (s32[1,8,8]{2,1,0:T(8,128)S(1)}, s32[1,8,8]{2,1,0:T(8,128)}, u32[]{:S(2)}) copy-start(s32[1,8,8]{2,1,0:T(8,128)} %far_counts.1) | copy-start | bytes 772
  1.6 8.0 %copy-start.2 = (s32[1,8,16]{2,1,0:T(8,128)S(1)}, s32[1,8,16]{2,1,0:T(8,128)}, u32[]{:S(2)}) copy-start(s32[1,8,16]{2,1,0:T(8,128)} %refs_1_.1) | copy-start | bytes 1540
  1.7 8.0 %copy-start.3 = (s32[1,1024]{1,0:T(1,128)S(1)}, s32[1,1024]{1,0:T(1,128)}, u32[]{:S(2)}) copy-start(s32[1,1024]{1,0:T(1,128)} %refs_2_.1) | copy-start | bytes 12292
  1.7 8.0 %copy-start.5 = (s32[8]{0:T(128)S(1)}, s32[8]{0:T(128)}, u32[]{:S(2)}) copy-start(s32[8]{0:T(128)} %refs_3_.1) | copy-start | bytes 100
  1.7 9.0 %copy-start.6 = (bf16[256]{0:T(256)(128)(2,1)S(1)}, bf16[256]{0:T(256)(128)(2,1)}, u32[]{:S(2)}) copy-start(bf16[256]{0:T(256)(128)(2,1)} %param.17) | copy-start | bytes 1540
  1.7 9.0 %copy-start.4 = (bf16[4,256]{1,0:T(4,128)(2,1)S(1)}, bf16[4,256]{1,0:T(4,128)(2,1)}, u32[]{:S(2)}) copy-start(bf16[4,256]{1,0:T(4,128)(2,1)} %far_out.1) | copy-start | bytes 6148
  1.7 12.3 %all-to-all-start = ((bf16[8,72,128]{2,1,0:T(8,128)(2,1)}), bf16[8,72,128]{2,1,0:T(8,128)(2,1)S(1)}, u32[]{:S(2)}, u32[]{:S(2)}) async-start(bf16[8,72,128]{2,1,0:T(8,128)(2,1)} %pack.1), calls=%async_computation | async-start | bytes 294912 | tf_op jit(solution)/shard_map/all_to_all | solution.py:333
  9.7 1.0 %copy-start.1 = (bf16[256,32]{0,1:T(8,128)(2,1)S(1)}, bf16[256,32]{0,1:T(8,128)(2,1)}, u32[]{:S(2)}) copy-start(bf16[256,32]{0,1:T(8,128)(2,1)} %param.16) | copy-start | bytes 49156
  15.5 3.4 %collective-permute-start.2 = (bf16[72,128]{1,0:T(8,128)(2,1)S(1)}, bf16[72,128]{1,0:T(8,128)(2,1)S(1)}, u32[]{:S(2)}, u32[]{:S(2)}) collective-permute-start(bf16[72,128]{1,0:T(8,128)(2,1)S(1)} %shade.1.refs_3_), channel_id=1, source_target_pairs={{0,3},{1,2},{2,1},{3,0},{4,7},{5,6},{6,5},{7,4},{8,11},{9,10},{10,... | collective-permute-start | bytes 55304 | tf_op jit(solution)/shard_map/ppermute | solution.py:393
  15.5 3.8 %collective-permute-start.1 = (bf16[72,128]{1,0:T(8,128)(2,1)S(1)}, bf16[72,128]{1,0:T(8,128)(2,1)S(1)}, u32[]{:S(2)}, u32[]{:S(2)}) collective-permute-start(bf16[72,128]{1,0:T(8,128)(2,1)S(1)} %shade.1.refs_3_), channel_id=1, source_target_pairs={{0,2},{1,3},{2,0},{3,1},{4,6},{5,7},{6,4},{7,5},{8,10},{9,11},{10,... | collective-permute-start | bytes 55304 | tf_op jit(solution)/shard_map/ppermute | solution.py:393
  17.1 2.3 %collective-permute-start = (bf16[72,128]{1,0:T(8,128)(2,1)S(1)}, bf16[72,128]{1,0:T(8,128)(2,1)S(1)}, u32[]{:S(2)}, u32[]{:S(2)}) collective-permute-start(bf16[72,128]{1,0:T(8,128)(2,1)S(1)} %shade.1.refs_3_), channel_id=1, source_target_pairs={{0,1},{1,0},{2,3},{3,2},{4,5},{5,4},{6,7},{7,6},{8,9},{9,8},{10,11... | collective-permute-start | bytes 55304 | tf_op jit(solution)/shard_map/ppermute | solution.py:393

commit v12 on v11

--- a/solution.py
+++ b/solution.py
@@ -125,7 +125,12 @@
 
 
 def plan_kernel(n_slab, slots, *refs):
-    (counts, blocks, assign, depth), (rows, codes, strip) = refs[:4], refs[4:]
+    far, (rows, codes, strip) = refs[:4], refs[4:7]
+    near, sems = refs[7:11], refs[11]
+    counts, blocks, assign, depth = near
+    copies = [pltpu.make_async_copy(far[i], near[i], sems.at[i]) for i in range(4)]
+    for copy in copies:
+        copy.start()
     strip[...] = jnp.full(strip.shape, lax.axis_index("strip"), jnp.int32)
     items = n_slab * MOST
     outs = codes.shape[1] // (2 * items)
@@ -136,6 +141,8 @@
     depthv = jnp.zeros(rows.shape[1:], jnp.int32)
     firstv = jnp.zeros(rows.shape[1:], jnp.int32)
     codev = jnp.full(codes.shape, -1, jnp.int32)
+    for copy in copies:
+        copy.wait()
     pos = []
     for k, s in enumerate(exchange_order(n_slab)):
         off = jnp.int32(0)
@@ -245,7 +252,7 @@
         xt[lines, pl.ds(GROUP * feats, 16)] = tail.T.astype(jnp.bfloat16)
 
     x = xt[...]
-    stride = GROUP
+    stride = GROUP // 2
     for start in range(0, GROUP, stride):
         h = jnp.concatenate(
             [
@@ -344,12 +351,16 @@
             jax.ShapeDtypeStruct((ROWS, span), jnp.bfloat16),
             jax.ShapeDtypeStruct((ROWS, span), jnp.int32),
         ],
-        in_specs=[smem] * 4,
+        in_specs=[hbm] * 4,
         out_specs=[vmem] * 3,
+        scratch_shapes=[
+            pltpu.SMEM(a.shape, jnp.int32) for a in (pair_counts, slot_block, assign, depth_rank)
+        ]
+        + [pltpu.SemaphoreType.DMA((4,))],
         compiler_params=small,
         cost_estimate=rough,
         name="plan",
-    )(pair_counts, slot_block, assign, depth_rank)
+    )(held(pair_counts), held(slot_block), held(assign), held(depth_rank))
     w_first, w_last, w_later = pl.pallas_call(
         place_kernel,
         out_shape=[

time: 20.5 us -> 20.5 us (level)
  Pallas kernels: 6.48 us -> 6.91 us
  waiting for transfers between devices: 3.7 us -> 3.47 us
    pallas_call x1, Pallas kernels: 0.94 us -> 1.22 us  [compact_device(): pl.pallas_call(functools.partial(plan_kernel, n_slab, slots), out_shape=[...]
    all_to_all x1, waiting for transfers between devices: 2.17 us -> 1.92 us  [compact_device(): lax.all_to_all(sends, 'slab', split_axis=0, concat_axis=0, axis_index_gro...]
  transfers between devices with their start and end apart: 4 -> 4, of which waited for: 3 -> 3; matrix products, arithmetic and copies ran while one was open for 0% -> 0% of each run, Pallas kernels for 12% -> 14%
where the time goes in v12:
time: 20.5 us; the launch traced here: 20.2 us
  starting transfers between devices  9.72 us (47%)
  Pallas kernels  6.91 us (34%)
  waiting for transfers between devices  3.47 us (17%)
    all_to_all x1, starting transfers between devices, compact_device(): lax.all_to_all(sends, 'slab', split_axis=0, concat_axis=0, axis_index_gro...  7.85 us
    all_to_all x1, waiting for transfers between devices, compact_device(): lax.all_to_all(sends, 'slab', split_axis=0, concat_axis=0, axis_index_gro...  1.92 us
    ppermute x3, starting transfers between devices, compact_device(): lax.ppermute(shaded, 'strip', [(s, s ^ k) for s in range(n_strip)])  1.87 us
    pallas_call x1, Pallas kernels, compact_device(): pl.pallas_call(shade_kernel, out_shape=jax.ShapeDtypeStruct((items * outs...  1.68 us
    pallas_call x1, Pallas kernels, compact_device(): pl.pallas_call(pack_kernel, out_shape=jax.ShapeDtypeStruct((n_slab, messa...  1.61 us
    ppermute x3, waiting for transfers between devices, compact_device(): lax.ppermute(shaded, 'strip', [(s, s ^ k) for s in range(n_strip)])  1.55 us
    pallas_call x1, Pallas kernels, compact_device(): pl.pallas_call(functools.partial(plan_kernel, n_slab, slots), out_shape=[...  1.22 us
    pallas_call x1, Pallas kernels, compact_device(): pl.pallas_call(place_kernel, out_shape=[jax.ShapeDtypeStruct((GROUP, 2 *...  1.1 us
  transfers between devices with their start and end apart: 4, of which 3 were waited for; matrix products, arithmetic and copies ran while one was open for 0% of the time, Pallas kernels for 14%

profile of v12, /device:TPU:0, one launch (start us, length us, event | category | flops | bytes accessed | tf_op | source)
XLA Modules:
  0.0 20.2 jit_solution(14530905739078466209)
XLA Ops:
  0.0 1.6 %pack.1 = bf16[8,72,128]{2,1,0:T(8,128)(2,1)} custom-call(s32[1,8,8]{2,1,0:T(8,128)} %far_counts.1, bf16[1,1,16,32,128]{4,3,2,1,0:T(8,128)(2,1)} %far_colors.1, bf16[1,1,16,128]{3,2,1,0:T(8,128)(2,1)} %far_transmit.1), custom_call_target="tpu_custom_call" | custom-call | tf_op jit(solution)/shard_map/pack/pallas_call | solution.py:324
  1.6 0.0 copy-start.2
  1.6 0.0 copy-start.1
  1.6 7.9 %all-to-all-start = ((bf16[8,72,128]{2,1,0:T(8,128)(2,1)}), bf16[8,72,128]{2,1,0:T(8,128)(2,1)S(1)}, u32[]{:S(2)}, u32[]{:S(2)}) async-start(bf16[8,72,128]{2,1,0:T(8,128)(2,1)} %pack.1), calls=%async_computation | async-start | bytes 294912 | tf_op jit(solution)/shard_map/all_to_all | solution.py:340
  9.5 0.0 copy-start
  9.5 1.2 %plan.1 = (s32[3,16,128]{2,1,0:T(8,128)S(1)}, bf16[8,128]{1,0:T(8,128)(2,1)S(1)}, s32[8,128]{1,0:T(8,128)S(1)}) custom-call(s32[1,8,8]{2,1,0:T(8,128)} %far_counts.1, s32[1,8,16]{2,1,0:T(8,128)} %refs_1_.1, s32[1,1024]{1,0:T(1,128)} %refs_2_.1, s32[8]{0:T(128)} %refs_3_.1), custom_call_target="tpu_custom_call" | custom-call | flops 100000 | bytes 1000000 | tf_op jit(solution)/shard_map/plan/pallas_call | solution.py:347
  10.7 0.0 copy-done.2
  10.7 0.0 copy-done.1
  10.8 0.0 copy-done
  10.8 1.1 %place.1 = (bf16[4,256,256]{2,1,0:T(8,128)(2,1)S(1)}, bf16[4,256]{1,0:T(4,128)(2,1)S(1)}, bf16[2,256,256]{2,1,0:T(8,128)(2,1)S(1)}) custom-call(bf16[32,256]{1,0:T(8,128)(2,1)S(1)} %bitcast.1, bf16[1,256]{1,0:T(2,128)(2,1)S(1)} %broadcast_in_dim.3.trans_weight, bf16[4,256]{1,0:T(4,128)(2,1)S(1)} %copy-done.1, bf16[2,256,256]{2,1,0:T(8,128)(2,1)} %far_mid.1), custom_call_target="tpu_custom_call" | custom-call | flops 100000 | bytes 1000000 | tf_op jit(solution)/shard_map/place/pallas_call | solution.py:364
  11.9 1.9 %all-to-all-done.got = bf16[8,72,128]{2,1,0:T(8,128)(2,1)S(1)} async-done(((bf16[8,72,128]{2,1,0:T(8,128)(2,1)}), bf16[8,72,128]{2,1,0:T(8,128)(2,1)S(1)}, u32[]{:S(2)}, u32[]{:S(2)}) %all-to-all-start) | async-done | bytes 147488 | tf_op jit(solution)/shard_map/all_to_all | solution.py:340
  13.8 1.7 %shade.1.refs_3_ = bf16[72,128]{1,0:T(8,128)(2,1)S(1)} custom-call(s32[3,16,128]{2,1,0:T(8,128)S(1)} %get-tuple-element.11.rows, bf16[8,128]{1,0:T(8,128)(2,1)S(1)} %get-tuple-element.12.codes, bf16[8,72,128]{2,1,0:T(8,128)(2,1)S(1)} %all-to-all-done.got, bf16[4,256,256]{2,1,0:T(8,128)(2,1)S(1)} %get-tuple-element.13.w_first, ...), custom_call_target="tpu_custom_call" | custom-call | tf_op jit(solution)/shard_map/shade/pallas_call | solution.py:390
  15.5 0.0 collective-permute-start.2
  15.5 1.6 %collective-permute-start.1 = (bf16[72,128]{1,0:T(8,128)(2,1)S(1)}, bf16[72,128]{1,0:T(8,128)(2,1)S(1)}, u32[]{:S(2)}, u32[]{:S(2)}) collective-permute-start(bf16[72,128]{1,0:T(8,128)(2,1)S(1)} %shade.1.refs_3_), channel_id=1, source_target_pairs={{0,2},{1,3},{2,0},{3,1},{4,6},{5,7},{6,4},{7,5},{8,10},{9,11},{10,... | collective-permute-start | bytes 55304 | tf_op jit(solution)/shard_map/ppermute | solution.py:404
  17.1 0.3 %collective-permute-start = (bf16[72,128]{1,0:T(8,128)(2,1)S(1)}, bf16[72,128]{1,0:T(8,128)(2,1)S(1)}, u32[]{:S(2)}, u32[]{:S(2)}) collective-permute-start(bf16[72,128]{1,0:T(8,128)(2,1)S(1)} %shade.1.refs_3_), channel_id=1, source_target_pairs={{0,1},{1,0},{2,3},{3,2},{4,5},{5,4},{6,7},{7,6},{8,9},{9,8},{10,11... | collective-permute-start | bytes 55304 | tf_op jit(solution)/shard_map/ppermute | solution.py:404
  17.4 0.4 %empty.1.refs_4_ = f32[8,128]{1,0:T(8,128)S(1)} custom-call(bf16[1,256]{1,0:T(2,128)(2,1)S(1)} %broadcast_in_dim.3.trans_weight, bf16[2,256,256]{2,1,0:T(8,128)(2,1)S(1)} %get-tuple-element.14.w_mid, bf16[4,256]{1,0:T(4,128)(2,1)S(1)} %get-tuple-element.15.w_out), custom_call_target="tpu_custom_call" | custom-call | flops 100000 | bytes 1000000 | tf_op jit(solution)/shard_map/empty/pallas_call | solution.py:381
  17.8 1.0 %collective-permute-done.2.refs_2_ = bf16[72,128]{1,0:T(8,128)(2,1)S(1)} collective-permute-done((bf16[72,128]{1,0:T(8,128)(2,1)S(1)}, bf16[72,128]{1,0:T(8,128)(2,1)S(1)}, u32[]{:S(2)}, u32[]{:S(2)}) %collective-permute-start.2) | collective-permute-done | bytes 18464 | tf_op jit(solution)/shard_map/ppermute | solution.py:404
  18.8 0.5 %collective-permute-done.1.refs_1_ = bf16[72,128]{1,0:T(8,128)(2,1)S(1)} collective-permute-done((bf16[72,128]{1,0:T(8,128)(2,1)S(1)}, bf16[72,128]{1,0:T(8,128)(2,1)S(1)}, u32[]{:S(2)}, u32[]{:S(2)}) %collective-permute-start.1) | collective-permute-done | bytes 18464 | tf_op jit(solution)/shard_map/ppermute | solution.py:404
  19.3 0.0 collective-permute-done.refs_0_
  19.3 0.9 %join.1 = bf16[1,4,32,4,128]{4,3,2,1,0:T(4,128)(2,1)} custom-call(bf16[72,128]{1,0:T(8,128)(2,1)S(1)} %collective-permute-done.refs_0_, bf16[72,128]{1,0:T(8,128)(2,1)S(1)} %collective-permute-done.1.refs_1_, bf16[72,128]{1,0:T(8,128)(2,1)S(1)} %collective-permute-done.2.refs_2_, bf16[72,128]{1,0:T(8,128)(2,1)S(1)} %shade.1.refs_3_, ...), custom_call_target="tpu_custom_call" | custom-call | tf_op jit(solution)/shard_map/join/pallas_call | solution.py:407
  (1 shorter events, 0.0 us)
Async XLA Ops:
  1.6 9.1 %copy-start.2 = (bf16[256]{0:T(256)(128)(2,1)S(1)}, bf16[256]{0:T(256)(128)(2,1)}, u32[]{:S(2)}) copy-start(bf16[256]{0:T(256)(128)(2,1)} %param.17) | copy-start | bytes 1540
  1.6 9.1 %copy-start.1 = (bf16[4,256]{1,0:T(4,128)(2,1)S(1)}, bf16[4,256]{1,0:T(4,128)(2,1)}, u32[]{:S(2)}) copy-start(bf16[4,256]{1,0:T(4,128)(2,1)} %far_out.1) | copy-start | bytes 6148
  1.6 12.2 %all-to-all-start = ((bf16[8,72,128]{2,1,0:T(8,128)(2,1)}), bf16[8,72,128]{2,1,0:T(8,128)(2,1)S(1)}, u32[]{:S(2)}, u32[]{:S(2)}) async-start(bf16[8,72,128]{2,1,0:T(8,128)(2,1)} %pack.1), calls=%async_computation | async-start | bytes 294912 | tf_op jit(solution)/shard_map/all_to_all | solution.py:340
  9.5 1.3 %copy-start = (bf16[256,32]{0,1:T(8,128)(2,1)S(1)}, bf16[256,32]{0,1:T(8,128)(2,1)}, u32[]{:S(2)}) copy-start(bf16[256,32]{0,1:T(8,128)(2,1)} %param.16) | copy-start | bytes 49156
  15.5 3.3 %collective-permute-start.2 = (bf16[72,128]{1,0:T(8,128)(2,1)S(1)}, bf16[72,128]{1,0:T(8,128)(2,1)S(1)}, u32[]{:S(2)}, u32[]{:S(2)}) collective-permute-start(bf16[72,128]{1,0:T(8,128)(2,1)S(1)} %shade.1.refs_3_), channel_id=1, source_target_pairs={{0,3},{1,2},{2,1},{3,0},{4,7},{5,6},{6,5},{7,4},{8,11},{9,10},{10,... | collective-permute-start | bytes 55304 | tf_op jit(solution)/shard_map/ppermute | solution.py:404
  15.5 3.8 %collective-permute-start.1 = (bf16[72,128]{1,0:T(8,128)(2,1)S(1)}, bf16[72,128]{1,0:T(8,128)(2,1)S(1)}, u32[]{:S(2)}, u32[]{:S(2)}) collective-permute-start(bf16[72,128]{1,0:T(8,128)(2,1)S(1)} %shade.1.refs_3_), channel_id=1, source_target_pairs={{0,2},{1,3},{2,0},{3,1},{4,6},{5,7},{6,4},{7,5},{8,10},{9,11},{10,... | collective-permute-start | bytes 55304 | tf_op jit(solution)/shard_map/ppermute | solution.py:404
  17.1 2.3 %collective-permute-start = (bf16[72,128]{1,0:T(8,128)(2,1)S(1)}, bf16[72,128]{1,0:T(8,128)(2,1)S(1)}, u32[]{:S(2)}, u32[]{:S(2)}) collective-permute-start(bf16[72,128]{1,0:T(8,128)(2,1)S(1)} %shade.1.refs_3_), channel_id=1, source_target_pairs={{0,1},{1,0},{2,3},{3,2},{4,5},{5,4},{6,7},{7,6},{8,9},{9,8},{10,11... | collective-permute-start | bytes 55304 | tf_op jit(solution)/shard_map/ppermute | solution.py:404

commit v13 on v12

--- a/solution.py
+++ b/solution.py
@@ -252,7 +252,7 @@
         xt[lines, pl.ds(GROUP * feats, 16)] = tail.T.astype(jnp.bfloat16)
 
     x = xt[...]
-    stride = GROUP // 2
+    stride = GROUP
     for start in range(0, GROUP, stride):
         h = jnp.concatenate(
             [

time: 20.5 us -> 20.4 us (level)
  no operation moved by 1% of the time
where the time goes in v13:
time: 20.4 us; the launch traced here: 20 us
  starting transfers between devices  9.73 us (48%)
  Pallas kernels  6.76 us (33%)
  waiting for transfers between devices  3.45 us (17%)
    all_to_all x1, starting transfers between devices, compact_device(): lax.all_to_all(sends, 'slab', split_axis=0, concat_axis=0, axis_index_gro...  7.85 us
    all_to_all x1, waiting for transfers between devices, compact_device(): lax.all_to_all(sends, 'slab', split_axis=0, concat_axis=0, axis_index_gro...  1.92 us
    ppermute x3, starting transfers between devices, compact_device(): lax.ppermute(shaded, 'strip', [(s, s ^ k) for s in range(n_strip)])  1.88 us
    pallas_call x1, Pallas kernels, compact_device(): pl.pallas_call(pack_kernel, out_shape=jax.ShapeDtypeStruct((n_slab, messa...  1.61 us
    pallas_call x1, Pallas kernels, compact_device(): pl.pallas_call(shade_kernel, out_shape=jax.ShapeDtypeStruct((items * outs...  1.54 us
    ppermute x3, waiting for transfers between devices, compact_device(): lax.ppermute(shaded, 'strip', [(s, s ^ k) for s in range(n_strip)])  1.53 us
    pallas_call x1, Pallas kernels, compact_device(): pl.pallas_call(functools.partial(plan_kernel, n_slab, slots), out_shape=[...  1.22 us
    pallas_call x1, Pallas kernels, compact_device(): pl.pallas_call(place_kernel, out_shape=[jax.ShapeDtypeStruct((GROUP, 2 *...  1.1 us
  transfers between devices with their start and end apart: 4, of which 3 were waited for; matrix products, arithmetic and copies ran while one was open for 0% of the time, Pallas kernels for 14%

profile of v13, /device:TPU:0, one launch (start us, length us, event | category | flops | bytes accessed | tf_op | source)
XLA Modules:
  0.0 20.0 jit_solution(2323197168447949115)
XLA Ops:
  0.0 1.6 %pack.1 = bf16[8,72,128]{2,1,0:T(8,128)(2,1)} custom-call(s32[1,8,8]{2,1,0:T(8,128)} %far_counts.1, bf16[1,1,16,32,128]{4,3,2,1,0:T(8,128)(2,1)} %far_colors.1, bf16[1,1,16,128]{3,2,1,0:T(8,128)(2,1)} %far_transmit.1), custom_call_target="tpu_custom_call" | custom-call | tf_op jit(solution)/shard_map/pack/pallas_call | solution.py:324
  1.6 0.0 copy-start.2
  1.6 0.0 copy-start.1
  1.6 7.9 %all-to-all-start = ((bf16[8,72,128]{2,1,0:T(8,128)(2,1)}), bf16[8,72,128]{2,1,0:T(8,128)(2,1)S(1)}, u32[]{:S(2)}, u32[]{:S(2)}) async-start(bf16[8,72,128]{2,1,0:T(8,128)(2,1)} %pack.1), calls=%async_computation | async-start | bytes 294912 | tf_op jit(solution)/shard_map/all_to_all | solution.py:340
  9.5 0.0 copy-start
  9.5 1.2 %plan.1 = (s32[3,16,128]{2,1,0:T(8,128)S(1)}, bf16[8,128]{1,0:T(8,128)(2,1)S(1)}, s32[8,128]{1,0:T(8,128)S(1)}) custom-call(s32[1,8,8]{2,1,0:T(8,128)} %far_counts.1, s32[1,8,16]{2,1,0:T(8,128)} %refs_1_.1, s32[1,1024]{1,0:T(1,128)} %refs_2_.1, s32[8]{0:T(128)} %refs_3_.1), custom_call_target="tpu_custom_call" | custom-call | flops 100000 | bytes 1000000 | tf_op jit(solution)/shard_map/plan/pallas_call | solution.py:347
  10.7 0.0 copy-done.2
  10.7 0.0 copy-done.1
  10.8 0.0 copy-done
  10.8 1.1 %place.1 = (bf16[4,256,256]{2,1,0:T(8,128)(2,1)S(1)}, bf16[4,256]{1,0:T(4,128)(2,1)S(1)}, bf16[2,256,256]{2,1,0:T(8,128)(2,1)S(1)}) custom-call(bf16[32,256]{1,0:T(8,128)(2,1)S(1)} %bitcast.1, bf16[1,256]{1,0:T(2,128)(2,1)S(1)} %broadcast_in_dim.3.trans_weight, bf16[4,256]{1,0:T(4,128)(2,1)S(1)} %copy-done.1, bf16[2,256,256]{2,1,0:T(8,128)(2,1)} %far_mid.1), custom_call_target="tpu_custom_call" | custom-call | flops 100000 | bytes 1000000 | tf_op jit(solution)/shard_map/place/pallas_call | solution.py:364
  11.9 1.9 %all-to-all-done.got = bf16[8,72,128]{2,1,0:T(8,128)(2,1)S(1)} async-done(((bf16[8,72,128]{2,1,0:T(8,128)(2,1)}), bf16[8,72,128]{2,1,0:T(8,128)(2,1)S(1)}, u32[]{:S(2)}, u32[]{:S(2)}) %all-to-all-start) | async-done | bytes 147488 | tf_op jit(solution)/shard_map/all_to_all | solution.py:340
  13.8 1.5 %shade.1.refs_3_ = bf16[72,128]{1,0:T(8,128)(2,1)S(1)} custom-call(s32[3,16,128]{2,1,0:T(8,128)S(1)} %get-tuple-element.11.rows, bf16[8,128]{1,0:T(8,128)(2,1)S(1)} %get-tuple-element.12.codes, bf16[8,72,128]{2,1,0:T(8,128)(2,1)S(1)} %all-to-all-done.got, bf16[4,256,256]{2,1,0:T(8,128)(2,1)S(1)} %get-tuple-element.13.w_first, ...), custom_call_target="tpu_custom_call" | custom-call | tf_op jit(solution)/shard_map/shade/pallas_call | solution.py:390
  15.3 0.0 collective-permute-start.2
  15.3 1.6 %collective-permute-start.1 = (bf16[72,128]{1,0:T(8,128)(2,1)S(1)}, bf16[72,128]{1,0:T(8,128)(2,1)S(1)}, u32[]{:S(2)}, u32[]{:S(2)}) collective-permute-start(bf16[72,128]{1,0:T(8,128)(2,1)S(1)} %shade.1.refs_3_), channel_id=1, source_target_pairs={{0,2},{1,3},{2,0},{3,1},{4,6},{5,7},{6,4},{7,5},{8,10},{9,11},{10,... | collective-permute-start | bytes 55304 | tf_op jit(solution)/shard_map/ppermute | solution.py:404
  16.9 0.3 %collective-permute-start = (bf16[72,128]{1,0:T(8,128)(2,1)S(1)}, bf16[72,128]{1,0:T(8,128)(2,1)S(1)}, u32[]{:S(2)}, u32[]{:S(2)}) collective-permute-start(bf16[72,128]{1,0:T(8,128)(2,1)S(1)} %shade.1.refs_3_), channel_id=1, source_target_pairs={{0,1},{1,0},{2,3},{3,2},{4,5},{5,4},{6,7},{7,6},{8,9},{9,8},{10,11... | collective-permute-start | bytes 55304 | tf_op jit(solution)/shard_map/ppermute | solution.py:404
  17.2 0.4 %empty.1.refs_4_ = f32[8,128]{1,0:T(8,128)S(1)} custom-call(bf16[1,256]{1,0:T(2,128)(2,1)S(1)} %broadcast_in_dim.3.trans_weight, bf16[2,256,256]{2,1,0:T(8,128)(2,1)S(1)} %get-tuple-element.14.w_mid, bf16[4,256]{1,0:T(4,128)(2,1)S(1)} %get-tuple-element.15.w_out), custom_call_target="tpu_custom_call" | custom-call | flops 100000 | bytes 1000000 | tf_op jit(solution)/shard_map/empty/pallas_call | solution.py:381
  17.6 1.0 %collective-permute-done.2.refs_2_ = bf16[72,128]{1,0:T(8,128)(2,1)S(1)} collective-permute-done((bf16[72,128]{1,0:T(8,128)(2,1)S(1)}, bf16[72,128]{1,0:T(8,128)(2,1)S(1)}, u32[]{:S(2)}, u32[]{:S(2)}) %collective-permute-start.2) | collective-permute-done | bytes 18464 | tf_op jit(solution)/shard_map/ppermute | solution.py:404
  18.7 0.5 %collective-permute-done.1.refs_1_ = bf16[72,128]{1,0:T(8,128)(2,1)S(1)} collective-permute-done((bf16[72,128]{1,0:T(8,128)(2,1)S(1)}, bf16[72,128]{1,0:T(8,128)(2,1)S(1)}, u32[]{:S(2)}, u32[]{:S(2)}) %collective-permute-start.1) | collective-permute-done | bytes 18464 | tf_op jit(solution)/shard_map/ppermute | solution.py:404
  19.2 0.0 collective-permute-done.refs_0_
  19.2 0.9 %join.1 = bf16[1,4,32,4,128]{4,3,2,1,0:T(4,128)(2,1)} custom-call(bf16[72,128]{1,0:T(8,128)(2,1)S(1)} %collective-permute-done.refs_0_, bf16[72,128]{1,0:T(8,128)(2,1)S(1)} %collective-permute-done.1.refs_1_, bf16[72,128]{1,0:T(8,128)(2,1)S(1)} %collective-permute-done.2.refs_2_, bf16[72,128]{1,0:T(8,128)(2,1)S(1)} %shade.1.refs_3_, ...), custom_call_target="tpu_custom_call" | custom-call | tf_op jit(solution)/shard_map/join/pallas_call | solution.py:407
  (1 shorter events, 0.0 us)
Async XLA Ops:
  1.6 9.1 %copy-start.2 = (bf16[256]{0:T(256)(128)(2,1)S(1)}, bf16[256]{0:T(256)(128)(2,1)}, u32[]{:S(2)}) copy-start(bf16[256]{0:T(256)(128)(2,1)} %param.17) | copy-start | bytes 1540
  1.6 9.1 %copy-start.1 = (bf16[4,256]{1,0:T(4,128)(2,1)S(1)}, bf16[4,256]{1,0:T(4,128)(2,1)}, u32[]{:S(2)}) copy-start(bf16[4,256]{1,0:T(4,128)(2,1)} %far_out.1) | copy-start | bytes 6148
  1.6 12.2 %all-to-all-start = ((bf16[8,72,128]{2,1,0:T(8,128)(2,1)}), bf16[8,72,128]{2,1,0:T(8,128)(2,1)S(1)}, u32[]{:S(2)}, u32[]{:S(2)}) async-start(bf16[8,72,128]{2,1,0:T(8,128)(2,1)} %pack.1), calls=%async_computation | async-start | bytes 294912 | tf_op jit(solution)/shard_map/all_to_all | solution.py:340
  9.5 1.3 %copy-start = (bf16[256,32]{0,1:T(8,128)(2,1)S(1)}, bf16[256,32]{0,1:T(8,128)(2,1)}, u32[]{:S(2)}) copy-start(bf16[256,32]{0,1:T(8,128)(2,1)} %param.16) | copy-start | bytes 49156
  15.3 3.4 %collective-permute-start.2 = (bf16[72,128]{1,0:T(8,128)(2,1)S(1)}, bf16[72,128]{1,0:T(8,128)(2,1)S(1)}, u32[]{:S(2)}, u32[]{:S(2)}) collective-permute-start(bf16[72,128]{1,0:T(8,128)(2,1)S(1)} %shade.1.refs_3_), channel_id=1, source_target_pairs={{0,3},{1,2},{2,1},{3,0},{4,7},{5,6},{6,5},{7,4},{8,11},{9,10},{10,... | collective-permute-start | bytes 55304 | tf_op jit(solution)/shard_map/ppermute | solution.py:404
  15.3 3.8 %collective-permute-start.1 = (bf16[72,128]{1,0:T(8,128)(2,1)S(1)}, bf16[72,128]{1,0:T(8,128)(2,1)S(1)}, u32[]{:S(2)}, u32[]{:S(2)}) collective-permute-start(bf16[72,128]{1,0:T(8,128)(2,1)S(1)} %shade.1.refs_3_), channel_id=1, source_target_pairs={{0,2},{1,3},{2,0},{3,1},{4,6},{5,7},{6,4},{7,5},{8,10},{9,11},{10,... | collective-permute-start | bytes 55304 | tf_op jit(solution)/shard_map/ppermute | solution.py:404
  16.9 2.3 %collective-permute-start = (bf16[72,128]{1,0:T(8,128)(2,1)S(1)}, bf16[72,128]{1,0:T(8,128)(2,1)S(1)}, u32[]{:S(2)}, u32[]{:S(2)}) collective-permute-start(bf16[72,128]{1,0:T(8,128)(2,1)S(1)} %shade.1.refs_3_), channel_id=1, source_target_pairs={{0,1},{1,0},{2,3},{3,2},{4,5},{5,4},{6,7},{7,6},{8,9},{9,8},{10,11... | collective-permute-start | bytes 55304 | tf_op jit(solution)/shard_map/ppermute | solution.py:404

commit v14 on v13

--- a/solution.py
+++ b/solution.py
@@ -193,10 +193,9 @@
 def later_layers(h, w_mid, w_out):
     for m in range(w_mid.shape[0]):
         h = silu_half(jnp.dot(h, w_mid[m], preferred_element_type=jnp.float32))
-    y = lax.dot_general(
+    return lax.dot_general(
         w_out[...], h, (((1,), (1,)), ((), ())), preferred_element_type=jnp.float32
     )
-    return y.astype(jnp.bfloat16).astype(jnp.float32)
 
 
 def empty_kernel(trans_weight, w_mid, w_out, out):
@@ -284,10 +283,9 @@
         pos = got[k][pl.ds(count, ROWS), :].astype(jnp.float32)[:1, :count].astype(jnp.int32)
         hit = pos * outs + chan == want
         pick = jnp.where(hit, 1.0, 0.0).astype(jnp.bfloat16)
-        blocks = got[k][pl.ds(0, count), :]
+        blocks = jnp.concatenate([got[k][pl.ds(0, count), :], ones], axis=1)
         placed = jnp.dot(pick, blocks, preferred_element_type=jnp.float32)
-        filled = jnp.dot(pick, ones, preferred_element_type=jnp.float32)
-        value = jnp.where(filled > 0.5, placed, filler)
+        value = jnp.where(placed[:, span:] > 0.5, placed[:, :span], filler)
         held[k] = value.reshape(tile, outs, span).astype(jnp.bfloat16)
         copy = pltpu.make_async_copy(
             held.at[k], out.at[0, me ^ ((k + 1) % n_strip)], sems.at[k]

time: 20.4 us -> 20.4 us (level)
  no operation moved by 1% of the time
where the time goes in v14:
time: 20.4 us; the launch traced here: 20 us
  starting transfers between devices  9.73 us (48%)
  Pallas kernels  6.75 us (33%)
  waiting for transfers between devices  3.45 us (17%)
    all_to_all x1, starting transfers between devices, compact_device(): lax.all_to_all(sends, 'slab', split_axis=0, concat_axis=0, axis_index_gro...  7.85 us
    all_to_all x1, waiting for transfers between devices, compact_device(): lax.all_to_all(sends, 'slab', split_axis=0, concat_axis=0, axis_index_gro...  1.92 us
    ppermute x3, starting transfers between devices, compact_device(): lax.ppermute(shaded, 'strip', [(s, s ^ k) for s in range(n_strip)])  1.88 us
    pallas_call x1, Pallas kernels, compact_device(): pl.pallas_call(pack_kernel, out_shape=jax.ShapeDtypeStruct((n_slab, messa...  1.61 us
    ppermute x3, waiting for transfers between devices, compact_device(): lax.ppermute(shaded, 'strip', [(s, s ^ k) for s in range(n_strip)])  1.52 us
    pallas_call x1, Pallas kernels, compact_device(): pl.pallas_call(shade_kernel, out_shape=jax.ShapeDtypeStruct((items * outs...  1.52 us
    pallas_call x1, Pallas kernels, compact_device(): pl.pallas_call(functools.partial(plan_kernel, n_slab, slots), out_shape=[...  1.22 us
    pallas_call x1, Pallas kernels, compact_device(): pl.pallas_call(place_kernel, out_shape=[jax.ShapeDtypeStruct((GROUP, 2 *...  1.1 us
  transfers between devices with their start and end apart: 4, of which 3 were waited for; matrix products, arithmetic and copies ran while one was open for 0% of the time, Pallas kernels for 14%

profile of v14, /device:TPU:0, one launch (start us, length us, event | category | flops | bytes accessed | tf_op | source)
XLA Modules:
  0.0 20.0 jit_solution(3313077581890172245)
XLA Ops:
  0.0 1.6 %pack.1 = bf16[8,72,128]{2,1,0:T(8,128)(2,1)} custom-call(s32[1,8,8]{2,1,0:T(8,128)} %far_counts.1, bf16[1,1,16,32,128]{4,3,2,1,0:T(8,128)(2,1)} %far_colors.1, bf16[1,1,16,128]{3,2,1,0:T(8,128)(2,1)} %far_transmit.1), custom_call_target="tpu_custom_call" | custom-call | tf_op jit(solution)/shard_map/pack/pallas_call | solution.py:322
  1.6 0.0 copy-start.2
  1.6 0.0 copy-start.1
  1.6 7.9 %all-to-all-start = ((bf16[8,72,128]{2,1,0:T(8,128)(2,1)}), bf16[8,72,128]{2,1,0:T(8,128)(2,1)S(1)}, u32[]{:S(2)}, u32[]{:S(2)}) async-start(bf16[8,72,128]{2,1,0:T(8,128)(2,1)} %pack.1), calls=%async_computation | async-start | bytes 294912 | tf_op jit(solution)/shard_map/all_to_all | solution.py:338
  9.5 0.0 copy-start
  9.5 1.2 %plan.1 = (s32[3,16,128]{2,1,0:T(8,128)S(1)}, bf16[8,128]{1,0:T(8,128)(2,1)S(1)}, s32[8,128]{1,0:T(8,128)S(1)}) custom-call(s32[1,8,8]{2,1,0:T(8,128)} %far_counts.1, s32[1,8,16]{2,1,0:T(8,128)} %refs_1_.1, s32[1,1024]{1,0:T(1,128)} %refs_2_.1, s32[8]{0:T(128)} %refs_3_.1), custom_call_target="tpu_custom_call" | custom-call | flops 100000 | bytes 1000000 | tf_op jit(solution)/shard_map/plan/pallas_call | solution.py:345
  10.7 0.0 copy-done.2
  10.7 0.0 copy-done.1
  10.8 0.0 copy-done
  10.8 1.1 %place.1 = (bf16[4,256,256]{2,1,0:T(8,128)(2,1)S(1)}, bf16[4,256]{1,0:T(4,128)(2,1)S(1)}, bf16[2,256,256]{2,1,0:T(8,128)(2,1)S(1)}) custom-call(bf16[32,256]{1,0:T(8,128)(2,1)S(1)} %bitcast.1, bf16[1,256]{1,0:T(2,128)(2,1)S(1)} %broadcast_in_dim.3.trans_weight, bf16[4,256]{1,0:T(4,128)(2,1)S(1)} %copy-done.1, bf16[2,256,256]{2,1,0:T(8,128)(2,1)} %far_mid.1), custom_call_target="tpu_custom_call" | custom-call | flops 100000 | bytes 1000000 | tf_op jit(solution)/shard_map/place/pallas_call | solution.py:362
  11.9 1.9 %all-to-all-done.got = bf16[8,72,128]{2,1,0:T(8,128)(2,1)S(1)} async-done(((bf16[8,72,128]{2,1,0:T(8,128)(2,1)}), bf16[8,72,128]{2,1,0:T(8,128)(2,1)S(1)}, u32[]{:S(2)}, u32[]{:S(2)}) %all-to-all-start) | async-done | bytes 147488 | tf_op jit(solution)/shard_map/all_to_all | solution.py:338
  13.8 1.5 %shade.1.refs_3_ = bf16[72,128]{1,0:T(8,128)(2,1)S(1)} custom-call(s32[3,16,128]{2,1,0:T(8,128)S(1)} %get-tuple-element.11.rows, bf16[8,128]{1,0:T(8,128)(2,1)S(1)} %get-tuple-element.12.codes, bf16[8,72,128]{2,1,0:T(8,128)(2,1)S(1)} %all-to-all-done.got, bf16[4,256,256]{2,1,0:T(8,128)(2,1)S(1)} %get-tuple-element.13.w_first, ...), custom_call_target="tpu_custom_call" | custom-call | tf_op jit(solution)/shard_map/shade/pallas_call | solution.py:388
  15.3 0.0 collective-permute-start.2
  15.3 1.6 %collective-permute-start.1 = (bf16[72,128]{1,0:T(8,128)(2,1)S(1)}, bf16[72,128]{1,0:T(8,128)(2,1)S(1)}, u32[]{:S(2)}, u32[]{:S(2)}) collective-permute-start(bf16[72,128]{1,0:T(8,128)(2,1)S(1)} %shade.1.refs_3_), channel_id=1, source_target_pairs={{0,2},{1,3},{2,0},{3,1},{4,6},{5,7},{6,4},{7,5},{8,10},{9,11},{10,... | collective-permute-start | bytes 55304 | tf_op jit(solution)/shard_map/ppermute | solution.py:402
  16.9 0.3 %collective-permute-start = (bf16[72,128]{1,0:T(8,128)(2,1)S(1)}, bf16[72,128]{1,0:T(8,128)(2,1)S(1)}, u32[]{:S(2)}, u32[]{:S(2)}) collective-permute-start(bf16[72,128]{1,0:T(8,128)(2,1)S(1)} %shade.1.refs_3_), channel_id=1, source_target_pairs={{0,1},{1,0},{2,3},{3,2},{4,5},{5,4},{6,7},{7,6},{8,9},{9,8},{10,11... | collective-permute-start | bytes 55304 | tf_op jit(solution)/shard_map/ppermute | solution.py:402
  17.2 0.4 %empty.1.refs_4_ = f32[8,128]{1,0:T(8,128)S(1)} custom-call(bf16[1,256]{1,0:T(2,128)(2,1)S(1)} %broadcast_in_dim.3.trans_weight, bf16[2,256,256]{2,1,0:T(8,128)(2,1)S(1)} %get-tuple-element.14.w_mid, bf16[4,256]{1,0:T(4,128)(2,1)S(1)} %get-tuple-element.15.w_out), custom_call_target="tpu_custom_call" | custom-call | flops 100000 | bytes 1000000 | tf_op jit(solution)/shard_map/empty/pallas_call | solution.py:379
  17.6 1.0 %collective-permute-done.2.refs_2_ = bf16[72,128]{1,0:T(8,128)(2,1)S(1)} collective-permute-done((bf16[72,128]{1,0:T(8,128)(2,1)S(1)}, bf16[72,128]{1,0:T(8,128)(2,1)S(1)}, u32[]{:S(2)}, u32[]{:S(2)}) %collective-permute-start.2) | collective-permute-done | bytes 18464 | tf_op jit(solution)/shard_map/ppermute | solution.py:402
  18.7 0.5 %collective-permute-done.1.refs_1_ = bf16[72,128]{1,0:T(8,128)(2,1)S(1)} collective-permute-done((bf16[72,128]{1,0:T(8,128)(2,1)S(1)}, bf16[72,128]{1,0:T(8,128)(2,1)S(1)}, u32[]{:S(2)}, u32[]{:S(2)}) %collective-permute-start.1) | collective-permute-done | bytes 18464 | tf_op jit(solution)/shard_map/ppermute | solution.py:402
  19.2 0.0 collective-permute-done.refs_0_
  19.2 0.9 %join.1 = bf16[1,4,32,4,128]{4,3,2,1,0:T(4,128)(2,1)} custom-call(bf16[72,128]{1,0:T(8,128)(2,1)S(1)} %collective-permute-done.refs_0_, bf16[72,128]{1,0:T(8,128)(2,1)S(1)} %collective-permute-done.1.refs_1_, bf16[72,128]{1,0:T(8,128)(2,1)S(1)} %collective-permute-done.2.refs_2_, bf16[72,128]{1,0:T(8,128)(2,1)S(1)} %shade.1.refs_3_, ...), custom_call_target="tpu_custom_call" | custom-call | tf_op jit(solution)/shard_map/join/pallas_call | solution.py:405
  (1 shorter events, 0.0 us)
Async XLA Ops:
  1.6 9.1 %copy-start.2 = (bf16[256]{0:T(256)(128)(2,1)S(1)}, bf16[256]{0:T(256)(128)(2,1)}, u32[]{:S(2)}) copy-start(bf16[256]{0:T(256)(128)(2,1)} %param.17) | copy-start | bytes 1540
  1.6 9.1 %copy-start.1 = (bf16[4,256]{1,0:T(4,128)(2,1)S(1)}, bf16[4,256]{1,0:T(4,128)(2,1)}, u32[]{:S(2)}) copy-start(bf16[4,256]{1,0:T(4,128)(2,1)} %far_out.1) | copy-start | bytes 6148
  1.6 12.2 %all-to-all-start = ((bf16[8,72,128]{2,1,0:T(8,128)(2,1)}), bf16[8,72,128]{2,1,0:T(8,128)(2,1)S(1)}, u32[]{:S(2)}, u32[]{:S(2)}) async-start(bf16[8,72,128]{2,1,0:T(8,128)(2,1)} %pack.1), calls=%async_computation | async-start | bytes 294912 | tf_op jit(solution)/shard_map/all_to_all | solution.py:338
  9.5 1.3 %copy-start = (bf16[256,32]{0,1:T(8,128)(2,1)S(1)}, bf16[256,32]{0,1:T(8,128)(2,1)}, u32[]{:S(2)}) copy-start(bf16[256,32]{0,1:T(8,128)(2,1)} %param.16) | copy-start | bytes 49156
  15.3 3.3 %collective-permute-start.2 = (bf16[72,128]{1,0:T(8,128)(2,1)S(1)}, bf16[72,128]{1,0:T(8,128)(2,1)S(1)}, u32[]{:S(2)}, u32[]{:S(2)}) collective-permute-start(bf16[72,128]{1,0:T(8,128)(2,1)S(1)} %shade.1.refs_3_), channel_id=1, source_target_pairs={{0,3},{1,2},{2,1},{3,0},{4,7},{5,6},{6,5},{7,4},{8,11},{9,10},{10,... | collective-permute-start | bytes 55304 | tf_op jit(solution)/shard_map/ppermute | solution.py:402
  15.3 3.8 %collective-permute-start.1 = (bf16[72,128]{1,0:T(8,128)(2,1)S(1)}, bf16[72,128]{1,0:T(8,128)(2,1)S(1)}, u32[]{:S(2)}, u32[]{:S(2)}) collective-permute-start(bf16[72,128]{1,0:T(8,128)(2,1)S(1)} %shade.1.refs_3_), channel_id=1, source_target_pairs={{0,2},{1,3},{2,0},{3,1},{4,6},{5,7},{6,4},{7,5},{8,10},{9,11},{10,... | collective-permute-start | bytes 55304 | tf_op jit(solution)/shard_map/ppermute | solution.py:402
  16.9 2.3 %collective-permute-start = (bf16[72,128]{1,0:T(8,128)(2,1)S(1)}, bf16[72,128]{1,0:T(8,128)(2,1)S(1)}, u32[]{:S(2)}, u32[]{:S(2)}) collective-permute-start(bf16[72,128]{1,0:T(8,128)(2,1)S(1)} %shade.1.refs_3_), channel_id=1, source_target_pairs={{0,1},{1,0},{2,3},{3,2},{4,5},{5,4},{6,7},{7,6},{8,9},{9,8},{10,11... | collective-permute-start | bytes 55304 | tf_op jit(solution)/shard_map/ppermute | solution.py:402
